TPU v7x, 128 devices: a whole 4x4x4 slice. The times are simulated.
128 devices in a mesh: occ: 16 (over x, z), vir: 8 (over y, core).
Axes of the slice: x: 4, y: 4, z: 4, core: 2. Of those that a mesh axis runs over, the one named last changes fastest.
Arguments:
- amplitudes: bfloat16 [512, 32768], P('occ', 'vir'), may hold values from -6 to 6
- tile_live: int32 [16, 32], P('occ', 'vir'), may hold values from 0 to 1, as said below
- integrals: bfloat16 [32, 32, 1024, 1024], P('occ', 'vir'), may hold values from -0.03125 to 0.03125
- block_live: int32 [32, 32], P('occ', 'vir'), may hold values 0 or 1
- row_owner: int32 [32], replicated, may hold values from 0 to 31, each once
Outputs:
- residual: float32 [512, 32768], P('occ', 'vir')
Inputs may be any that keep to these rules, and one draw needn't show every extreme that they name: `tile_live`: in each pair block and each range of 4 tile pairs between 1 and 2 tiles are nonzero; some range has exactly 2. `row_owner`: each tile pair stands in exactly one slot.
All inputs are finite; a program needn't handle non-finite values. No bound on the sum of `block_live` on one device may be relied on, other than what follows from the above.
Results may differ from a plain program's by a relative error of at most 0.0003.
Values may be sent and summed in bfloat16 or wider, within the bound.
No kernel may reach another device: no remote copies, remote signals or barrier semaphores. Data moves between devices by JAX's collectives and lax.ppermute only.
A program may use at most 128 MiB of HBM per device.

v0:
```python
import jax
import jax.numpy as jnp
from jax import lax
from jax.sharding import PartitionSpec as P


def block_term(left_rows, right_block, live_flag):
    return lax.cond(
        live_flag > 0,
        lambda: jnp.dot(left_rows, right_block, preferred_element_type=jnp.float32),
        lambda: jnp.zeros((left_rows.shape[0], right_block.shape[1]), jnp.float32),
    )


def shards(amplitudes, tile_live, integrals, block_live, row_owner):
    pair_dev = amplitudes.shape[0]
    tile_count = tile_live.shape[1]
    held_rows = integrals.shape[0]
    entry_count = integrals.shape[2]
    live_row = tile_live[0]
    masked = amplitudes.reshape(pair_dev, tile_count, entry_count) * live_row[None, :, None].astype(
        amplitudes.dtype
    )
    flattened = masked.reshape(pair_dev, tile_count * entry_count)
    row_piece = lax.all_gather(flattened, "occ", axis=0, tiled=True)
    columns = []
    for slot_index in range(held_rows):
        running = jnp.zeros((row_piece.shape[0], entry_count), jnp.float32)
        for tile_index in range(tile_count):
            offset = tile_index * entry_count
            running = running + block_term(
                row_piece[:, offset : offset + entry_count],
                integrals[slot_index, tile_index],
                block_live[slot_index, tile_index],
            )
        columns.append(running)
    partial_value = jnp.stack(columns, axis=1)
    inverse = (
        jnp.zeros(row_owner.shape, jnp.int32)
        .at[row_owner]
        .set(jnp.arange(row_owner.shape[0], dtype=jnp.int32))
    )
    exchanged = lax.all_to_all(partial_value, "occ", split_axis=0, concat_axis=1, tiled=True)
    ordered = jnp.take(exchanged, inverse, axis=1)
    summed = lax.psum_scatter(ordered, "vir", scatter_dimension=1, tiled=True)
    return summed.reshape(pair_dev, summed.shape[1] * entry_count)


def solution(mesh):
    return jax.shard_map(
        shards,
        mesh=mesh,
        in_specs=(
            P("occ", "vir"),
            P("occ", "vir"),
            P("occ", "vir", None, None),
            P("occ", "vir"),
            P(),
        ),
        out_specs=P("occ", "vir"),
        check_vma=False,
    )
```

profile of v0, /device:TPU:1, one launch (start us, length us, event | category | flops | bytes accessed | tf_op | source)
XLA Modules:
  0.0 245.7 jit_solution(4642200605081216339)
XLA Ops:
  6.5 0.0 all-gather.2.cloned.1.call-start
  6.5 0.7 convert_bitcast_fusion
  7.2 0.1 broadcast_bitcast_fusion
  7.3 1.7 broadcast_multiply_fusion
  9.0 0.0 all-gather.2.cloned.1.call-update
  9.0 1.7 fusion.27
  15.7 48.7 %all-gather.2.cloned.1.call-done = bf16[512,4096]{1,0:T(8,128)(2,1)} async-done(((bf16[32,4096]{1,0:T(8,128)(2,1)}), bf16[512,4096]{1,0:T(8,128)(2,1)}) %all-gather.2.cloned.1.call-update) | async-done | bytes 4194320 | tf_op jit(solution)/shard_map/all_gather | solution.py:25
  64.4 4.0 %fusion.26 = (bf16[512,1024]{1,0:T(8,128)(2,1)}, bf16[512,1024]{1,0:T(8,128)(2,1)S(1)}, bf16[512,1024]{1,0:T(8,128)(2,1)}, bf16[512,1024]{1,0:T(8,128)(2,1)}) fusion(bf16[512,4096]{1,0:T(8,128)(2,1)} %all-gather.2.cloned.1.call-done), kind=kLoop, calls=%fused_computation.40 | loop fusion | bytes 8388608 | tf_op jit(solution)/shard_map/slice | solution.py:32
  68.4 0.2 conditional.10
  68.4 0.2 broadcast.25
  68.6 4.2 %conditional.11 = (f32[512,1024]{1,0:T(8,128)}) conditional(s32[]{:T(128)} %bitcast.12, () %tuple.59, (bf16[2,4,1024,1024]{3,2,1,0:T(8,128)(2,1)}, bf16[512,1024]{1,0:T(8,128)(2,1)S(1)}) %tuple.60), branch_computations={%region_7.0_spmd, %region_8.0_spmd} | conditional | flops 1073741824 | bytes 5242888 | solution.py:8
  68.7 4.2 %fusion.9 = f32[512,1024]{1,0:T(8,128)} fusion(bf16[512,1024]{1,0:T(8,128)(2,1)S(1)} %get-tuple-element.83, bf16[2,4,1024,1024]{3,2,1,0:T(8,128)(2,1)} %get-tuple-element.84), kind=kOutput, calls=%fused_computation.11 | convolution fusion | flops 1073741824 | bytes 5242880 | tf_op jit(solution)/shard_map/cond/branch_1_fun/dot_general | solution.py:10
  72.8 4.5 %conditional.8 = (f32[512,1024]{1,0:T(8,128)}) conditional(s32[]{:T(128)} %bitcast.8, () %tuple.53, (bf16[2,4,1024,1024]{3,2,1,0:T(8,128)(2,1)}, bf16[512,1024]{1,0:T(8,128)(2,1)}) %tuple.54), branch_computations={%region_1.0_spmd, %region_2.0_spmd} | conditional | flops 1073741824 | bytes 5242888 | solution.py:8
  72.8 4.5 %fusion = f32[512,1024]{1,0:T(8,128)} fusion(bf16[512,1024]{1,0:T(8,128)(2,1)} %get-tuple-element.77, bf16[2,4,1024,1024]{3,2,1,0:T(8,128)(2,1)} %get-tuple-element.78), kind=kOutput, calls=%fused_computation.2 | convolution fusion | flops 1073741824 | bytes 5242880 | tf_op jit(solution)/shard_map/cond/branch_1_fun/dot_general | solution.py:10
  77.3 4.6 %conditional.9 = (f32[512,1024]{1,0:T(8,128)}) conditional(s32[]{:T(128)} %bitcast.10, () %tuple.55, (bf16[2,4,1024,1024]{3,2,1,0:T(8,128)(2,1)}, bf16[512,1024]{1,0:T(8,128)(2,1)}) %tuple.56), branch_computations={%region_3.0_spmd, %region_4.0_spmd} | conditional | flops 1073741824 | bytes 5242888 | solution.py:8
  77.3 4.6 %fusion.3 = f32[512,1024]{1,0:T(8,128)} fusion(bf16[512,1024]{1,0:T(8,128)(2,1)} %get-tuple-element.79, bf16[2,4,1024,1024]{3,2,1,0:T(8,128)(2,1)} %get-tuple-element.80), kind=kOutput, calls=%fused_computation.5 | convolution fusion | flops 1073741824 | bytes 5242880 | tf_op jit(solution)/shard_map/cond/branch_1_fun/dot_general | solution.py:10
  81.9 3.8 %add_add_fusion.1 = f32[512,1024]{1,0:T(8,128)S(1)} fusion(f32[512,1024]{1,0:T(8,128)} %get-tuple-element.108, f32[512,1024]{1,0:T(8,128)S(1)} %get-tuple-element.107, f32[512,1024]{1,0:T(8,128)} %get-tuple-element.105, f32[512,1024]{1,0:T(8,128)} %get-tuple-element.106), kind=kLoop, calls=%fused_computation.29 | loop fusion | flops 1572864 | bytes 10485760 | tf_op jit(solution)/shard_map/add | solution.py:31
  85.7 2.7 %stack.9 = f32[512,1,1024]{2,1,0:T(1,128)} reshape(f32[512,1024]{1,0:T(8,128)S(1)} %add_add_fusion.1) | data formatting | bytes 4194304 | tf_op jit(solution)/shard_map/stack | solution.py:37
  88.4 3.2 %conditional.12 = (f32[512,1024]{1,0:T(8,128)S(1)}) conditional(s32[]{:T(128)} %bitcast.13, () %tuple.61, (bf16[2,4,1024,1024]{3,2,1,0:T(8,128)(2,1)}, bf16[512,1024]{1,0:T(8,128)(2,1)}) %tuple.54), branch_computations={%region_9.0_spmd, %region_10.0_spmd} | conditional | flops 1073741824 | bytes 5242888 | solution.py:8
  88.4 3.2 %fusion.12 = f32[512,1024]{1,0:T(8,128)S(1)} fusion(bf16[512,1024]{1,0:T(8,128)(2,1)} %get-tuple-element.85, bf16[2,4,1024,1024]{3,2,1,0:T(8,128)(2,1)} %get-tuple-element.86), kind=kOutput, calls=%fused_computation.14 | convolution fusion | flops 1073741824 | bytes 5242880 | tf_op jit(solution)/shard_map/cond/branch_1_fun/dot_general | solution.py:10
  91.6 4.5 %conditional.13 = (f32[512,1024]{1,0:T(8,128)}) conditional(s32[]{:T(128)} %bitcast.14, () %tuple.62, (bf16[2,4,1024,1024]{3,2,1,0:T(8,128)(2,1)}, bf16[512,1024]{1,0:T(8,128)(2,1)}) %tuple.56), branch_computations={%region_11.0_spmd, %region_12.0_spmd} | conditional | flops 1073741824 | bytes 5242888 | solution.py:8
  91.6 4.5 %fusion.15 = f32[512,1024]{1,0:T(8,128)} fusion(bf16[512,1024]{1,0:T(8,128)(2,1)} %get-tuple-element.87, bf16[2,4,1024,1024]{3,2,1,0:T(8,128)(2,1)} %get-tuple-element.88), kind=kOutput, calls=%fused_computation.17 | convolution fusion | flops 1073741824 | bytes 5242880 | tf_op jit(solution)/shard_map/cond/branch_1_fun/dot_general | solution.py:10
  96.1 4.5 %conditional.14 = (f32[512,1024]{1,0:T(8,128)}) conditional(s32[]{:T(128)} %bitcast.15, () %tuple.63, (bf16[2,4,1024,1024]{3,2,1,0:T(8,128)(2,1)}, bf16[512,1024]{1,0:T(8,128)(2,1)}) %tuple.58), branch_computations={%region_13.0_spmd, %region_14.0_spmd} | conditional | flops 1073741824 | bytes 5242888 | solution.py:8
  96.1 4.5 %fusion.18 = f32[512,1024]{1,0:T(8,128)} fusion(bf16[512,1024]{1,0:T(8,128)(2,1)} %get-tuple-element.89, bf16[2,4,1024,1024]{3,2,1,0:T(8,128)(2,1)} %get-tuple-element.90), kind=kOutput, calls=%fused_computation.20 | convolution fusion | flops 1073741824 | bytes 5242880 | tf_op jit(solution)/shard_map/cond/branch_1_fun/dot_general | solution.py:10
  100.7 4.2 %conditional.15 = (f32[512,1024]{1,0:T(8,128)}) conditional(s32[]{:T(128)} %bitcast.16, () %tuple.64, (bf16[2,4,1024,1024]{3,2,1,0:T(8,128)(2,1)}, bf16[512,1024]{1,0:T(8,128)(2,1)S(1)}) %tuple.60), branch_computations={%region_15.0_spmd, %region_16.0_spmd} | conditional | flops 1073741824 | bytes 5242888 | solution.py:8
  100.7 4.2 %fusion.21 = f32[512,1024]{1,0:T(8,128)} fusion(bf16[512,1024]{1,0:T(8,128)(2,1)S(1)} %get-tuple-element.91, bf16[2,4,1024,1024]{3,2,1,0:T(8,128)(2,1)} %get-tuple-element.92), kind=kOutput, calls=%fused_computation.23 | convolution fusion | flops 1073741824 | bytes 5242880 | tf_op jit(solution)/shard_map/cond/branch_1_fun/dot_general | solution.py:10
  104.9 3.8 %add_add_fusion = f32[512,1024]{1,0:T(8,128)S(1)} fusion(f32[512,1024]{1,0:T(8,128)} %get-tuple-element.112, f32[512,1024]{1,0:T(8,128)} %get-tuple-element.111, f32[512,1024]{1,0:T(8,128)S(1)} %get-tuple-element.109, f32[512,1024]{1,0:T(8,128)} %get-tuple-element.110), kind=kLoop, calls=%fused_computation.28 | loop fusion | flops 1572864 | bytes 10485760 | tf_op jit(solution)/shard_map/add | solution.py:31
  108.7 0.0 copy-start
  108.7 1.4 stack.10
  110.1 0.1 copy-done
  110.3 5.8 %pad_maximum_fusion = f32[512,2,1024]{2,1,0:T(2,128)} fusion(f32[512,1,1024]{2,1,0:T(1,128)S(1)} %stack.10, f32[512,1,1024]{2,1,0:T(1,128)S(1)} %copy-done), kind=kLoop, calls=%fused_computation.26 | loop fusion | flops 1048576 | bytes 8388608 | tf_op jit(solution)/shard_map/stack | solution.py:37
  116.0 0.0 copy-start.1
  116.0 5.3 %all-to-all-start = ((f32[512,2,1024]{2,1,0:T(2,128)}), f32[512,2,1024]{2,1,0:T(2,128)}, u32[]{:S(2)}, u32[]{:S(2)}) async-start(f32[512,2,1024]{2,1,0:T(2,128)} %pad_maximum_fusion), calls=%async_computation | async-start | bytes 8388608 | tf_op jit(solution)/shard_map/all_to_all | solution.py:43
  121.3 0.0 reduce-scatter.2.cloned.1.call-start
  121.4 0.0 copy-done.1
  121.4 0.7 scatter_custom_fusion
  122.1 45.5 %all-to-all-done = f32[512,2,1024]{2,1,0:T(2,128)} async-done(((f32[512,2,1024]{2,1,0:T(2,128)}), f32[512,2,1024]{2,1,0:T(2,128)}, u32[]{:S(2)}, u32[]{:S(2)}) %all-to-all-start) | async-done | bytes 4194336 | tf_op jit(solution)/shard_map/all_to_all | solution.py:43
  167.6 3.5 %copy.8 = f32[512,2,1024]{2,0,1:T(8,128)S(1)} copy(f32[512,2,1024]{2,1,0:T(2,128)} %all-to-all-done) | data formatting | bytes 8388608 | tf_op jit(solution)/shard_map/all_to_all | solution.py:43
  171.2 2.3 copy.9
  173.5 5.0 %gather_fusion = f32[32,32,1024]{2,1,0:T(8,128)} fusion(f32[32,32,1024]{2,0,1:T(8,128)} %bitcast.55, s32[1024]{0:T(1024)S(1)} %pad_clamp_fusion), kind=kCustom, calls=%fused_computation | custom fusion | bytes 8388736 | tf_op jit(solution)/shard_map/jit(_take)/gather | solution.py:44
  178.4 5.0 %select_bitcast_fusion = f32[32,32,1024]{2,0,1:T(8,128)} fusion(f32[32,32,1024]{2,1,0:T(8,128)} %gather_fusion, pred[32]{0:T(512)(128)(4,1)S(1)} %compare_and_fusion), kind=kLoop, calls=%fused_computation.27 | loop fusion | flops 1048576 | bytes 8388640 | tf_op jit(solution)/shard_map/jit(_take)/select_n | solution.py:44
  183.4 0.0 reduce-scatter.2.cloned.1.call-update
  183.5 53.5 %reduce-scatter.2.cloned.1.call-done = f32[32,4,1024]{2,0,1:T(8,128)} async-done(((f32[32,32,1024]{2,0,1:T(8,128)}), f32[32,4,1024]{2,0,1:T(8,128)}) %reduce-scatter.2.cloned.1.call-update) | async-done | bytes 524304 | tf_op jit(solution)/shard_map/reduce_scatter | solution.py:45
  237.0 1.9 copy.11
  (6 shorter events, 0.0 us)
Async XLA Ops:
  6.5 57.9 %all-gather.2.cloned.1.call-start = ((), (), s32[]{:S(2)}) async-start(), calls=%async_computation.2 | async-start | bytes 4456448 | tf_op jit(solution)/shard_map/all_gather | solution.py:25
  108.7 1.6 copy-start
  116.0 5.3 %copy-start.1 = (s32[32]{0:T(128)S(1)}, s32[32]{0:T(128)}, u32[]{:S(2)}) copy-start(s32[32]{0:T(128)} %param.25) | copy-start | bytes 388
  116.0 51.6 %all-to-all-start = ((f32[512,2,1024]{2,1,0:T(2,128)}), f32[512,2,1024]{2,1,0:T(2,128)}, u32[]{:S(2)}, u32[]{:S(2)}) async-start(f32[512,2,1024]{2,1,0:T(2,128)} %pad_maximum_fusion), calls=%async_computation | async-start | bytes 8388608 | tf_op jit(solution)/shard_map/all_to_all | solution.py:43
  121.3 115.7 %reduce-scatter.2.cloned.1.call-start = ((), (), s32[]{:S(2)}) async-start(), calls=%async_computation.3 | async-start | bytes 4718592 | tf_op jit(solution)/shard_map/reduce_scatter | solution.py:45
Sparse Core Ops, SparseCore 0:
  9.5 54.8 all-gather.1
  183.6 53.3 reduce-scatter.1
where the time goes:
time: 249 us; the launch traced here: 246 us
  waiting for transfers between devices  148 us (59%)
  matrix products  29.6 us (12%)
  local copies, waits for them, and re-layouts  23.6 us (9%)
  other arithmetic  20.7 us (8%)
  between operations  18.5 us (7%)
  starting transfers between devices  5.31 us (2%)
    reduce_scatter x1, waiting for transfers between devices, shards(): summed = lax.psum_scatter(ordered, 'vir', scatter_dimension=1, tiled=True)  53.5 us
    all_gather x1, waiting for transfers between devices, shards(): row_piece = lax.all_gather(flattened, 'occ', axis=0, tiled=True)  48.7 us
    all_to_all x1, waiting for transfers between devices, shards(): lax.all_to_all(partial_value, 'occ', split_axis=0, concat_axis=1, tiled=T...  45.5 us
    dot_general x7, matrix products, block_term(): jnp.dot(left_rows, right_block, preferred_element_type=jnp.float32)  29.6 us
    add x2, other arithmetic, shards(): running + block_term(row_piece[:, offset:offset + entry_count], integrals...  7.61 us
    all_to_all x2, local copies, waits for them, and re-layouts, shards(): lax.all_to_all(partial_value, 'occ', split_axis=0, concat_axis=1, tiled=T...  5.83 us
    another operation x1, other arithmetic, shards(): partial_value = jnp.stack(columns, axis=1)  5.76 us
    all_to_all x1, starting transfers between devices, shards(): lax.all_to_all(partial_value, 'occ', split_axis=0, concat_axis=1, tiled=T...  5.26 us
  transfers between devices with their start and end apart: 3, of which 3 were waited for; matrix products, arithmetic and copies ran while one was open for 1% of the time, Pallas kernels for 0%

commit v1 on v0

v1 whole, which is shorter than its diff:
```python
import functools

import jax
import jax.numpy as jnp
from jax import lax
from jax.experimental import pallas as pl
from jax.experimental.pallas import tpu as pltpu
from jax.sharding import PartitionSpec as P

RING = 4
TILES = 4
LIVE = 2
ROWS = 32
ENTRY = 1024
SLOTS = 2
BLOCKS = 16
LANES = 128
KB = ENTRY // LANES
PIECE = KB // 2 * LIVE * ROWS
META = 16
HALF = ENTRY // 2
CHUNK = 256
CODE = 32700.0
TINY = 1e-33

f32, bf16, i32, i16 = jnp.float32, jnp.bfloat16, jnp.int32, jnp.int16
VMEM = pl.BlockSpec(memory_space=pltpu.VMEM)
SMEM = pl.BlockSpec(memory_space=pltpu.SMEM)
HBM = pl.BlockSpec(memory_space=pl.ANY)


def shape(dims, dtype):
    return jax.ShapeDtypeStruct(dims, dtype)


def params(mib=16):
    return pltpu.CompilerParams(vmem_limit_bytes=mib * 1024 * 1024)


def pack_kernel(live_ref, amp_ref, first_ref, second_ref):
    live = [live_ref[0, c] != 0 for c in range(TILES)]
    c0 = jnp.int32(0)
    for c in reversed(range(TILES)):
        c0 = jnp.where(live[c], c, c0)
    c1 = jnp.int32(TILES)
    for c in reversed(range(TILES)):
        c1 = jnp.where(live[c] & (c > c0), c, c1)
    for slot, c in enumerate((c0, jnp.minimum(c1, TILES - 1))):
        for kb in range(KB):
            start = pl.multiple_of(c * ENTRY + kb * LANES, LANES)
            part = amp_ref[:, pl.ds(start, LANES)]
            half, k = divmod(kb, KB // 2)
            (first_ref, second_ref)[half][pl.ds((k * LIVE + slot) * ROWS, ROWS), :] = part
    row = lax.broadcasted_iota(i32, (META, LANES), 0)
    first_ref[pl.ds(PIECE, META), :] = jnp.where(row < 8, c0, c1).astype(f32).astype(bf16)


def pack(tile_live, amplitudes):
    return pl.pallas_call(
        pack_kernel,
        out_shape=(shape((PIECE + META, LANES), bf16), shape((PIECE, LANES), bf16)),
        in_specs=[SMEM, VMEM],
        out_specs=(VMEM, VMEM),
        compiler_params=params(),
    )(tile_live, amplitudes)


def occ_shift(value, dx, dz):
    pairs = [
        (x * RING + z, (x + dx) % RING * RING + (z + dz) % RING) for x in range(RING) for z in range(RING)
    ]
    return lax.ppermute(value, "occ", pairs)


def vir_shift(value, dy, dc):
    pairs = [(y * 2 + c, (y + dy) % RING * 2 + (c + dc) % 2) for y in range(RING) for c in range(2)]
    return lax.ppermute(value, "vir", pairs)


def compute_kernel(half_ref, live_ref, ints_ref, *refs):
    firsts, seconds = refs[:RING], refs[RING : 2 * RING]
    out_ref, left, block, product, meta_f, meta_v, meta, count, where, sems, meta_sem = refs[2 * RING :]
    half = pl.multiple_of(half_ref[0] * HALF, HALF)

    def fetch(r, c):
        return pltpu.make_async_copy(
            ints_ref.at[r, c, :, pl.ds(half, HALF)], block.at[c * SLOTS + r], sems.at[c * SLOTS + r]
        )

    for c in range(TILES):
        for r in range(SLOTS):
            pl.when(live_ref[r, c] != 0)(lambda: fetch(r, c).start())

    for e in range(RING):
        for d in range(RING):
            o = e * RING + d
            tags = firsts[e][pl.ds(d * (PIECE + META) + PIECE, META), :].astype(f32)
            meta_f[pl.ds(o * META, META), :] = tags
    meta_v[...] = meta_f[...].astype(i32)
    copy = pltpu.make_async_copy(meta_v, meta, meta_sem)
    copy.start()
    out_ref[...] = jnp.zeros_like(out_ref)
    copy.wait()
    for c in range(TILES):
        count[c] = 0

    for e in range(RING):
        for d in range(RING):
            o = e * RING + d
            for slot in range(LIVE):
                c = meta[o * META + slot * 8, 0]

                @pl.when(c < TILES)
                def _():
                    at = count[c]
                    count[c] = at + 1
                    where[c * BLOCKS + at] = o
                    rows = pl.multiple_of(at * ROWS, ROWS)
                    for kb in range(KB):
                        h, k = divmod(kb, KB // 2)
                        source, base = (
                            (firsts[e], d * (PIECE + META)) if h == 0 else (seconds[d], e * PIECE)
                        )
                        left[c, pl.ds(rows, ROWS), kb * LANES : (kb + 1) * LANES] = source[
                            pl.ds(base + (k * LIVE + slot) * ROWS, ROWS), :
                        ]

    def one_block(i, carry):
        c, r = i // SLOTS, i % SLOTS

        @pl.when(live_ref[r, c] != 0)
        def _():
            fetch(r, c).wait()
            n = count[c]

            def one_chunk(j, inner):
                product[...] = jnp.dot(
                    left[c, pl.ds(pl.multiple_of(j * CHUNK, CHUNK), CHUNK), :],
                    block[i],
                    preferred_element_type=f32,
                )

                def add(t, last):
                    o = where[c * BLOCKS + j * (CHUNK // ROWS) + t]
                    rows = pl.multiple_of(t * ROWS, ROWS)
                    for q in range(RING):
                        at = pl.ds(pl.multiple_of((o * SLOTS + r) * ROWS, ROWS), ROWS)
                        out_ref[q, at, :] += product[pl.ds(rows, ROWS), q * LANES : (q + 1) * LANES]
                    return last

                lax.fori_loop(0, jnp.minimum(n - j * (CHUNK // ROWS), CHUNK // ROWS), add, 0)
                return inner

            lax.fori_loop(0, pl.cdiv(n * ROWS, CHUNK), one_chunk, 0)

        return carry

    lax.fori_loop(0, TILES * SLOTS, one_block, 0)


def compute(half, block_live, integrals, firsts, seconds):
    return pl.pallas_call(
        compute_kernel,
        out_shape=shape((RING, BLOCKS * SLOTS * ROWS, LANES), f32),
        in_specs=[SMEM, SMEM, HBM] + [VMEM] * (2 * RING),
        out_specs=VMEM,
        scratch_shapes=[
            pltpu.VMEM((TILES, BLOCKS * ROWS, ENTRY), bf16),
            pltpu.VMEM((TILES * SLOTS, ENTRY, HALF), bf16),
            pltpu.VMEM((CHUNK, HALF), f32),
            pltpu.VMEM((BLOCKS * META, LANES), f32),
            pltpu.VMEM((BLOCKS * META, LANES), i32),
            pltpu.SMEM((BLOCKS * META, LANES), i32),
            pltpu.SMEM((TILES,), i32),
            pltpu.SMEM((TILES * BLOCKS,), i32),
            pltpu.SemaphoreType.DMA((TILES * SLOTS,)),
            pltpu.SemaphoreType.DMA,
        ],
        compiler_params=params(32),
        cost_estimate=pl.CostEstimate(flops=2 * 512 * 4096 * 1024, bytes_accessed=8 << 20, transcendentals=0),
    )(half, block_live, integrals, *firsts, *seconds)


def encode(value):
    top = jnp.maximum(jnp.max(jnp.abs(value), axis=0, keepdims=True), TINY)
    exponent = jnp.ceil(jnp.log(top) * (8.0 / 0.6931471805599453) + 0.01)
    inverse = jnp.exp(exponent * (-0.6931471805599453 / 8.0)) * CODE
    return jnp.round(value * inverse).astype(i32).astype(i16), exponent


def scale_of(exponent):
    return jnp.exp(exponent * (0.6931471805599453 / 8.0)) * (1.0 / CODE)


SUMS = BLOCKS * SLOTS
SUM_ROWS = SUMS * ROWS


def core_sum_kernel(y_ref, mine_ref, other_ref, own_ref, *refs):
    sends, exps = refs[: RING - 1], refs[RING - 1]
    y = y_ref[0]
    for d in range(RING):
        q = lax.rem(y + d, RING)
        if d == 0:
            own_ref[...] = mine_ref[q] + other_ref[q]
            continue

        def group(g, carry):
            at = pl.ds(pl.multiple_of(g * ROWS, ROWS), ROWS)
            codes, exponent = encode(mine_ref[q, at, :] + other_ref[q, at, :])
            sends[d - 1][at, :] = codes
            exps[pl.ds(g, 1), :] = exponent
            return carry

        lax.fori_loop(0, SUMS, group, 0, unroll=4)
        sends[d - 1][pl.ds(SUM_ROWS, SUMS), :] = exps[...].astype(i32).astype(i16)


def core_sum(y, mine, other):
    code = shape((SUM_ROWS + SUMS, LANES), i16)
    return pl.pallas_call(
        core_sum_kernel,
        out_shape=(shape((SUM_ROWS, LANES), f32), code, code, code),
        in_specs=[SMEM, VMEM, VMEM],
        out_specs=(VMEM,) * RING,
        scratch_shapes=[pltpu.VMEM((SUMS, LANES), f32)],
        compiler_params=params(),
    )(y, mine, other)


PART = SLOTS * ROWS + META


def ring_sum_kernel(place_ref, own_ref, a_ref, b_ref, c_ref, out_ref, scales, exps):
    x, z = place_ref[0], place_ref[1]
    codes = (a_ref, b_ref, c_ref)
    for d in range(RING - 1):
        scales[d] = scale_of(codes[d][pl.ds(SUM_ROWS, SUMS), :].astype(i32).astype(f32))
    exps[...] = jnp.zeros_like(exps)

    def block(o, carry):
        e, d = o // RING, lax.rem(o, RING)
        to = lax.rem(x - e + RING, RING) * RING + lax.rem(z - d + RING, RING)
        for r in range(SLOTS):
            g = o * SLOTS + r
            at = pl.ds(pl.multiple_of(g * ROWS, ROWS), ROWS)
            total = own_ref[at, :]
            for k in range(RING - 1):
                total += codes[k][at, :].astype(i32).astype(f32) * scales[k, pl.ds(g, 1), :]
            code, exponent = encode(total)
            out_ref[to, r * ROWS : (r + 1) * ROWS, :] = code
            exps[r : r + 1, :] = exponent
        out_ref[to, SLOTS * ROWS : PART, :] = exps[...].astype(i32).astype(i16)
        return carry

    lax.fori_loop(0, BLOCKS, block, 0, unroll=2)


def ring_sum(place, own, codes):
    return pl.pallas_call(
        ring_sum_kernel,
        out_shape=shape((BLOCKS, PART, LANES), i16),
        in_specs=[SMEM] + [VMEM] * RING,
        out_specs=VMEM,
        scratch_shapes=[pltpu.VMEM((RING - 1, SUMS, LANES), f32), pltpu.VMEM((META, LANES), f32)],
        compiler_params=params(),
    )(place, own, *codes)


RANGES = 8
DEST = TILES * ROWS + META


def reorder_kernel(owner_ref, in_ref, out_ref, exps):
    for s in range(BLOCKS * SLOTS):
        owner, r = divmod(s, SLOTS)
        p = owner_ref[s]
        v, t = p // TILES, lax.rem(p, TILES)
        out_ref[v, pl.ds(pl.multiple_of(t * ROWS, ROWS), ROWS), :] = in_ref[owner, r * ROWS : (r + 1) * ROWS, :]
        tags = in_ref[owner, SLOTS * ROWS : PART, :].astype(i32).astype(f32)
        exps[pl.ds(v * META + t, 1), :] = tags[r : r + 1, :]
    for v in range(RANGES):
        out_ref[v, TILES * ROWS : DEST, :] = exps[v * META : (v + 1) * META, :].astype(i32).astype(i16)


def reorder(row_owner, parts):
    return pl.pallas_call(
        reorder_kernel,
        out_shape=shape((RANGES, DEST, LANES), i16),
        in_specs=[SMEM, VMEM],
        out_specs=VMEM,
        scratch_shapes=[pltpu.VMEM((RANGES * META, LANES), f32)],
        compiler_params=params(),
    )(row_owner, parts)


def finish_kernel(in_ref, out_ref):
    for v in range(RANGES):
        y, core = divmod(v, 2)
        scale = scale_of(in_ref[v, TILES * ROWS : DEST, :].astype(i32).astype(f32))
        for t in range(TILES):
            column = t * ENTRY + core * HALF + y * LANES
            value = in_ref[v, t * ROWS : (t + 1) * ROWS, :].astype(i32).astype(f32)
            out_ref[:, column : column + LANES] = value * scale[t : t + 1, :]


def finish(parts):
    return pl.pallas_call(
        finish_kernel,
        out_shape=shape((ROWS, TILES * ENTRY), f32),
        in_specs=[VMEM],
        out_specs=VMEM,
        compiler_params=params(),
    )(parts)


def shards(amplitudes, tile_live, integrals, block_live, row_owner):
    occ, vir = lax.axis_index("occ"), lax.axis_index("vir")
    x, z, y, core = occ // RING, occ % RING, vir // 2, vir % 2
    place = jnp.stack([x, z]).astype(i32)

    first, second = pack(tile_live, amplitudes)
    along_z = jnp.concatenate([first] + [occ_shift(first, 0, d) for d in range(1, RING)], 0)
    along_x = jnp.concatenate([second] + [occ_shift(second, e, 0) for e in range(1, RING)], 0)
    firsts = [along_z] + [occ_shift(along_z, e, 0) for e in range(1, RING)]
    seconds = [along_x] + [occ_shift(along_x, 0, d) for d in range(1, RING)]

    theirs = compute((1 - core).reshape(1).astype(i32), block_live, integrals, firsts, seconds)
    other = vir_shift(theirs, 0, 1)
    mine = compute(core.reshape(1).astype(i32), block_live, integrals, firsts, seconds)
    own, *sends = core_sum(y.reshape(1).astype(i32), mine, other)
    codes = [vir_shift(sends[d - 1], d, 0) for d in range(1, RING)]
    parts = ring_sum(place, own, codes)
    parts = lax.all_to_all(parts, "occ", split_axis=0, concat_axis=0, tiled=True)
    parts = reorder(row_owner, parts)
    parts = lax.all_to_all(parts, "vir", split_axis=0, concat_axis=0, tiled=True)
    return finish(parts)


def solution(mesh):
    return jax.shard_map(
        shards,
        mesh=mesh,
        in_specs=(
            P("occ", "vir"),
            P("occ", "vir"),
            P("occ", "vir", None, None),
            P("occ", "vir"),
            P(),
        ),
        out_specs=P("occ", "vir"),
        check_vma=False,
    )
```

time: 249 us -> 120 us (0.48); the launches traced: 246 us -> 120 us
  waiting for transfers between devices: 148 us -> 21.7 us
  matrix products: 29.6 us -> 0 us
  blocking collectives: 0 us -> 27.8 us
  Pallas kernels: 0 us -> 23.5 us
  other arithmetic: 20.7 us -> 0.07 us
  starting transfers between devices: 5.31 us -> 25 us
  between operations: 18.5 us -> 0.16 us
    reduce_scatter x1 -> x0, waiting for transfers between devices: 53.5 us -> none  [shards(): summed = lax.psum_scatter(ordered, 'vir', scatter_dimension=1, tiled=True)]
    all_gather x1 -> x0, waiting for transfers between devices: 48.7 us -> none  [shards(): row_piece = lax.all_gather(flattened, 'occ', axis=0, tiled=True)]
    all_to_all x1 -> x0, waiting for transfers between devices: 45.5 us -> none  [shards(): lax.all_to_all(partial_value, 'occ', split_axis=0, concat_axis=1, tiled=T...]
    dot_general x7 -> x0, matrix products: 29.6 us -> none  [block_term(): jnp.dot(left_rows, right_block, preferred_element_type=jnp.float32)]
    all_to_all x0 -> x2, blocking collectives: none -> 27.8 us  [the longest x1 14.3 us: shards(): lax.all_to_all(parts, 'vir', split_axis=0, concat_axis=0, tiled=True)]
    ppermute x0 -> x16, starting transfers between devices: none -> 25 us  [the longest x12 17.2 us: occ_shift(): return lax.ppermute(value, 'occ', pairs)]
    pallas_call x0 -> x7, Pallas kernels: none -> 23.5 us  [the longest x2 17.4 us: compute(): pl.pallas_call(compute_kernel, out_shape=shape((RING, BLOCKS * SLOTS * RO...]
    ppermute x0 -> x16, waiting for transfers between devices: none -> 21.7 us  [the longest x12 11.3 us: occ_shift(): return lax.ppermute(value, 'occ', pairs)]
  transfers between devices with their start and end apart: 3 -> 16, of which waited for: 3 -> 7; matrix products, arithmetic and copies ran while one was open for 1% -> 0% of each run, Pallas kernels for 0% -> 7%
where the time goes in v1:
time: 120 us
  blocking collectives  27.8 us (23%)
  starting transfers between devices  25 us (21%)
  Pallas kernels  23.5 us (20%)
  local copies, waits for them, and re-layouts  21.8 us (18%)
  waiting for transfers between devices  21.7 us (18%)
    unnamed x38, local copies, waits for them, and re-layouts  21.7 us
    pallas_call x2, Pallas kernels, compute(): pl.pallas_call(compute_kernel, out_shape=shape((RING, BLOCKS * SLOTS * RO...  17.4 us
    ppermute x12, starting transfers between devices, occ_shift(): return lax.ppermute(value, 'occ', pairs)  17.2 us
    all_to_all x1, blocking collectives, shards(): lax.all_to_all(parts, 'vir', split_axis=0, concat_axis=0, tiled=True)  14.3 us
    all_to_all x1, blocking collectives, shards(): lax.all_to_all(parts, 'occ', split_axis=0, concat_axis=0, tiled=True)  13.5 us
    ppermute x12, waiting for transfers between devices, occ_shift(): return lax.ppermute(value, 'occ', pairs)  11.3 us
    ppermute x4, waiting for transfers between devices, vir_shift(): return lax.ppermute(value, 'vir', pairs)  10.4 us
    ppermute x4, starting transfers between devices, vir_shift(): return lax.ppermute(value, 'vir', pairs)  7.81 us
  transfers between devices with their start and end apart: 16, of which 7 were waited for; matrix products, arithmetic and copies ran while one was open for 0% of the time, Pallas kernels for 7%

profile of v1, /device:TPU:1, one launch (start us, length us, event | category | flops | bytes accessed | tf_op | source)
XLA Modules:
  0.0 120.1 jit_solution(10603697572205435176)
XLA Ops:
  0.0 0.0 copy-start.11
  0.0 0.9 copy-done.11
  1.0 0.0 copy-start.14
  1.0 0.7 copy-done.14
  1.6 0.6 shard_map.55
  2.2 3.4 %collective-permute-start.8 = (bf16[256,128]{1,0:T(8,128)(2,1)S(1)}, bf16[256,128]{1,0:T(8,128)(2,1)S(1)}, u32[]{:S(2)}, u32[]{:S(2)}) collective-permute-start(bf16[256,128]{1,0:T(8,128)(2,1)S(1)} %get-tuple-element.12), channel_id=1, source_target_pairs={{0,96},{8,104},{16,112},{24,120},{32,0},{40,8},{48,16},{56,24},{64... | collective-permute-start | bytes 196616 | tf_op jit(solution)/shard_map/ppermute | solution.py:72
  5.6 0.5 collective-permute-start.7
  6.1 0.6 collective-permute-start.6
  6.7 3.8 %collective-permute-start.2 = (bf16[272,128]{1,0:T(8,128)(2,1)S(1)}, bf16[272,128]{1,0:T(8,128)(2,1)S(1)}, u32[]{:S(2)}, u32[]{:S(2)}) collective-permute-start(bf16[272,128]{1,0:T(8,128)(2,1)S(1)} %get-tuple-element.11), channel_id=1, source_target_pairs={{0,24},{8,0},{16,8},{24,16},{32,56},{40,32},{48,40},{56,48},{64,88... | collective-permute-start | bytes 208904 | tf_op jit(solution)/shard_map/ppermute | solution.py:72
  10.5 0.0 collective-permute-start.1
  10.5 0.4 collective-permute-done.6
  10.9 1.6 %collective-permute-start = (bf16[272,128]{1,0:T(8,128)(2,1)S(1)}, bf16[272,128]{1,0:T(8,128)(2,1)S(1)}, u32[]{:S(2)}, u32[]{:S(2)}) collective-permute-start(bf16[272,128]{1,0:T(8,128)(2,1)S(1)} %get-tuple-element.11), channel_id=1, source_target_pairs={{0,8},{8,16},{16,24},{24,0},{32,40},{40,48},{48,56},{56,32},{64,72... | collective-permute-start | bytes 208904 | tf_op jit(solution)/shard_map/ppermute | solution.py:72
  12.5 0.0 collective-permute-done.7
  12.6 0.0 collective-permute-done.8
  12.6 2.2 %collective-permute-start.11 = (bf16[1024,128]{1,0:T(8,128)(2,1)S(1)}, bf16[1024,128]{1,0:T(8,128)(2,1)S(1)}, u32[]{:S(2)}, u32[]{:S(2)}) collective-permute-start(bf16[1024,128]{1,0:T(8,128)(2,1)S(1)} %constant_dynamic-update-slice_fusion.4.refs_4_), channel_id=1, source_target_pairs={{0,24},{8,0},{16,8},{24,16},{32,56},{40,32},{48,40},{56,48},{64,88... | collective-permute-start | bytes 786440 | tf_op jit(solution)/shard_map/ppermute | solution.py:72
  14.8 1.6 %collective-permute-done = bf16[272,128]{1,0:T(8,128)(2,1)S(1)} collective-permute-done((bf16[272,128]{1,0:T(8,128)(2,1)S(1)}, bf16[272,128]{1,0:T(8,128)(2,1)S(1)}, u32[]{:S(2)}, u32[]{:S(2)}) %collective-permute-start) | collective-permute-done | bytes 69664 | tf_op jit(solution)/shard_map/ppermute | solution.py:72
  16.4 0.0 collective-permute-done.1
  16.4 0.0 collective-permute-done.2
  16.4 1.5 %collective-permute-start.5 = (bf16[1088,128]{1,0:T(8,128)(2,1)S(1)}, bf16[1088,128]{1,0:T(8,128)(2,1)S(1)}, u32[]{:S(2)}, u32[]{:S(2)}) collective-permute-start(bf16[1088,128]{1,0:T(8,128)(2,1)S(1)} %constant_dynamic-update-slice_fusion.refs_0_), channel_id=1, source_target_pairs={{0,96},{8,104},{16,112},{24,120},{32,0},{40,8},{48,16},{56,24},{64... | collective-permute-start | bytes 835592 | tf_op jit(solution)/shard_map/ppermute | solution.py:72
  17.9 1.2 %collective-permute-start.4 = (bf16[1088,128]{1,0:T(8,128)(2,1)S(1)}, bf16[1088,128]{1,0:T(8,128)(2,1)S(1)}, u32[]{:S(2)}, u32[]{:S(2)}) collective-permute-start(bf16[1088,128]{1,0:T(8,128)(2,1)S(1)} %constant_dynamic-update-slice_fusion.refs_0_), channel_id=1, source_target_pairs={{0,64},{8,72},{16,80},{24,88},{32,96},{40,104},{48,112},{56,120},{... | collective-permute-start | bytes 835592 | tf_op jit(solution)/shard_map/ppermute | solution.py:72
  19.1 0.0 collective-permute-start.3
  19.1 1.7 %collective-permute-start.10 = (bf16[1024,128]{1,0:T(8,128)(2,1)S(1)}, bf16[1024,128]{1,0:T(8,128)(2,1)S(1)}, u32[]{:S(2)}, u32[]{:S(2)}) collective-permute-start(bf16[1024,128]{1,0:T(8,128)(2,1)S(1)} %constant_dynamic-update-slice_fusion.4.refs_4_), channel_id=1, source_target_pairs={{0,16},{8,24},{16,0},{24,8},{32,48},{40,56},{48,32},{56,40},{64,80... | collective-permute-start | bytes 786440 | tf_op jit(solution)/shard_map/ppermute | solution.py:72
  20.9 0.0 collective-permute-done.11.refs_7_
  20.9 0.7 copy-done.2
  21.6 0.7 collective-permute-start.9
  22.3 3.9 %collective-permute-done.10.refs_6_ = bf16[1024,128]{1,0:T(8,128)(2,1)S(1)} collective-permute-done((bf16[1024,128]{1,0:T(8,128)(2,1)S(1)}, bf16[1024,128]{1,0:T(8,128)(2,1)S(1)}, u32[]{:S(2)}, u32[]{:S(2)}) %collective-permute-start.10) | collective-permute-done | bytes 262176 | tf_op jit(solution)/shard_map/ppermute | solution.py:72
  26.2 0.0 copy-start.5
  26.2 0.7 copy-done.5
  26.9 5.5 %collective-permute-done.9.refs_5_ = bf16[1024,128]{1,0:T(8,128)(2,1)S(1)} collective-permute-done((bf16[1024,128]{1,0:T(8,128)(2,1)S(1)}, bf16[1024,128]{1,0:T(8,128)(2,1)S(1)}, u32[]{:S(2)}, u32[]{:S(2)}) %collective-permute-start.9) | collective-permute-done | bytes 262176 | tf_op jit(solution)/shard_map/ppermute | solution.py:72
  32.3 0.0 copy-start.8
  32.3 0.7 copy-done.8
  33.0 0.0 collective-permute-done.5.refs_3_
  33.0 0.0 collective-permute-done.4.refs_2_
  33.0 0.0 collective-permute-done.3.refs_1_
  33.1 0.0 copy-start
  33.1 5.8 %copy-done = bf16[2,4,1024,1024]{3,2,1,0:T(8,128)(2,1)S(1)} copy-done((bf16[2,4,1024,1024]{3,2,1,0:T(8,128)(2,1)S(1)}, bf16[2,4,1024,1024]{3,2,1,0:T(8,128)(2,1)}, u32[]{:S(2)}) %copy-start) | copy-done | bytes 16777240
  38.8 0.9 copy-done.3
  39.8 0.9 copy-done.6
  40.7 0.9 copy-done.9
  41.7 0.7 copy-done.12
  42.4 8.7 %shard_map.57 = f32[4,1024,128]{2,1,0:T(8,128)S(1)} custom-call(s32[1]{0:T(128)} %bitcast.4.half_ref, s32[2,4]{1,0:T(2,128)S(1)} %copy-done.12, bf16[2,4,1024,1024]{3,2,1,0:T(8,128)(2,1)S(1)} %copy-done, bf16[1088,128]{1,0:T(8,128)(2,1)S(1)} %constant_dynamic-update-slice_fusion.refs_0_, bf16[1088,128]{1,0:T(8,128)(2,1)S(1)} %collective-permute-done.3.refs_1_, ...), custom_call_target="tpu_custom_call" | custom-call | flops 4294967296 | bytes 8388608 | tf_op jit(solution)/shard_map/pallas_call | solution.py:162
  51.1 2.7 %collective-permute-start.12 = (f32[4,1024,128]{2,1,0:T(8,128)S(1)}, f32[4,1024,128]{2,1,0:T(8,128)}, u32[]{:S(2)}, u32[]{:S(2)}) collective-permute-start(f32[4,1024,128]{2,1,0:T(8,128)S(1)} %shard_map.57), channel_id=1, source_target_pairs={{0,1},{1,0},{2,3},{3,2},{4,5},{5,4},{6,7},{7,6},{8,9},{9,8},{10,11... | collective-permute-start | bytes 6291464 | tf_op jit(solution)/shard_map/ppermute | solution.py:77
  53.8 0.0 copy-done.13
  53.8 5.8 %copy-done.1 = bf16[2,4,1024,1024]{3,2,1,0:T(8,128)(2,1)S(1)} copy-done((bf16[2,4,1024,1024]{3,2,1,0:T(8,128)(2,1)S(1)}, bf16[2,4,1024,1024]{3,2,1,0:T(8,128)(2,1)}, u32[]{:S(2)}) %copy-start.1) | copy-done | bytes 16777240
  59.5 0.9 copy-done.4
  60.5 0.9 copy-done.7
  61.4 0.9 copy-done.10
  62.4 8.7 %shard_map.56.mine_ref = f32[4,1024,128]{2,1,0:T(8,128)S(1)} custom-call(s32[1]{0:T(128)} %bitcast.3.half_ref, s32[2,4]{1,0:T(2,128)S(1)} %copy-done.13, bf16[2,4,1024,1024]{3,2,1,0:T(8,128)(2,1)S(1)} %copy-done.1, bf16[1088,128]{1,0:T(8,128)(2,1)S(1)} %constant_dynamic-update-slice_fusion.refs_0_, bf16[1088,128]{1,0:T(8,128)(2,1)S(1)} %collective-permute-done.3.refs_1_, ...), custom_call_target="tpu_custom_call" | custom-call | flops 4294967296 | bytes 8388608 | tf_op jit(solution)/shard_map/pallas_call | solution.py:162
  71.1 0.0 collective-permute-done.12.other_ref
  71.1 2.7 %shard_map.58 = (f32[1024,128]{1,0:T(8,128)S(1)}, s16[1056,128]{1,0:T(8,128)(2,1)S(1)}, s16[1056,128]{1,0:T(8,128)(2,1)S(1)}, s16[1056,128]{1,0:T(8,128)(2,1)S(1)}) custom-call(s32[1]{0:T(128)} %bitcast.2.y_ref, f32[4,1024,128]{2,1,0:T(8,128)S(1)} %shard_map.56.mine_ref, f32[4,1024,128]{2,1,0:T(8,128)} %collective-permute-done.12.other_ref), custom_call_target="tpu_custom_call" | custom-call | tf_op jit(solution)/shard_map/pallas_call | solution.py:221
  73.9 0.0 copy-start.15
  73.9 1.3 %collective-permute-start.13 = (s16[1056,128]{1,0:T(8,128)(2,1)S(1)}, s16[1056,128]{1,0:T(8,128)(2,1)S(1)}, u32[]{:S(2)}, u32[]{:S(2)}) collective-permute-start(s16[1056,128]{1,0:T(8,128)(2,1)S(1)} %get-tuple-element.14), channel_id=1, source_target_pairs={{0,2},{1,3},{2,4},{3,5},{4,6},{5,7},{6,0},{7,1},{8,10},{9,11},{10,... | collective-permute-start | bytes 811016 | tf_op jit(solution)/shard_map/ppermute | solution.py:77
  75.1 3.1 %collective-permute-start.14 = (s16[1056,128]{1,0:T(8,128)(2,1)S(1)}, s16[1056,128]{1,0:T(8,128)(2,1)S(1)}, u32[]{:S(2)}, u32[]{:S(2)}) collective-permute-start(s16[1056,128]{1,0:T(8,128)(2,1)S(1)} %get-tuple-element.15), channel_id=1, source_target_pairs={{0,4},{1,5},{2,6},{3,7},{4,0},{5,1},{6,2},{7,3},{8,12},{9,13},{10,... | collective-permute-start | bytes 811016 | tf_op jit(solution)/shard_map/ppermute | solution.py:77
  78.3 0.7 collective-permute-start.15
  79.0 0.1 pad_add_fusion.place_ref
  79.1 3.1 %collective-permute-done.13.a_ref = s16[1056,128]{1,0:T(8,128)(2,1)S(1)} collective-permute-done((s16[1056,128]{1,0:T(8,128)(2,1)S(1)}, s16[1056,128]{1,0:T(8,128)(2,1)S(1)}, u32[]{:S(2)}, u32[]{:S(2)}) %collective-permute-start.13) | collective-permute-done | bytes 270368 | tf_op jit(solution)/shard_map/ppermute | solution.py:77
  82.2 6.7 %collective-permute-done.14.b_ref = s16[1056,128]{1,0:T(8,128)(2,1)S(1)} collective-permute-done((s16[1056,128]{1,0:T(8,128)(2,1)S(1)}, s16[1056,128]{1,0:T(8,128)(2,1)S(1)}, u32[]{:S(2)}, u32[]{:S(2)}) %collective-permute-start.14) | collective-permute-done | bytes 270368 | tf_op jit(solution)/shard_map/ppermute | solution.py:77
  88.9 0.6 collective-permute-done.15.c_ref
  89.5 1.1 shard_map.59
  90.6 13.5 %all_to_all.10.in_ref = s16[16,80,128]{2,1,0:T(8,128)(2,1)S(1)} all-to-all(s16[16,80,128]{2,1,0:T(8,128)(2,1)S(1)} %shard_map.59), channel_id=1, replica_groups=mesh['occ'=16,'vir'=8] {'occ'}, dimensions={0} | all-to-all | bytes 655360 | tf_op jit(solution)/shard_map/all_to_all | solution.py:334
  104.1 0.0 copy-done.15
  104.1 0.8 shard_map.60
  104.9 14.3 %all_to_all.11.in_ref = s16[8,144,128]{2,1,0:T(8,128)(2,1)S(1)} all-to-all(s16[8,144,128]{2,1,0:T(8,128)(2,1)S(1)} %shard_map.60), channel_id=1, replica_groups=mesh['occ'=16,'vir'=8] {'vir'}, dimensions={0} | all-to-all | bytes 589824 | tf_op jit(solution)/shard_map/all_to_all | solution.py:336
  119.2 0.9 shard_map.61
  (18 shorter events, 0.1 us)
Async XLA Ops:
  0.0 0.9 copy-start.11
  1.0 0.7 copy-start.14
  2.2 10.4 %collective-permute-start.8 = (bf16[256,128]{1,0:T(8,128)(2,1)S(1)}, bf16[256,128]{1,0:T(8,128)(2,1)S(1)}, u32[]{:S(2)}, u32[]{:S(2)}) collective-permute-start(bf16[256,128]{1,0:T(8,128)(2,1)S(1)} %get-tuple-element.12), channel_id=1, source_target_pairs={{0,96},{8,104},{16,112},{24,120},{32,0},{40,8},{48,16},{56,24},{64... | collective-permute-start | bytes 196616 | tf_op jit(solution)/shard_map/ppermute | solution.py:72
  5.6 7.0 %collective-permute-start.7 = (bf16[256,128]{1,0:T(8,128)(2,1)S(1)}, bf16[256,128]{1,0:T(8,128)(2,1)S(1)}, u32[]{:S(2)}, u32[]{:S(2)}) collective-permute-start(bf16[256,128]{1,0:T(8,128)(2,1)S(1)} %get-tuple-element.12), channel_id=1, source_target_pairs={{0,64},{8,72},{16,80},{24,88},{32,96},{40,104},{48,112},{56,120},{... | collective-permute-start | bytes 196616 | tf_op jit(solution)/shard_map/ppermute | solution.py:72
  6.1 4.8 %collective-permute-start.6 = (bf16[256,128]{1,0:T(8,128)(2,1)S(1)}, bf16[256,128]{1,0:T(8,128)(2,1)S(1)}, u32[]{:S(2)}, u32[]{:S(2)}) collective-permute-start(bf16[256,128]{1,0:T(8,128)(2,1)S(1)} %get-tuple-element.12), channel_id=1, source_target_pairs={{0,32},{8,40},{16,48},{24,56},{32,64},{40,72},{48,80},{56,88},{64,... | collective-permute-start | bytes 196616 | tf_op jit(solution)/shard_map/ppermute | solution.py:72
  6.7 9.7 %collective-permute-start.2 = (bf16[272,128]{1,0:T(8,128)(2,1)S(1)}, bf16[272,128]{1,0:T(8,128)(2,1)S(1)}, u32[]{:S(2)}, u32[]{:S(2)}) collective-permute-start(bf16[272,128]{1,0:T(8,128)(2,1)S(1)} %get-tuple-element.11), channel_id=1, source_target_pairs={{0,24},{8,0},{16,8},{24,16},{32,56},{40,32},{48,40},{56,48},{64,88... | collective-permute-start | bytes 208904 | tf_op jit(solution)/shard_map/ppermute | solution.py:72
  10.5 5.9 %collective-permute-start.1 = (bf16[272,128]{1,0:T(8,128)(2,1)S(1)}, bf16[272,128]{1,0:T(8,128)(2,1)S(1)}, u32[]{:S(2)}, u32[]{:S(2)}) collective-permute-start(bf16[272,128]{1,0:T(8,128)(2,1)S(1)} %get-tuple-element.11), channel_id=1, source_target_pairs={{0,16},{8,24},{16,0},{24,8},{32,48},{40,56},{48,32},{56,40},{64,80... | collective-permute-start | bytes 208904 | tf_op jit(solution)/shard_map/ppermute | solution.py:72
  10.9 5.5 %collective-permute-start = (bf16[272,128]{1,0:T(8,128)(2,1)S(1)}, bf16[272,128]{1,0:T(8,128)(2,1)S(1)}, u32[]{:S(2)}, u32[]{:S(2)}) collective-permute-start(bf16[272,128]{1,0:T(8,128)(2,1)S(1)} %get-tuple-element.11), channel_id=1, source_target_pairs={{0,8},{8,16},{16,24},{24,0},{32,40},{40,48},{48,56},{56,32},{64,72... | collective-permute-start | bytes 208904 | tf_op jit(solution)/shard_map/ppermute | solution.py:72
  12.6 8.3 %collective-permute-start.11 = (bf16[1024,128]{1,0:T(8,128)(2,1)S(1)}, bf16[1024,128]{1,0:T(8,128)(2,1)S(1)}, u32[]{:S(2)}, u32[]{:S(2)}) collective-permute-start(bf16[1024,128]{1,0:T(8,128)(2,1)S(1)} %constant_dynamic-update-slice_fusion.4.refs_4_), channel_id=1, source_target_pairs={{0,24},{8,0},{16,8},{24,16},{32,56},{40,32},{48,40},{56,48},{64,88... | collective-permute-start | bytes 786440 | tf_op jit(solution)/shard_map/ppermute | solution.py:72
  16.4 16.6 %collective-permute-start.5 = (bf16[1088,128]{1,0:T(8,128)(2,1)S(1)}, bf16[1088,128]{1,0:T(8,128)(2,1)S(1)}, u32[]{:S(2)}, u32[]{:S(2)}) collective-permute-start(bf16[1088,128]{1,0:T(8,128)(2,1)S(1)} %constant_dynamic-update-slice_fusion.refs_0_), channel_id=1, source_target_pairs={{0,96},{8,104},{16,112},{24,120},{32,0},{40,8},{48,16},{56,24},{64... | collective-permute-start | bytes 835592 | tf_op jit(solution)/shard_map/ppermute | solution.py:72
  17.9 15.2 %collective-permute-start.4 = (bf16[1088,128]{1,0:T(8,128)(2,1)S(1)}, bf16[1088,128]{1,0:T(8,128)(2,1)S(1)}, u32[]{:S(2)}, u32[]{:S(2)}) collective-permute-start(bf16[1088,128]{1,0:T(8,128)(2,1)S(1)} %constant_dynamic-update-slice_fusion.refs_0_), channel_id=1, source_target_pairs={{0,64},{8,72},{16,80},{24,88},{32,96},{40,104},{48,112},{56,120},{... | collective-permute-start | bytes 835592 | tf_op jit(solution)/shard_map/ppermute | solution.py:72
  19.1 13.9 %collective-permute-start.3 = (bf16[1088,128]{1,0:T(8,128)(2,1)S(1)}, bf16[1088,128]{1,0:T(8,128)(2,1)S(1)}, u32[]{:S(2)}, u32[]{:S(2)}) collective-permute-start(bf16[1088,128]{1,0:T(8,128)(2,1)S(1)} %constant_dynamic-update-slice_fusion.refs_0_), channel_id=1, source_target_pairs={{0,32},{8,40},{16,48},{24,56},{32,64},{40,72},{48,80},{56,88},{64,... | collective-permute-start | bytes 835592 | tf_op jit(solution)/shard_map/ppermute | solution.py:72
  19.1 7.0 %collective-permute-start.10 = (bf16[1024,128]{1,0:T(8,128)(2,1)S(1)}, bf16[1024,128]{1,0:T(8,128)(2,1)S(1)}, u32[]{:S(2)}, u32[]{:S(2)}) collective-permute-start(bf16[1024,128]{1,0:T(8,128)(2,1)S(1)} %constant_dynamic-update-slice_fusion.4.refs_4_), channel_id=1, source_target_pairs={{0,16},{8,24},{16,0},{24,8},{32,48},{40,56},{48,32},{56,40},{64,80... | collective-permute-start | bytes 786440 | tf_op jit(solution)/shard_map/ppermute | solution.py:72
  20.9 0.7 copy-start.2
  21.6 10.7 %collective-permute-start.9 = (bf16[1024,128]{1,0:T(8,128)(2,1)S(1)}, bf16[1024,128]{1,0:T(8,128)(2,1)S(1)}, u32[]{:S(2)}, u32[]{:S(2)}) collective-permute-start(bf16[1024,128]{1,0:T(8,128)(2,1)S(1)} %constant_dynamic-update-slice_fusion.4.refs_4_), channel_id=1, source_target_pairs={{0,8},{8,16},{16,24},{24,0},{32,40},{40,48},{48,56},{56,32},{64,72... | collective-permute-start | bytes 786440 | tf_op jit(solution)/shard_map/ppermute | solution.py:72
  26.2 0.7 copy-start.5
  32.3 0.7 copy-start.8
  33.1 5.8 %copy-start = (bf16[2,4,1024,1024]{3,2,1,0:T(8,128)(2,1)S(1)}, bf16[2,4,1024,1024]{3,2,1,0:T(8,128)(2,1)}, u32[]{:S(2)}) copy-start(bf16[2,4,1024,1024]{3,2,1,0:T(8,128)(2,1)} %ints_ref.3) | copy-start | bytes 50331652
  38.8 0.9 copy-start.3
  39.8 0.9 copy-start.6
  40.7 0.9 copy-start.9
  41.7 0.7 copy-start.12
  42.4 11.4 %copy-start.13 = (s32[2,4]{1,0:T(2,128)S(1)}, s32[2,4]{1,0:T(2,128)}, u32[]{:S(2)}) copy-start(s32[2,4]{1,0:T(2,128)} %live_ref.5) | copy-start | bytes 100
  51.1 20.0 %collective-permute-start.12 = (f32[4,1024,128]{2,1,0:T(8,128)S(1)}, f32[4,1024,128]{2,1,0:T(8,128)}, u32[]{:S(2)}, u32[]{:S(2)}) collective-permute-start(f32[4,1024,128]{2,1,0:T(8,128)S(1)} %shard_map.57), channel_id=1, source_target_pairs={{0,1},{1,0},{2,3},{3,2},{4,5},{5,4},{6,7},{7,6},{8,9},{9,8},{10,11... | collective-permute-start | bytes 6291464 | tf_op jit(solution)/shard_map/ppermute | solution.py:77
  53.8 5.8 %copy-start.1 = (bf16[2,4,1024,1024]{3,2,1,0:T(8,128)(2,1)S(1)}, bf16[2,4,1024,1024]{3,2,1,0:T(8,128)(2,1)}, u32[]{:S(2)}) copy-start(bf16[2,4,1024,1024]{3,2,1,0:T(8,128)(2,1)} %ints_ref.3) | copy-start | bytes 50331652
  59.5 0.9 copy-start.4
  60.5 0.9 copy-start.7
  61.4 0.9 copy-start.10
  73.9 30.3 %copy-start.15 = (s32[32]{0:T(128)S(1)}, s32[32]{0:T(128)}, u32[]{:S(2)}) copy-start(s32[32]{0:T(128)} %owner_ref.1) | copy-start | bytes 388
  73.9 8.3 %collective-permute-start.13 = (s16[1056,128]{1,0:T(8,128)(2,1)S(1)}, s16[1056,128]{1,0:T(8,128)(2,1)S(1)}, u32[]{:S(2)}, u32[]{:S(2)}) collective-permute-start(s16[1056,128]{1,0:T(8,128)(2,1)S(1)} %get-tuple-element.14), channel_id=1, source_target_pairs={{0,2},{1,3},{2,4},{3,5},{4,6},{5,7},{6,0},{7,1},{8,10},{9,11},{10,... | collective-permute-start | bytes 811016 | tf_op jit(solution)/shard_map/ppermute | solution.py:77
  75.1 13.7 %collective-permute-start.14 = (s16[1056,128]{1,0:T(8,128)(2,1)S(1)}, s16[1056,128]{1,0:T(8,128)(2,1)S(1)}, u32[]{:S(2)}, u32[]{:S(2)}) collective-permute-start(s16[1056,128]{1,0:T(8,128)(2,1)S(1)} %get-tuple-element.15), channel_id=1, source_target_pairs={{0,4},{1,5},{2,6},{3,7},{4,0},{5,1},{6,2},{7,3},{8,12},{9,13},{10,... | collective-permute-start | bytes 811016 | tf_op jit(solution)/shard_map/ppermute | solution.py:77
  78.3 11.2 %collective-permute-start.15 = (s16[1056,128]{1,0:T(8,128)(2,1)S(1)}, s16[1056,128]{1,0:T(8,128)(2,1)S(1)}, u32[]{:S(2)}, u32[]{:S(2)}) collective-permute-start(s16[1056,128]{1,0:T(8,128)(2,1)S(1)} %get-tuple-element.16), channel_id=1, source_target_pairs={{0,6},{1,7},{2,0},{3,1},{4,2},{5,3},{6,4},{7,5},{8,14},{9,15},{10,... | collective-permute-start | bytes 811016 | tf_op jit(solution)/shard_map/ppermute | solution.py:77

commit v2 on v1

v2 whole, which is shorter than its diff:
```python
import functools

import jax
import jax.numpy as jnp
from jax import lax
from jax.experimental import pallas as pl
from jax.experimental.pallas import tpu as pltpu
from jax.sharding import PartitionSpec as P

RING = 4
TILES = 4
LIVE = 2
ROWS = 32
ENTRY = 1024
SLOTS = 2
BLOCKS = 16
LANES = 128
KB = ENTRY // LANES
META = 16
TAG = KB * LIVE * ROWS
PIECE = TAG + META
HALF = ENTRY // 2
CHUNK = 256
SIZES = (64, 128, CHUNK)
CODE = 32700.0
TINY = 1e-33

f32, bf16, i32, i16 = jnp.float32, jnp.bfloat16, jnp.int32, jnp.int16
VMEM = pl.BlockSpec(memory_space=pltpu.VMEM)
SMEM = pl.BlockSpec(memory_space=pltpu.SMEM)
HBM = pl.BlockSpec(memory_space=pltpu.HBM)
ANY = pl.BlockSpec(memory_space=pl.ANY)


def shape(dims, dtype):
    return jax.ShapeDtypeStruct(dims, dtype)


def in_hbm(*arrays):
    return [pltpu.with_memory_space_constraint(a, pltpu.HBM) for a in arrays]


def in_vmem(*arrays):
    return [pltpu.with_memory_space_constraint(a, pltpu.VMEM) for a in arrays]


def params(mib=4):
    return pltpu.CompilerParams(vmem_limit_bytes=mib * 1024 * 1024)


def pack_kernel(live_hbm, amp_hbm, out_ref, amp, live, sems):
    copies = (
        pltpu.make_async_copy(live_hbm, live, sems.at[0]),
        pltpu.make_async_copy(amp_hbm, amp, sems.at[1]),
    )
    for copy in copies:
        copy.start()
    for copy in copies:
        copy.wait()
    c0 = jnp.int32(0)
    for c in reversed(range(TILES)):
        c0 = jnp.where(live[0, c] != 0, c, c0)
    c1 = jnp.int32(TILES)
    for c in reversed(range(TILES)):
        c1 = jnp.where((live[0, c] != 0) & (c > c0), c, c1)
    for slot, c in enumerate((c0, jnp.minimum(c1, TILES - 1))):
        for kb in range(KB):
            start = pl.multiple_of(c * ENTRY + kb * LANES, LANES)
            out_ref[pl.ds((kb * LIVE + slot) * ROWS, ROWS), :] = amp[:, pl.ds(start, LANES)]
    tag = jnp.full((META, LANES), c0 * 8 + c1, i32)
    out_ref[pl.ds(TAG, META), :] = tag.astype(f32).astype(bf16)


def pack(tile_live, amplitudes):
    return pl.pallas_call(
        pack_kernel,
        out_shape=shape((PIECE, LANES), bf16),
        in_specs=[HBM, HBM],
        out_specs=VMEM,
        scratch_shapes=[
            pltpu.VMEM(amplitudes.shape, bf16),
            pltpu.SMEM(tile_live.shape, i32),
            pltpu.SemaphoreType.DMA((2,)),
        ],
        compiler_params=params(),
    )(*in_hbm(tile_live, amplitudes))


def shift(value, place):
    def index(x, z, y, core):
        return ((x % RING) * RING + z % RING) * 2 * RING + (y % RING) * 2 + core % 2

    spots = [(x, z, y, c) for x in range(RING) for z in range(RING) for y in range(RING) for c in range(2)]
    return lax.ppermute(value, ("occ", "vir"), [(index(*s), index(*place(*s))) for s in spots])


def shift_first(value, n):
    return shift(value, lambda x, z, y, c: (x, z + n, y, c) if c == 0 else (x + n, z, y, c))


def shift_second(value, n):
    return shift(value, lambda x, z, y, c: (x + n, z, y, c) if c == 0 else (x, z + n, y, c))


def shift_y(value, n):
    return shift(value, lambda x, z, y, c: (x, z, y + n, c))


def shift_core(value):
    return shift(value, lambda x, z, y, c: (x, z, y, c + 1))


NEAR = (0, 1, 3)
GROUPS = (
    [(e, d) for e in NEAR for d in NEAR],
    [(2, d) for d in range(RING)] + [(e, 2) for e in NEAR],
)


def compute_kernel(group, shifts, fetches, core_ref, live_hbm, ints_hbm, block_in, *refs):
    amps = dict(zip(shifts, refs[: len(shifts)]))
    refs = refs[len(shifts) :]
    theirs_ref, mine_ref, block_ref, left, product, table_v, table, live, count, where, sem, sems = refs
    del block_in
    core = core_ref[0]
    copy_live = pltpu.make_async_copy(live_hbm, live, sem.at[0])
    copy_live.start()

    lane = lax.broadcasted_iota(i32, (8, LANES), 1)
    entries = jnp.zeros((8, LANES), i32)
    for k, (a, b) in enumerate(group):
        tag = amps[a][pl.ds(b * PIECE + TAG, META), :].astype(f32)[:8].astype(i32)
        entries = jnp.where(lane == k, tag, entries)
    table_v[...] = entries
    copy_table = pltpu.make_async_copy(table_v, table, sem.at[1])
    copy_table.start()

    def fetch(i):
        return pltpu.make_async_copy(ints_hbm.at[lax.rem(i, SLOTS), i // SLOTS], block_ref.at[i], sems.at[i])

    copy_live.wait()
    if fetches:
        for i in range(TILES * SLOTS):
            pl.when(live[i % SLOTS, i // SLOTS] != 0)(functools.partial(lambda i: fetch(i).start(), i))
    theirs_ref[...] = jnp.zeros_like(theirs_ref)
    mine_ref[...] = jnp.zeros_like(mine_ref)
    for c in range(TILES):
        count[c] = 0
    copy_table.wait()

    for k, (a, b) in enumerate(group):
        tag = table[0, k]
        o = jnp.where(core == 0, k, group.index((b, a)))
        for slot in range(LIVE):
            c = tag // 8 if slot == 0 else lax.rem(tag, 8)

            @pl.when(c < TILES)
            def _():
                at = count[c]
                count[c] = at + 1
                where[c * BLOCKS + at] = o
                rows = pl.multiple_of(at * ROWS, ROWS)
                for kb in range(KB):
                    left[c, pl.ds(rows, ROWS), kb * LANES : (kb + 1) * LANES] = amps[a][
                        pl.ds(b * PIECE + (kb * LIVE + slot) * ROWS, ROWS), :
                    ]

    def one_block(i, carry):
        c, r = i // SLOTS, lax.rem(i, SLOTS)

        @pl.when(live[r, c] != 0)
        def _():
            if fetches:
                fetch(i).wait()
            n = count[c]

            def one_chunk(j, inner):
                rest = n - j * (CHUNK // ROWS)
                start = pl.multiple_of(j * CHUNK, CHUNK)

                def multiply(rows):
                    product[:rows, :] = jnp.dot(
                        left[c, pl.ds(start, rows), :], block_ref[i], preferred_element_type=f32
                    )

                low = 0
                for rows in SIZES:
                    tiles = rows // ROWS
                    pl.when((rest > low) & ((rest <= tiles) | (rows == CHUNK)))(functools.partial(multiply, rows))
                    low = tiles

                def add(t, last):
                    o = where[c * BLOCKS + j * (CHUNK // ROWS) + t]
                    rows = pl.ds(pl.multiple_of(t * ROWS, ROWS), ROWS)
                    at = pl.ds(pl.multiple_of((o * SLOTS + r) * ROWS, ROWS), ROWS)
                    for part, ref in enumerate((mine_ref, theirs_ref)):
                        start = pl.multiple_of(jnp.where(core == 0, part, 1 - part) * HALF, HALF)
                        for q in range(RING):
                            ref[q, at, :] += product[rows, pl.ds(start + q * LANES, LANES)]
                    return last

                lax.fori_loop(0, jnp.minimum(rest, CHUNK // ROWS), add, 0)
                return inner

            lax.fori_loop(0, pl.cdiv(n * ROWS, CHUNK), one_chunk, 0)

        return carry

    lax.fori_loop(0, TILES * SLOTS, one_block, 0)


def compute(which, core, block_live, integrals, blocks, amps):
    group = GROUPS[which]
    shifts = sorted(amps)
    fetches = blocks is None
    total = pltpu.VMEM((RING, len(group) * SLOTS * ROWS, LANES), f32)
    held = (TILES * SLOTS, ENTRY, ENTRY)
    return pl.pallas_call(
        functools.partial(compute_kernel, group, shifts, fetches),
        out_shape=(total, total, pltpu.VMEM(held, bf16)),
        in_specs=[SMEM, HBM, HBM] + [SMEM if fetches else VMEM] + [VMEM] * len(shifts),
        out_specs=(VMEM,) * 3,
        input_output_aliases={} if fetches else {3: 2},
        scratch_shapes=[
            pltpu.VMEM((TILES, 2 * CHUNK, ENTRY), bf16),
            pltpu.VMEM((CHUNK, ENTRY), f32),
            pltpu.VMEM((8, LANES), i32),
            pltpu.SMEM((8, LANES), i32),
            pltpu.SMEM(block_live.shape, i32),
            pltpu.SMEM((TILES,), i32),
            pltpu.SMEM((TILES * BLOCKS,), i32),
            pltpu.SemaphoreType.DMA((2,)),
            pltpu.SemaphoreType.DMA((TILES * SLOTS,)),
        ],
        compiler_params=params(8),
        cost_estimate=pl.CostEstimate(flops=1 << 32, bytes_accessed=8 << 20, transcendentals=0),
    )(core, *in_hbm(block_live, integrals), *([core] if fetches else in_vmem(blocks)), *[amps[a] for a in shifts])


def encode(value):
    top = jnp.maximum(jnp.max(jnp.abs(value), axis=0, keepdims=True), TINY)
    exponent = jnp.ceil(jnp.log(top) * (8.0 / 0.6931471805599453) + 0.01)
    inverse = jnp.exp(exponent * (-0.6931471805599453 / 8.0)) * CODE
    return jnp.round(value * inverse).astype(i32).astype(i16), exponent


def scale_of(exponent):
    return jnp.exp(exponent * (0.6931471805599453 / 8.0)) * (1.0 / CODE)


def tag_rows(sums):
    return pl.cdiv(sums, META) * META


def core_sum_kernel(y_ref, mine_ref, other_ref, own_ref, *refs):
    sends, exps = refs[: RING - 1], refs[RING - 1]
    y = y_ref[0]
    rows = own_ref.shape[0]
    own_ref[...] = mine_ref[y] + other_ref[y]
    exps[...] = jnp.zeros_like(exps)
    for d in range(1, RING):
        q = lax.rem(y + d, RING)

        def group(g, carry):
            at = pl.ds(pl.multiple_of(g * ROWS, ROWS), ROWS)
            codes, exponent = encode(mine_ref[q, at, :] + other_ref[q, at, :])
            sends[d - 1][at, :] = codes
            exps[pl.ds(g, 1), :] = exponent
            return carry

        lax.fori_loop(0, rows // ROWS, group, 0, unroll=2)
        sends[d - 1][pl.ds(rows, exps.shape[0]), :] = exps[...].astype(i32).astype(i16)


def core_sum(y, mine, other):
    rows = mine.shape[1]
    tags = tag_rows(rows // ROWS)
    code = shape((rows + tags, LANES), i16)
    return pl.pallas_call(
        core_sum_kernel,
        out_shape=(shape((rows, LANES), f32), code, code, code),
        in_specs=[SMEM, VMEM, VMEM],
        out_specs=(VMEM,) * RING,
        scratch_shapes=[pltpu.VMEM((tags, LANES), f32)],
        compiler_params=params(),
    )(y, mine, other)


PART = SLOTS * ROWS + META


def ring_sum_kernel(group, place_ref, own_ref, a_ref, b_ref, c_ref, *refs):
    out_ref, scales, exps = refs[-3:]
    x, z = place_ref[0], place_ref[1]
    codes = (a_ref, b_ref, c_ref)
    rows, tags = own_ref.shape[0], scales.shape[1]
    for k in range(RING - 1):
        scales[k] = scale_of(codes[k][pl.ds(rows, tags), :].astype(i32).astype(f32))
    exps[...] = jnp.zeros_like(exps)
    for o, (e, d) in enumerate(group):
        to = lax.rem(x - e + RING, RING) * RING + lax.rem(z - d + RING, RING)
        for r in range(SLOTS):
            g = o * SLOTS + r
            at = pl.ds(g * ROWS, ROWS)
            total = own_ref[at, :]
            for k in range(RING - 1):
                total += codes[k][at, :].astype(i32).astype(f32) * scales[k, g : g + 1, :]
            code, exponent = encode(total)
            out_ref[to, r * ROWS : (r + 1) * ROWS, :] = code
            exps[r : r + 1, :] = exponent
        out_ref[to, SLOTS * ROWS : PART, :] = exps[...].astype(i32).astype(i16)


def ring_sum(which, place, own, codes, parts=None):
    more = [] if parts is None else [parts]
    return pl.pallas_call(
        functools.partial(ring_sum_kernel, GROUPS[which]),
        out_shape=shape((BLOCKS, PART, LANES), i16),
        in_specs=[SMEM] + [VMEM] * (RING + len(more)),
        out_specs=VMEM,
        input_output_aliases={RING + 1: 0} if more else {},
        scratch_shapes=[
            pltpu.VMEM((RING - 1, tag_rows(own.shape[0] // ROWS), LANES), f32),
            pltpu.VMEM((META, LANES), f32),
        ],
        compiler_params=params(),
    )(place, own, *codes, *more)


RANGES = 8
DEST = TILES * ROWS + META


def reorder_kernel(owner_ref, in_ref, out_ref, exps):
    for s in range(BLOCKS * SLOTS):
        owner, r = divmod(s, SLOTS)
        p = owner_ref[s]
        v, t = p // TILES, lax.rem(p, TILES)
        out_ref[v, pl.ds(pl.multiple_of(t * ROWS, ROWS), ROWS), :] = in_ref[owner, r * ROWS : (r + 1) * ROWS, :]
        tags = in_ref[owner, SLOTS * ROWS : PART, :].astype(i32).astype(f32)
        exps[pl.ds(v * META + t, 1), :] = tags[r : r + 1, :]
    for v in range(RANGES):
        out_ref[v, TILES * ROWS : DEST, :] = exps[v * META : (v + 1) * META, :].astype(i32).astype(i16)


def reorder(row_owner, parts):
    return pl.pallas_call(
        reorder_kernel,
        out_shape=shape((RANGES, DEST, LANES), i16),
        in_specs=[SMEM, VMEM],
        out_specs=VMEM,
        scratch_shapes=[pltpu.VMEM((RANGES * META, LANES), f32)],
        compiler_params=params(),
    )(row_owner, parts)


def finish_kernel(in_ref, out_ref):
    for v in range(RANGES):
        y, core = divmod(v, 2)
        scale = scale_of(in_ref[v, TILES * ROWS : DEST, :].astype(i32).astype(f32))
        for t in range(TILES):
            column = t * ENTRY + core * HALF + y * LANES
            value = in_ref[v, t * ROWS : (t + 1) * ROWS, :].astype(i32).astype(f32)
            out_ref[:, column : column + LANES] = value * scale[t : t + 1, :]


def finish(parts):
    return pl.pallas_call(
        finish_kernel,
        out_shape=shape((ROWS, TILES * ENTRY), f32),
        in_specs=[VMEM],
        out_specs=VMEM,
        compiler_params=params(),
    )(parts)


def shards(amplitudes, tile_live, integrals, block_live, row_owner):
    occ, vir = lax.axis_index("occ"), lax.axis_index("vir")
    x, z, y, core = occ // RING, occ % RING, vir // 2, vir % 2
    place = jnp.stack([x, z]).astype(i32)

    packed = pack(tile_live, amplitudes)
    row = jnp.concatenate([packed] + [shift_first(packed, b) for b in range(1, RING)], 0)
    amps = {0: row, 1: shift_second(row, 1), 3: shift_second(row, 3)}
    late, amps[3] = lax.optimization_barrier((row, amps[3]))
    amps[2] = shift_second(late, 2)

    which_core, which_y = core.reshape(1).astype(i32), y.reshape(1).astype(i32)

    theirs0, mine0, blocks = compute(
        0, which_core, block_live, integrals, None, {a: amps[a] for a in NEAR}
    )
    other0 = shift_core(theirs0)
    theirs1, mine1, _ = compute(1, which_core, block_live, integrals, blocks, amps)
    other1 = shift_core(theirs1)
    own0, *sends0 = core_sum(which_y, mine0, other0)
    codes0 = [shift_y(sends0[d - 1], d) for d in range(1, RING)]
    own1, *sends1 = core_sum(which_y, mine1, other1)
    codes1 = [shift_y(sends1[d - 1], d) for d in range(1, RING)]
    parts = ring_sum(0, place, own0, codes0)
    parts = ring_sum(1, place, own1, codes1, parts)
    parts = lax.all_to_all(parts, "occ", split_axis=0, concat_axis=0, tiled=True)
    parts = reorder(row_owner, parts)
    parts = lax.all_to_all(parts, "vir", split_axis=0, concat_axis=0, tiled=True)
    return finish(parts)


def solution(mesh):
    return jax.shard_map(
        shards,
        mesh=mesh,
        in_specs=(
            P("occ", "vir"),
            P("occ", "vir"),
            P("occ", "vir", None, None),
            P("occ", "vir"),
            P(),
        ),
        out_specs=P("occ", "vir"),
        check_vma=False,
    )
```

time: 120 us -> 90.5 us (0.75)
  local copies, waits for them, and re-layouts: 21.8 us -> 0.93 us
  waiting for transfers between devices: 21.7 us -> 16.5 us
  starting transfers between devices: 25 us -> 22.2 us
    unnamed x38 -> x6, local copies, waits for them, and re-layouts: 21.7 us -> 0.93 us
    ppermute x16 -> x14, waiting for transfers between devices: 21.7 us -> 16.5 us  [shift(): lax.ppermute(value, ('occ', 'vir'), [(index(*s), index(*place(*s))) for s...]
    ppermute x16 -> x14, starting transfers between devices: 25 us -> 22.2 us  [shift(): lax.ppermute(value, ('occ', 'vir'), [(index(*s), index(*place(*s))) for s...]
    pallas_call x5 -> x7, Pallas kernels: 21.9 us -> 20.7 us  [the longest x2 15 us: compute(): pl.pallas_call(functools.partial(compute_kernel, group, shifts, fetches),...]
  transfers between devices with their start and end apart: 16 -> 14, of which waited for: 7 -> 8; matrix products, arithmetic and copies ran while one was open for 0% -> 0% of each run, Pallas kernels for 7% -> 21%
where the time goes in v2:
time: 90.5 us
  blocking collectives  28.3 us (31%)
  Pallas kernels  22.3 us (25%)
  starting transfers between devices  22.2 us (25%)
  waiting for transfers between devices  16.5 us (18%)
  local copies, waits for them, and re-layouts  0.93 us (1%)
    ppermute x14, starting transfers between devices, shift(): lax.ppermute(value, ('occ', 'vir'), [(index(*s), index(*place(*s))) for s...  22.2 us
    ppermute x14, waiting for transfers between devices, shift(): lax.ppermute(value, ('occ', 'vir'), [(index(*s), index(*place(*s))) for s...  16.5 us
    pallas_call x2, Pallas kernels, compute(): pl.pallas_call(functools.partial(compute_kernel, group, shifts, fetches),...  15 us
    all_to_all x1, blocking collectives, shards(): lax.all_to_all(parts, 'occ', split_axis=0, concat_axis=0, tiled=True)  14.5 us
    all_to_all x1, blocking collectives, shards(): lax.all_to_all(parts, 'vir', split_axis=0, concat_axis=0, tiled=True)  13.8 us
    pallas_call x2, Pallas kernels, core_sum(): pl.pallas_call(core_sum_kernel, out_shape=(shape((rows, LANES), f32), cod...  3.16 us
  transfers between devices with their start and end apart: 14, of which 8 were waited for; matrix products, arithmetic and copies ran while one was open for 0% of the time, Pallas kernels for 21%

profile of v2, /device:TPU:1, one launch (start us, length us, event | category | flops | bytes accessed | tf_op | source)
XLA Modules:
  0.0 90.5 jit_solution(7273878720637955371)
XLA Ops:
  0.0 1.0 %shard_map.55 = bf16[528,128]{1,0:T(8,128)(2,1)S(1)} custom-call(s32[1,4]{1,0:T(1,128)} %live_hbm.3, bf16[32,4096]{1,0:T(8,128)(2,1)} %amp_hbm.1), custom_call_target="tpu_custom_call" | custom-call | tf_op jit(solution)/shard_map/pallas_call | solution.py:75
  1.0 2.1 %collective-permute-start = (bf16[528,128]{1,0:T(8,128)(2,1)S(1)}, bf16[528,128]{1,0:T(8,128)(2,1)S(1)}, u32[]{:S(2)}, u32[]{:S(2)}) collective-permute-start(bf16[528,128]{1,0:T(8,128)(2,1)S(1)} %shard_map.55), channel_id=1, source_target_pairs={{0,8},{1,33},{2,10},{3,35},{4,12},{5,37},{6,14},{7,39},{8,16},{9,4... | collective-permute-start | bytes 405512 | tf_op jit(solution)/shard_map/ppermute | solution.py:94
  3.1 2.5 %collective-permute-start.1 = (bf16[528,128]{1,0:T(8,128)(2,1)S(1)}, bf16[528,128]{1,0:T(8,128)(2,1)S(1)}, u32[]{:S(2)}, u32[]{:S(2)}) collective-permute-start(bf16[528,128]{1,0:T(8,128)(2,1)S(1)} %shard_map.55), channel_id=1, source_target_pairs={{0,16},{1,65},{2,18},{3,67},{4,20},{5,69},{6,22},{7,71},{8,24},{9,... | collective-permute-start | bytes 405512 | tf_op jit(solution)/shard_map/ppermute | solution.py:94
  5.6 1.2 %collective-permute-start.2 = (bf16[528,128]{1,0:T(8,128)(2,1)S(1)}, bf16[528,128]{1,0:T(8,128)(2,1)S(1)}, u32[]{:S(2)}, u32[]{:S(2)}) collective-permute-start(bf16[528,128]{1,0:T(8,128)(2,1)S(1)} %shard_map.55), channel_id=1, source_target_pairs={{0,24},{1,97},{2,26},{3,99},{4,28},{5,101},{6,30},{7,103},{8,0},{9... | collective-permute-start | bytes 405512 | tf_op jit(solution)/shard_map/ppermute | solution.py:94
  6.7 0.1 collective-permute-done
  6.8 2.6 %collective-permute-done.1 = bf16[528,128]{1,0:T(8,128)(2,1)S(1)} collective-permute-done((bf16[528,128]{1,0:T(8,128)(2,1)S(1)}, bf16[528,128]{1,0:T(8,128)(2,1)S(1)}, u32[]{:S(2)}, u32[]{:S(2)}) %collective-permute-start.1) | collective-permute-done | bytes 135200 | tf_op jit(solution)/shard_map/ppermute | solution.py:94
  9.4 0.0 collective-permute-done.2
  9.5 4.1 %collective-permute-start.4 = (bf16[2112,128]{1,0:T(8,128)(2,1)S(1)}, bf16[2112,128]{1,0:T(8,128)(2,1)S(1)}, u32[]{:S(2)}, u32[]{:S(2)}) collective-permute-start(bf16[2112,128]{1,0:T(8,128)(2,1)S(1)} %pad_maximum_fusion.refs_0_), channel_id=1, source_target_pairs={{0,96},{1,25},{2,98},{3,27},{4,100},{5,29},{6,102},{7,31},{8,104},... | collective-permute-start | bytes 1622024 | tf_op jit(solution)/shard_map/ppermute | solution.py:94
  13.6 0.0 collective-permute-start.3
  13.6 6.3 %collective-permute-done.4.refs_2_.refs_3_ = bf16[2112,128]{1,0:T(8,128)(2,1)S(1)} collective-permute-done((bf16[2112,128]{1,0:T(8,128)(2,1)S(1)}, bf16[2112,128]{1,0:T(8,128)(2,1)S(1)}, u32[]{:S(2)}, u32[]{:S(2)}) %collective-permute-start.4) | collective-permute-done | bytes 540704 | tf_op jit(solution)/shard_map/ppermute | solution.py:94
  19.9 2.0 %collective-permute-start.5 = (bf16[2112,128]{1,0:T(8,128)(2,1)S(1)}, bf16[2112,128]{1,0:T(8,128)(2,1)S(1)}, u32[]{:S(2)}, u32[]{:S(2)}) collective-permute-start(bf16[2112,128]{1,0:T(8,128)(2,1)S(1)} %pad_maximum_fusion.refs_0_), channel_id=1, source_target_pairs={{0,64},{1,17},{2,66},{3,19},{4,68},{5,21},{6,70},{7,23},{8,72},{9,... | collective-permute-start | bytes 1622024 | tf_op jit(solution)/shard_map/ppermute | solution.py:94
  21.9 1.4 %collective-permute-done.3.refs_1_ = bf16[2112,128]{1,0:T(8,128)(2,1)S(1)} collective-permute-done((bf16[2112,128]{1,0:T(8,128)(2,1)S(1)}, bf16[2112,128]{1,0:T(8,128)(2,1)S(1)}, u32[]{:S(2)}, u32[]{:S(2)}) %collective-permute-start.3) | collective-permute-done | bytes 540704 | tf_op jit(solution)/shard_map/ppermute | solution.py:94
  23.3 8.2 %shard_map.56 = (f32[4,576,128]{2,1,0:T(8,128)}, f32[4,576,128]{2,1,0:T(8,128)S(1)}, bf16[8,1024,1024]{2,1,0:T(8,128)(2,1)S(1)}) custom-call(s32[1]{0:T(128)} %bitcast.3.core_ref.block_in, s32[2,4]{1,0:T(2,128)} %live_hbm.5, bf16[2,4,1024,1024]{3,2,1,0:T(8,128)(2,1)} %ints_hbm.3, s32[1]{0:T(128)} %bitcast.3.core_ref.block_in, ...), custom_call_target="tpu_custom_call" | custom-call | flops 4294967296 | bytes 8388608 | tf_op jit(solution)/shard_map/pallas_call | solution.py:218
  31.5 2.6 %collective-permute-start.10 = (f32[4,576,128]{2,1,0:T(8,128)}, f32[4,576,128]{2,1,0:T(8,128)}, u32[]{:S(2)}, u32[]{:S(2)}) collective-permute-start(f32[4,576,128]{2,1,0:T(8,128)} %get-tuple-element.30), channel_id=1, source_target_pairs={{0,1},{1,0},{2,3},{3,2},{4,5},{5,4},{6,7},{7,6},{8,9},{9,8},{10,11... | collective-permute-start | bytes 3538952 | tf_op jit(solution)/shard_map/ppermute | solution.py:94
  34.2 0.0 collective-permute-done.5.refs_2_
  34.2 6.8 %shard_map.57 = (f32[4,448,128]{2,1,0:T(8,128)}, f32[4,448,128]{2,1,0:T(8,128)S(1)}, bf16[8,1024,1024]{2,1,0:T(8,128)(2,1)S(1)}) custom-call(s32[1]{0:T(128)} %bitcast.3.core_ref.block_in, s32[2,4]{1,0:T(2,128)} %live_hbm.5, bf16[2,4,1024,1024]{3,2,1,0:T(8,128)(2,1)} %ints_hbm.3, ...), custom_call_target="tpu_custom_call", output_to_operand_aliasing={{2}: (3, {})} | custom-call | flops 4294967296 | bytes 8388608 | tf_op jit(solution)/shard_map/pallas_call | solution.py:218
  40.9 0.0 copy-start
  41.0 0.9 %copy-done = f32[4,448,128]{2,1,0:T(8,128)} copy-done((f32[4,448,128]{2,1,0:T(8,128)}, f32[4,448,128]{2,1,0:T(8,128)S(1)}, u32[]{:S(2)}) %copy-start) | copy-done | bytes 917528
  41.9 0.0 collective-permute-start.6
  41.9 0.0 collective-permute-done.10.other_ref
  41.9 0.0 copy-start.1
  41.9 2.4 %shard_map.59 = (f32[576,128]{1,0:T(8,128)S(1)}, s16[608,128]{1,0:T(8,128)(2,1)S(1)}, s16[608,128]{1,0:T(8,128)(2,1)S(1)}, s16[608,128]{1,0:T(8,128)(2,1)S(1)}) custom-call(s32[1]{0:T(128)} %bitcast.2.y_ref, f32[4,576,128]{2,1,0:T(8,128)S(1)} %get-tuple-element.29.mine_ref, f32[4,576,128]{2,1,0:T(8,128)} %collective-permute-done.10.other_ref), custom_call_target="tpu_custom_call" | custom-call | tf_op jit(solution)/shard_map/pallas_call | solution.py:279
  44.3 0.7 collective-permute-start.11
  44.9 2.5 %collective-permute-start.12 = (s16[608,128]{1,0:T(8,128)(2,1)S(1)}, s16[608,128]{1,0:T(8,128)(2,1)S(1)}, u32[]{:S(2)}, u32[]{:S(2)}) collective-permute-start(s16[608,128]{1,0:T(8,128)(2,1)S(1)} %get-tuple-element.33), channel_id=1, source_target_pairs={{0,4},{1,5},{2,6},{3,7},{4,0},{5,1},{6,2},{7,3},{8,12},{9,13},{10,... | collective-permute-start | bytes 466952 | tf_op jit(solution)/shard_map/ppermute | solution.py:94
  47.5 1.8 %collective-permute-start.13 = (s16[608,128]{1,0:T(8,128)(2,1)S(1)}, s16[608,128]{1,0:T(8,128)(2,1)S(1)}, u32[]{:S(2)}, u32[]{:S(2)}) collective-permute-start(s16[608,128]{1,0:T(8,128)(2,1)S(1)} %get-tuple-element.34), channel_id=1, source_target_pairs={{0,6},{1,7},{2,0},{3,1},{4,2},{5,3},{6,4},{7,5},{8,14},{9,15},{10,... | collective-permute-start | bytes 466952 | tf_op jit(solution)/shard_map/ppermute | solution.py:94
  49.2 0.0 collective-permute-done.6.other_ref
  49.2 0.0 copy-done.1
  49.3 0.8 shard_map.58
  50.0 0.1 collective-permute-start.7
  50.1 1.2 %collective-permute-start.8 = (s16[464,128]{1,0:T(8,128)(2,1)S(1)}, s16[464,128]{1,0:T(8,128)(2,1)S(1)}, u32[]{:S(2)}, u32[]{:S(2)}) collective-permute-start(s16[464,128]{1,0:T(8,128)(2,1)S(1)} %get-tuple-element.27), channel_id=1, source_target_pairs={{0,4},{1,5},{2,6},{3,7},{4,0},{5,1},{6,2},{7,3},{8,12},{9,13},{10,... | collective-permute-start | bytes 356360 | tf_op jit(solution)/shard_map/ppermute | solution.py:94
  51.3 0.0 collective-permute-done.11.a_ref
  51.3 1.5 %collective-permute-start.9 = (s16[464,128]{1,0:T(8,128)(2,1)S(1)}, s16[464,128]{1,0:T(8,128)(2,1)S(1)}, u32[]{:S(2)}, u32[]{:S(2)}) collective-permute-start(s16[464,128]{1,0:T(8,128)(2,1)S(1)} %get-tuple-element.28), channel_id=1, source_target_pairs={{0,6},{1,7},{2,0},{3,1},{4,2},{5,3},{6,4},{7,5},{8,14},{9,15},{10,... | collective-permute-start | bytes 356360 | tf_op jit(solution)/shard_map/ppermute | solution.py:94
  52.8 0.1 pad_add_fusion.place_ref
  52.9 1.6 %collective-permute-done.12.b_ref = s16[608,128]{1,0:T(8,128)(2,1)S(1)} collective-permute-done((s16[608,128]{1,0:T(8,128)(2,1)S(1)}, s16[608,128]{1,0:T(8,128)(2,1)S(1)}, u32[]{:S(2)}, u32[]{:S(2)}) %collective-permute-start.12) | collective-permute-done | bytes 155680 | tf_op jit(solution)/shard_map/ppermute | solution.py:94
  54.5 0.0 collective-permute-done.13.c_ref
  54.5 0.8 shard_map.60.refs_0_
  55.3 0.0 copy-start.2
  55.3 2.5 %collective-permute-done.7.a_ref = s16[464,128]{1,0:T(8,128)(2,1)S(1)} collective-permute-done((s16[464,128]{1,0:T(8,128)(2,1)S(1)}, s16[464,128]{1,0:T(8,128)(2,1)S(1)}, u32[]{:S(2)}, u32[]{:S(2)}) %collective-permute-start.7) | collective-permute-done | bytes 118816 | tf_op jit(solution)/shard_map/ppermute | solution.py:94
  57.9 1.7 %collective-permute-done.8.b_ref = s16[464,128]{1,0:T(8,128)(2,1)S(1)} collective-permute-done((s16[464,128]{1,0:T(8,128)(2,1)S(1)}, s16[464,128]{1,0:T(8,128)(2,1)S(1)}, u32[]{:S(2)}, u32[]{:S(2)}) %collective-permute-start.8) | collective-permute-done | bytes 118816 | tf_op jit(solution)/shard_map/ppermute | solution.py:94
  59.6 0.2 collective-permute-done.9.c_ref
  59.8 0.7 shard_map.61
  60.5 14.5 %all_to_all.10.in_ref = s16[16,80,128]{2,1,0:T(8,128)(2,1)S(1)} all-to-all(s16[16,80,128]{2,1,0:T(8,128)(2,1)S(1)} %shard_map.61), channel_id=1, replica_groups=mesh['occ'=16,'vir'=8] {'occ'}, dimensions={0} | all-to-all | bytes 655360 | tf_op jit(solution)/shard_map/all_to_all | solution.py:402
  75.0 0.0 copy-done.2
  75.0 0.8 shard_map.62
  75.8 13.8 %all_to_all.11.in_ref = s16[8,144,128]{2,1,0:T(8,128)(2,1)S(1)} all-to-all(s16[8,144,128]{2,1,0:T(8,128)(2,1)S(1)} %shard_map.62), channel_id=1, replica_groups=mesh['occ'=16,'vir'=8] {'vir'}, dimensions={0} | all-to-all | bytes 589824 | tf_op jit(solution)/shard_map/all_to_all | solution.py:404
  89.6 0.9 shard_map.63
  (1 shorter events, 0.0 us)
Async XLA Ops:
  1.0 5.8 %collective-permute-start = (bf16[528,128]{1,0:T(8,128)(2,1)S(1)}, bf16[528,128]{1,0:T(8,128)(2,1)S(1)}, u32[]{:S(2)}, u32[]{:S(2)}) collective-permute-start(bf16[528,128]{1,0:T(8,128)(2,1)S(1)} %shard_map.55), channel_id=1, source_target_pairs={{0,8},{1,33},{2,10},{3,35},{4,12},{5,37},{6,14},{7,39},{8,16},{9,4... | collective-permute-start | bytes 405512 | tf_op jit(solution)/shard_map/ppermute | solution.py:94
  3.1 6.3 %collective-permute-start.1 = (bf16[528,128]{1,0:T(8,128)(2,1)S(1)}, bf16[528,128]{1,0:T(8,128)(2,1)S(1)}, u32[]{:S(2)}, u32[]{:S(2)}) collective-permute-start(bf16[528,128]{1,0:T(8,128)(2,1)S(1)} %shard_map.55), channel_id=1, source_target_pairs={{0,16},{1,65},{2,18},{3,67},{4,20},{5,69},{6,22},{7,71},{8,24},{9,... | collective-permute-start | bytes 405512 | tf_op jit(solution)/shard_map/ppermute | solution.py:94
  5.6 3.9 %collective-permute-start.2 = (bf16[528,128]{1,0:T(8,128)(2,1)S(1)}, bf16[528,128]{1,0:T(8,128)(2,1)S(1)}, u32[]{:S(2)}, u32[]{:S(2)}) collective-permute-start(bf16[528,128]{1,0:T(8,128)(2,1)S(1)} %shard_map.55), channel_id=1, source_target_pairs={{0,24},{1,97},{2,26},{3,99},{4,28},{5,101},{6,30},{7,103},{8,0},{9... | collective-permute-start | bytes 405512 | tf_op jit(solution)/shard_map/ppermute | solution.py:94
  9.5 10.4 %collective-permute-start.4 = (bf16[2112,128]{1,0:T(8,128)(2,1)S(1)}, bf16[2112,128]{1,0:T(8,128)(2,1)S(1)}, u32[]{:S(2)}, u32[]{:S(2)}) collective-permute-start(bf16[2112,128]{1,0:T(8,128)(2,1)S(1)} %pad_maximum_fusion.refs_0_), channel_id=1, source_target_pairs={{0,96},{1,25},{2,98},{3,27},{4,100},{5,29},{6,102},{7,31},{8,104},... | collective-permute-start | bytes 1622024 | tf_op jit(solution)/shard_map/ppermute | solution.py:94
  13.6 9.7 %collective-permute-start.3 = (bf16[2112,128]{1,0:T(8,128)(2,1)S(1)}, bf16[2112,128]{1,0:T(8,128)(2,1)S(1)}, u32[]{:S(2)}, u32[]{:S(2)}) collective-permute-start(bf16[2112,128]{1,0:T(8,128)(2,1)S(1)} %pad_maximum_fusion.refs_0_), channel_id=1, source_target_pairs={{0,32},{1,9},{2,34},{3,11},{4,36},{5,13},{6,38},{7,15},{8,40},{9,1... | collective-permute-start | bytes 1622024 | tf_op jit(solution)/shard_map/ppermute | solution.py:94
  19.9 14.3 %collective-permute-start.5 = (bf16[2112,128]{1,0:T(8,128)(2,1)S(1)}, bf16[2112,128]{1,0:T(8,128)(2,1)S(1)}, u32[]{:S(2)}, u32[]{:S(2)}) collective-permute-start(bf16[2112,128]{1,0:T(8,128)(2,1)S(1)} %pad_maximum_fusion.refs_0_), channel_id=1, source_target_pairs={{0,64},{1,17},{2,66},{3,19},{4,68},{5,21},{6,70},{7,23},{8,72},{9,... | collective-permute-start | bytes 1622024 | tf_op jit(solution)/shard_map/ppermute | solution.py:94
  31.5 10.3 %collective-permute-start.10 = (f32[4,576,128]{2,1,0:T(8,128)}, f32[4,576,128]{2,1,0:T(8,128)}, u32[]{:S(2)}, u32[]{:S(2)}) collective-permute-start(f32[4,576,128]{2,1,0:T(8,128)} %get-tuple-element.30), channel_id=1, source_target_pairs={{0,1},{1,0},{2,3},{3,2},{4,5},{5,4},{6,7},{7,6},{8,9},{9,8},{10,11... | collective-permute-start | bytes 3538952 | tf_op jit(solution)/shard_map/ppermute | solution.py:94
  40.9 0.9 %copy-start = (f32[4,448,128]{2,1,0:T(8,128)}, f32[4,448,128]{2,1,0:T(8,128)S(1)}, u32[]{:S(2)}) copy-start(f32[4,448,128]{2,1,0:T(8,128)S(1)} %get-tuple-element.23.mine_ref) | copy-start | bytes 2752516
  41.9 7.4 %collective-permute-start.6 = (f32[4,448,128]{2,1,0:T(8,128)}, f32[4,448,128]{2,1,0:T(8,128)S(1)}, u32[]{:S(2)}, u32[]{:S(2)}) collective-permute-start(f32[4,448,128]{2,1,0:T(8,128)} %get-tuple-element.24), channel_id=1, source_target_pairs={{0,1},{1,0},{2,3},{3,2},{4,5},{5,4},{6,7},{7,6},{8,9},{9,8},{10,11... | collective-permute-start | bytes 2752520 | tf_op jit(solution)/shard_map/ppermute | solution.py:94
  41.9 7.4 %copy-start.1 = (f32[4,448,128]{2,1,0:T(8,128)S(1)}, f32[4,448,128]{2,1,0:T(8,128)}, u32[]{:S(2)}) copy-start(f32[4,448,128]{2,1,0:T(8,128)} %copy-done) | copy-start | bytes 2752516
  44.3 7.1 %collective-permute-start.11 = (s16[608,128]{1,0:T(8,128)(2,1)S(1)}, s16[608,128]{1,0:T(8,128)(2,1)S(1)}, u32[]{:S(2)}, u32[]{:S(2)}) collective-permute-start(s16[608,128]{1,0:T(8,128)(2,1)S(1)} %get-tuple-element.32), channel_id=1, source_target_pairs={{0,2},{1,3},{2,4},{3,5},{4,6},{5,7},{6,0},{7,1},{8,10},{9,11},{10,... | collective-permute-start | bytes 466952 | tf_op jit(solution)/shard_map/ppermute | solution.py:94
  44.9 9.6 %collective-permute-start.12 = (s16[608,128]{1,0:T(8,128)(2,1)S(1)}, s16[608,128]{1,0:T(8,128)(2,1)S(1)}, u32[]{:S(2)}, u32[]{:S(2)}) collective-permute-start(s16[608,128]{1,0:T(8,128)(2,1)S(1)} %get-tuple-element.33), channel_id=1, source_target_pairs={{0,4},{1,5},{2,6},{3,7},{4,0},{5,1},{6,2},{7,3},{8,12},{9,13},{10,... | collective-permute-start | bytes 466952 | tf_op jit(solution)/shard_map/ppermute | solution.py:94
  47.5 7.1 %collective-permute-start.13 = (s16[608,128]{1,0:T(8,128)(2,1)S(1)}, s16[608,128]{1,0:T(8,128)(2,1)S(1)}, u32[]{:S(2)}, u32[]{:S(2)}) collective-permute-start(s16[608,128]{1,0:T(8,128)(2,1)S(1)} %get-tuple-element.34), channel_id=1, source_target_pairs={{0,6},{1,7},{2,0},{3,1},{4,2},{5,3},{6,4},{7,5},{8,14},{9,15},{10,... | collective-permute-start | bytes 466952 | tf_op jit(solution)/shard_map/ppermute | solution.py:94
  50.0 7.8 %collective-permute-start.7 = (s16[464,128]{1,0:T(8,128)(2,1)S(1)}, s16[464,128]{1,0:T(8,128)(2,1)S(1)}, u32[]{:S(2)}, u32[]{:S(2)}) collective-permute-start(s16[464,128]{1,0:T(8,128)(2,1)S(1)} %get-tuple-element.26), channel_id=1, source_target_pairs={{0,2},{1,3},{2,4},{3,5},{4,6},{5,7},{6,0},{7,1},{8,10},{9,11},{10,... | collective-permute-start | bytes 356360 | tf_op jit(solution)/shard_map/ppermute | solution.py:94
  50.1 9.5 %collective-permute-start.8 = (s16[464,128]{1,0:T(8,128)(2,1)S(1)}, s16[464,128]{1,0:T(8,128)(2,1)S(1)}, u32[]{:S(2)}, u32[]{:S(2)}) collective-permute-start(s16[464,128]{1,0:T(8,128)(2,1)S(1)} %get-tuple-element.27), channel_id=1, source_target_pairs={{0,4},{1,5},{2,6},{3,7},{4,0},{5,1},{6,2},{7,3},{8,12},{9,13},{10,... | collective-permute-start | bytes 356360 | tf_op jit(solution)/shard_map/ppermute | solution.py:94
  51.3 8.5 %collective-permute-start.9 = (s16[464,128]{1,0:T(8,128)(2,1)S(1)}, s16[464,128]{1,0:T(8,128)(2,1)S(1)}, u32[]{:S(2)}, u32[]{:S(2)}) collective-permute-start(s16[464,128]{1,0:T(8,128)(2,1)S(1)} %get-tuple-element.28), channel_id=1, source_target_pairs={{0,6},{1,7},{2,0},{3,1},{4,2},{5,3},{6,4},{7,5},{8,14},{9,15},{10,... | collective-permute-start | bytes 356360 | tf_op jit(solution)/shard_map/ppermute | solution.py:94
  55.3 19.7 %copy-start.2 = (s32[32]{0:T(128)S(1)}, s32[32]{0:T(128)}, u32[]{:S(2)}) copy-start(s32[32]{0:T(128)} %owner_ref.1) | copy-start | bytes 388

commit v3 on v2

--- a/solution.py
+++ b/solution.py
@@ -34,6 +34,11 @@
 
 def shape(dims, dtype):
     return jax.ShapeDtypeStruct(dims, dtype)
+
+
+def position():
+    occ, vir = lax.axis_index("occ"), lax.axis_index("vir")
+    return occ // RING, lax.rem(occ, RING), vir // 2, lax.rem(vir, 2)
 
 
 def in_hbm(*arrays):
@@ -110,6 +115,40 @@
     return shift(value, lambda x, z, y, c: (x, z, y, c + 1))
 
 
+def fetch_kernel(live_hbm, ints_hbm, after_ref, block_ref, live, sem, sems):
+    del after_ref
+    copy = pltpu.make_async_copy(live_hbm, live, sem)
+    copy.start()
+    copy.wait()
+
+    def fetch(r, c):
+        i = c * SLOTS + r
+        return pltpu.make_async_copy(ints_hbm.at[r, c], block_ref.at[i], sems.at[i])
+
+    for c in range(TILES):
+        for r in range(SLOTS):
+            pl.when(live[r, c] != 0)(lambda: fetch(r, c).start())
+    for c in range(TILES):
+        for r in range(SLOTS):
+            pl.when(live[r, c] != 0)(lambda: fetch(r, c).wait())
+
+
+def fetch_blocks(block_live, integrals, after):
+    return pl.pallas_call(
+        fetch_kernel,
+        out_shape=pltpu.VMEM((TILES * SLOTS, ENTRY, ENTRY), bf16),
+        in_specs=[HBM, HBM, ANY],
+        out_specs=VMEM,
+        scratch_shapes=[
+            pltpu.SMEM(block_live.shape, i32),
+            pltpu.SemaphoreType.DMA,
+            pltpu.SemaphoreType.DMA((TILES * SLOTS,)),
+        ],
+        compiler_params=params(2),
+        cost_estimate=pl.CostEstimate(flops=0, bytes_accessed=32 << 20, transcendentals=0),
+    )(*in_hbm(block_live, integrals), after)
+
+
 NEAR = (0, 1, 3)
 GROUPS = (
     [(e, d) for e in NEAR for d in NEAR],
@@ -117,12 +156,10 @@
 )
 
 
-def compute_kernel(group, shifts, fetches, core_ref, live_hbm, ints_hbm, block_in, *refs):
+def compute_kernel(group, shifts, live_hbm, block_ref, *refs):
     amps = dict(zip(shifts, refs[: len(shifts)]))
-    refs = refs[len(shifts) :]
-    theirs_ref, mine_ref, block_ref, left, product, table_v, table, live, count, where, sem, sems = refs
-    del block_in
-    core = core_ref[0]
+    theirs_ref, mine_ref, left, product, table_v, table, live, count, where, sem = refs[len(shifts) :]
+    core = position()[3]
     copy_live = pltpu.make_async_copy(live_hbm, live, sem.at[0])
     copy_live.start()
 
@@ -135,17 +172,11 @@
     copy_table = pltpu.make_async_copy(table_v, table, sem.at[1])
     copy_table.start()
 
-    def fetch(i):
-        return pltpu.make_async_copy(ints_hbm.at[lax.rem(i, SLOTS), i // SLOTS], block_ref.at[i], sems.at[i])
-
-    copy_live.wait()
-    if fetches:
-        for i in range(TILES * SLOTS):
-            pl.when(live[i % SLOTS, i // SLOTS] != 0)(functools.partial(lambda i: fetch(i).start(), i))
     theirs_ref[...] = jnp.zeros_like(theirs_ref)
     mine_ref[...] = jnp.zeros_like(mine_ref)
     for c in range(TILES):
         count[c] = 0
+    copy_live.wait()
     copy_table.wait()
 
     for k, (a, b) in enumerate(group):
@@ -170,8 +201,6 @@
 
         @pl.when(live[r, c] != 0)
         def _():
-            if fetches:
-                fetch(i).wait()
             n = count[c]
 
             def one_chunk(j, inner):
@@ -209,18 +238,15 @@
     lax.fori_loop(0, TILES * SLOTS, one_block, 0)
 
 
-def compute(which, core, block_live, integrals, blocks, amps):
+def compute(which, block_live, blocks, amps):
     group = GROUPS[which]
     shifts = sorted(amps)
-    fetches = blocks is None
     total = pltpu.VMEM((RING, len(group) * SLOTS * ROWS, LANES), f32)
-    held = (TILES * SLOTS, ENTRY, ENTRY)
-    return pl.pallas_call(
-        functools.partial(compute_kernel, group, shifts, fetches),
-        out_shape=(total, total, pltpu.VMEM(held, bf16)),
-        in_specs=[SMEM, HBM, HBM] + [SMEM if fetches else VMEM] + [VMEM] * len(shifts),
-        out_specs=(VMEM,) * 3,
-        input_output_aliases={} if fetches else {3: 2},
+    return pl.pallas_call(
+        functools.partial(compute_kernel, group, shifts),
+        out_shape=(total, total),
+        in_specs=[HBM] + [VMEM] * (1 + len(shifts)),
+        out_specs=(VMEM,) * 2,
         scratch_shapes=[
             pltpu.VMEM((TILES, 2 * CHUNK, ENTRY), bf16),
             pltpu.VMEM((CHUNK, ENTRY), f32),
@@ -230,11 +256,10 @@
             pltpu.SMEM((TILES,), i32),
             pltpu.SMEM((TILES * BLOCKS,), i32),
             pltpu.SemaphoreType.DMA((2,)),
-            pltpu.SemaphoreType.DMA((TILES * SLOTS,)),
         ],
         compiler_params=params(8),
         cost_estimate=pl.CostEstimate(flops=1 << 32, bytes_accessed=8 << 20, transcendentals=0),
-    )(core, *in_hbm(block_live, integrals), *([core] if fetches else in_vmem(blocks)), *[amps[a] for a in shifts])
+    )(*in_hbm(block_live), *in_vmem(blocks), *[amps[a] for a in shifts])
 
 
 def encode(value):
@@ -252,9 +277,9 @@
     return pl.cdiv(sums, META) * META
 
 
-def core_sum_kernel(y_ref, mine_ref, other_ref, own_ref, *refs):
+def core_sum_kernel(mine_ref, other_ref, own_ref, *refs):
     sends, exps = refs[: RING - 1], refs[RING - 1]
-    y = y_ref[0]
+    y = position()[2]
     rows = own_ref.shape[0]
     own_ref[...] = mine_ref[y] + other_ref[y]
     exps[...] = jnp.zeros_like(exps)
@@ -272,26 +297,26 @@
         sends[d - 1][pl.ds(rows, exps.shape[0]), :] = exps[...].astype(i32).astype(i16)
 
 
-def core_sum(y, mine, other):
+def core_sum(mine, other):
     rows = mine.shape[1]
     tags = tag_rows(rows // ROWS)
     code = shape((rows + tags, LANES), i16)
     return pl.pallas_call(
         core_sum_kernel,
         out_shape=(shape((rows, LANES), f32), code, code, code),
-        in_specs=[SMEM, VMEM, VMEM],
+        in_specs=[VMEM, VMEM],
         out_specs=(VMEM,) * RING,
         scratch_shapes=[pltpu.VMEM((tags, LANES), f32)],
         compiler_params=params(),
-    )(y, mine, other)
+    )(mine, other)
 
 
 PART = SLOTS * ROWS + META
 
 
-def ring_sum_kernel(group, place_ref, own_ref, a_ref, b_ref, c_ref, *refs):
+def ring_sum_kernel(group, own_ref, a_ref, b_ref, c_ref, *refs):
     out_ref, scales, exps = refs[-3:]
-    x, z = place_ref[0], place_ref[1]
+    x, z = position()[:2]
     codes = (a_ref, b_ref, c_ref)
     rows, tags = own_ref.shape[0], scales.shape[1]
     for k in range(RING - 1):
@@ -311,20 +336,20 @@
         out_ref[to, SLOTS * ROWS : PART, :] = exps[...].astype(i32).astype(i16)
 
 
-def ring_sum(which, place, own, codes, parts=None):
+def ring_sum(which, own, codes, parts=None):
     more = [] if parts is None else [parts]
     return pl.pallas_call(
         functools.partial(ring_sum_kernel, GROUPS[which]),
         out_shape=shape((BLOCKS, PART, LANES), i16),
-        in_specs=[SMEM] + [VMEM] * (RING + len(more)),
+        in_specs=[VMEM] * (RING + len(more)),
         out_specs=VMEM,
-        input_output_aliases={RING + 1: 0} if more else {},
+        input_output_aliases={RING: 0} if more else {},
         scratch_shapes=[
             pltpu.VMEM((RING - 1, tag_rows(own.shape[0] // ROWS), LANES), f32),
             pltpu.VMEM((META, LANES), f32),
         ],
         compiler_params=params(),
-    )(place, own, *codes, *more)
+    )(own, *codes, *more)
 
 
 RANGES = 8
@@ -375,30 +400,23 @@
 
 
 def shards(amplitudes, tile_live, integrals, block_live, row_owner):
-    occ, vir = lax.axis_index("occ"), lax.axis_index("vir")
-    x, z, y, core = occ // RING, occ % RING, vir // 2, vir % 2
-    place = jnp.stack([x, z]).astype(i32)
-
     packed = pack(tile_live, amplitudes)
     row = jnp.concatenate([packed] + [shift_first(packed, b) for b in range(1, RING)], 0)
     amps = {0: row, 1: shift_second(row, 1), 3: shift_second(row, 3)}
-    late, amps[3] = lax.optimization_barrier((row, amps[3]))
+    blocks = fetch_blocks(block_live, integrals, row)
+    late, amps[3], blocks = lax.optimization_barrier((row, amps[3], blocks))
     amps[2] = shift_second(late, 2)
 
-    which_core, which_y = core.reshape(1).astype(i32), y.reshape(1).astype(i32)
-
-    theirs0, mine0, blocks = compute(
-        0, which_core, block_live, integrals, None, {a: amps[a] for a in NEAR}
-    )
+    theirs0, mine0 = compute(0, block_live, blocks, {a: amps[a] for a in NEAR})
     other0 = shift_core(theirs0)
-    theirs1, mine1, _ = compute(1, which_core, block_live, integrals, blocks, amps)
+    theirs1, mine1 = compute(1, block_live, blocks, amps)
     other1 = shift_core(theirs1)
-    own0, *sends0 = core_sum(which_y, mine0, other0)
+    own0, *sends0 = core_sum(mine0, other0)
     codes0 = [shift_y(sends0[d - 1], d) for d in range(1, RING)]
-    own1, *sends1 = core_sum(which_y, mine1, other1)
+    own1, *sends1 = core_sum(mine1, other1)
     codes1 = [shift_y(sends1[d - 1], d) for d in range(1, RING)]
-    parts = ring_sum(0, place, own0, codes0)
-    parts = ring_sum(1, place, own1, codes1, parts)
+    parts = ring_sum(0, own0, codes0)
+    parts = ring_sum(1, own1, codes1, parts)
     parts = lax.all_to_all(parts, "occ", split_axis=0, concat_axis=0, tiled=True)
     parts = reorder(row_owner, parts)
     parts = lax.all_to_all(parts, "vir", split_axis=0, concat_axis=0, tiled=True)

time: 90.5 us -> 86 us (0.950)
  Pallas kernels: 22.3 us -> 16.5 us
  starting transfers between devices: 22.2 us -> 25.1 us
  blocking collectives: 28.3 us -> 26.7 us
  local copies, waits for them, and re-layouts: 0.93 us -> 0.01 us
    pallas_call x2 -> x3, Pallas kernels: 15 us -> 11.6 us  [the longest x2 7.4 us: compute(): pl.pallas_call(functools.partial(compute_kernel, group, shifts), out_shap...]
    ppermute x14, starting transfers between devices: 22.2 us -> 25.1 us  [shift(): lax.ppermute(value, ('occ', 'vir'), [(index(*s), index(*place(*s))) for s...]
    all_to_all x1, blocking collectives: 14.5 us -> 12.9 us  [shards(): lax.all_to_all(parts, 'occ', split_axis=0, concat_axis=0, tiled=True)]
    pallas_call x2, Pallas kernels: 3.16 us -> 1.8 us  [core_sum(): pl.pallas_call(core_sum_kernel, out_shape=(shape((rows, LANES), f32), cod...]
    pallas_call x2, Pallas kernels: 1.52 us -> 0.45 us  [ring_sum(): pl.pallas_call(functools.partial(ring_sum_kernel, GROUPS[which]), out_sha...]
    unnamed x6 -> x2, local copies, waits for them, and re-layouts: 0.93 us -> 0.01 us
  transfers between devices with their start and end apart: 14 -> 14, of which waited for: 8 -> 9; matrix products, arithmetic and copies ran while one was open for 0% -> 0% of each run, Pallas kernels for 21% -> 16%
where the time goes in v3:
time: 86 us; the launch traced here: 85.7 us
  blocking collectives  26.7 us (31%)
  starting transfers between devices  25.1 us (29%)
  waiting for transfers between devices  17.2 us (20%)
  Pallas kernels  16.5 us (19%)
    ppermute x14, starting transfers between devices, shift(): lax.ppermute(value, ('occ', 'vir'), [(index(*s), index(*place(*s))) for s...  25.1 us
    ppermute x14, waiting for transfers between devices, shift(): lax.ppermute(value, ('occ', 'vir'), [(index(*s), index(*place(*s))) for s...  17.2 us
    all_to_all x1, blocking collectives, shards(): lax.all_to_all(parts, 'vir', split_axis=0, concat_axis=0, tiled=True)  13.8 us
    all_to_all x1, blocking collectives, shards(): lax.all_to_all(parts, 'occ', split_axis=0, concat_axis=0, tiled=True)  12.9 us
    pallas_call x2, Pallas kernels, compute(): pl.pallas_call(functools.partial(compute_kernel, group, shifts), out_shap...  7.4 us
    pallas_call x1, Pallas kernels, fetch_blocks(): pl.pallas_call(fetch_kernel, out_shape=pltpu.VMEM((TILES * SLOTS, ENTRY,...  4.24 us
    pallas_call x2, Pallas kernels, core_sum(): pl.pallas_call(core_sum_kernel, out_shape=(shape((rows, LANES), f32), cod...  1.8 us
  transfers between devices with their start and end apart: 14, of which 9 were waited for; matrix products, arithmetic and copies ran while one was open for 0% of the time, Pallas kernels for 16%

profile of v3, /device:TPU:1, one launch (start us, length us, event | category | flops | bytes accessed | tf_op | source)
XLA Modules:
  0.0 85.7 jit_solution(5593849709105703291)
XLA Ops:
  0.0 1.0 %shard_map.55 = bf16[528,128]{1,0:T(8,128)(2,1)S(1)} custom-call(s32[1,4]{1,0:T(1,128)} %live_hbm.4, bf16[32,4096]{1,0:T(8,128)(2,1)} %amp_hbm.1), custom_call_target="tpu_custom_call" | custom-call | tf_op jit(solution)/shard_map/pallas_call | solution.py:80
  1.0 3.4 %collective-permute-start.2 = (bf16[528,128]{1,0:T(8,128)(2,1)S(1)}, bf16[528,128]{1,0:T(8,128)(2,1)S(1)}, u32[]{:S(2)}, u32[]{:S(2)}) collective-permute-start(bf16[528,128]{1,0:T(8,128)(2,1)S(1)} %shard_map.55), channel_id=1, source_target_pairs={{0,24},{1,97},{2,26},{3,99},{4,28},{5,101},{6,30},{7,103},{8,0},{9... | collective-permute-start | bytes 405512 | tf_op jit(solution)/shard_map/ppermute | solution.py:99
  4.4 0.5 collective-permute-start.1
  4.9 0.6 collective-permute-start
  5.5 2.3 %collective-permute-done.2 = bf16[528,128]{1,0:T(8,128)(2,1)S(1)} collective-permute-done((bf16[528,128]{1,0:T(8,128)(2,1)S(1)}, bf16[528,128]{1,0:T(8,128)(2,1)S(1)}, u32[]{:S(2)}, u32[]{:S(2)}) %collective-permute-start.2) | collective-permute-done | bytes 135200 | tf_op jit(solution)/shard_map/ppermute | solution.py:99
  7.8 2.1 %collective-permute-done.1 = bf16[528,128]{1,0:T(8,128)(2,1)S(1)} collective-permute-done((bf16[528,128]{1,0:T(8,128)(2,1)S(1)}, bf16[528,128]{1,0:T(8,128)(2,1)S(1)}, u32[]{:S(2)}, u32[]{:S(2)}) %collective-permute-start.1) | collective-permute-done | bytes 135200 | tf_op jit(solution)/shard_map/ppermute | solution.py:99
  9.9 1.6 %collective-permute-done = bf16[528,128]{1,0:T(8,128)(2,1)S(1)} collective-permute-done((bf16[528,128]{1,0:T(8,128)(2,1)S(1)}, bf16[528,128]{1,0:T(8,128)(2,1)S(1)}, u32[]{:S(2)}, u32[]{:S(2)}) %collective-permute-start) | collective-permute-done | bytes 135200 | tf_op jit(solution)/shard_map/ppermute | solution.py:99
  11.5 3.5 %collective-permute-start.3 = (bf16[2112,128]{1,0:T(8,128)(2,1)S(1)}, bf16[2112,128]{1,0:T(8,128)(2,1)S(1)}, u32[]{:S(2)}, u32[]{:S(2)}) collective-permute-start(bf16[2112,128]{1,0:T(8,128)(2,1)S(1)} %pad_maximum_fusion.after_ref.refs_0_), channel_id=1, source_target_pairs={{0,96},{1,25},{2,98},{3,27},{4,100},{5,29},{6,102},{7,31},{8,104},... | collective-permute-start | bytes 1622024 | tf_op jit(solution)/shard_map/ppermute | solution.py:99
  15.1 0.0 collective-permute-start.4
  15.1 4.2 %shard_map.56.block_ref = bf16[8,1024,1024]{2,1,0:T(8,128)(2,1)S(1)} custom-call(s32[2,4]{1,0:T(2,128)} %live_hbm.7, bf16[2,4,1024,1024]{3,2,1,0:T(8,128)(2,1)} %ints_hbm.1, bf16[2112,128]{1,0:T(8,128)(2,1)S(1)} %pad_maximum_fusion.after_ref.refs_0_), custom_call_target="tpu_custom_call" | custom-call | bytes 33554432 | tf_op jit(solution)/shard_map/pallas_call | solution.py:137
  19.3 2.1 %collective-permute-done.3.refs_3_.refs_2_ = bf16[2112,128]{1,0:T(8,128)(2,1)S(1)} collective-permute-done((bf16[2112,128]{1,0:T(8,128)(2,1)S(1)}, bf16[2112,128]{1,0:T(8,128)(2,1)S(1)}, u32[]{:S(2)}, u32[]{:S(2)}) %collective-permute-start.3) | collective-permute-done | bytes 540704 | tf_op jit(solution)/shard_map/ppermute | solution.py:99
  21.4 2.0 %collective-permute-start.5 = (bf16[2112,128]{1,0:T(8,128)(2,1)S(1)}, bf16[2112,128]{1,0:T(8,128)(2,1)S(1)}, u32[]{:S(2)}, u32[]{:S(2)}) collective-permute-start(bf16[2112,128]{1,0:T(8,128)(2,1)S(1)} %pad_maximum_fusion.after_ref.refs_0_), channel_id=1, source_target_pairs={{0,64},{1,17},{2,66},{3,19},{4,68},{5,21},{6,70},{7,23},{8,72},{9,... | collective-permute-start | bytes 1622024 | tf_op jit(solution)/shard_map/ppermute | solution.py:99
  23.4 1.4 %collective-permute-done.4.refs_1_ = bf16[2112,128]{1,0:T(8,128)(2,1)S(1)} collective-permute-done((bf16[2112,128]{1,0:T(8,128)(2,1)S(1)}, bf16[2112,128]{1,0:T(8,128)(2,1)S(1)}, u32[]{:S(2)}, u32[]{:S(2)}) %collective-permute-start.4) | collective-permute-done | bytes 540704 | tf_op jit(solution)/shard_map/ppermute | solution.py:99
  24.8 3.9 %shard_map.59 = (f32[4,576,128]{2,1,0:T(8,128)S(1)}, f32[4,576,128]{2,1,0:T(8,128)S(1)}) custom-call(s32[2,4]{1,0:T(2,128)} %live_hbm.7, bf16[8,1024,1024]{2,1,0:T(8,128)(2,1)S(1)} %shard_map.56.block_ref, bf16[2112,128]{1,0:T(8,128)(2,1)S(1)} %pad_maximum_fusion.after_ref.refs_0_, bf16[2112,128]{1,0:T(8,128)(2,1)S(1)} %collective-permute-done.4.refs_1_, ...), custom_call_target="tpu_custom_call" | custom-call | flops 4294967296 | bytes 8388608 | tf_op jit(solution)/shard_map/pallas_call | solution.py:245
  28.7 5.0 %collective-permute-start.10 = (f32[4,576,128]{2,1,0:T(8,128)S(1)}, f32[4,576,128]{2,1,0:T(8,128)S(1)}, u32[]{:S(2)}, u32[]{:S(2)}) collective-permute-start(f32[4,576,128]{2,1,0:T(8,128)S(1)} %get-tuple-element.30), channel_id=1, source_target_pairs={{0,1},{1,0},{2,3},{3,2},{4,5},{5,4},{6,7},{7,6},{8,9},{9,8},{10,11... | collective-permute-start | bytes 3538952 | tf_op jit(solution)/shard_map/ppermute | solution.py:99
  33.7 0.0 collective-permute-done.5.refs_2_
  33.7 3.5 %shard_map.57 = (f32[4,448,128]{2,1,0:T(8,128)S(1)}, f32[4,448,128]{2,1,0:T(8,128)S(1)}) custom-call(s32[2,4]{1,0:T(2,128)} %live_hbm.7, bf16[8,1024,1024]{2,1,0:T(8,128)(2,1)S(1)} %shard_map.56.block_ref, bf16[2112,128]{1,0:T(8,128)(2,1)S(1)} %pad_maximum_fusion.after_ref.refs_0_, bf16[2112,128]{1,0:T(8,128)(2,1)S(1)} %collective-permute-done.4.refs_1_, ...), custom_call_target="tpu_custom_call" | custom-call | flops 4294967296 | bytes 8388608 | tf_op jit(solution)/shard_map/pallas_call | solution.py:245
  37.2 2.9 %collective-permute-start.6 = (f32[4,448,128]{2,1,0:T(8,128)S(1)}, f32[4,448,128]{2,1,0:T(8,128)S(1)}, u32[]{:S(2)}, u32[]{:S(2)}) collective-permute-start(f32[4,448,128]{2,1,0:T(8,128)S(1)} %get-tuple-element.24), channel_id=1, source_target_pairs={{0,1},{1,0},{2,3},{3,2},{4,5},{5,4},{6,7},{7,6},{8,9},{9,8},{10,11... | collective-permute-start | bytes 2752520 | tf_op jit(solution)/shard_map/ppermute | solution.py:99
  40.1 0.0 collective-permute-done.10.other_ref
  40.1 1.0 %shard_map.60 = (f32[576,128]{1,0:T(8,128)S(1)}, s16[608,128]{1,0:T(8,128)(2,1)S(1)}, s16[608,128]{1,0:T(8,128)(2,1)S(1)}, s16[608,128]{1,0:T(8,128)(2,1)S(1)}) custom-call(f32[4,576,128]{2,1,0:T(8,128)S(1)} %get-tuple-element.29.mine_ref, f32[4,576,128]{2,1,0:T(8,128)S(1)} %collective-permute-done.10.other_ref), custom_call_target="tpu_custom_call" | custom-call | tf_op jit(solution)/shard_map/pallas_call | solution.py:304
  41.1 1.3 %collective-permute-start.11 = (s16[608,128]{1,0:T(8,128)(2,1)S(1)}, s16[608,128]{1,0:T(8,128)(2,1)S(1)}, u32[]{:S(2)}, u32[]{:S(2)}) collective-permute-start(s16[608,128]{1,0:T(8,128)(2,1)S(1)} %get-tuple-element.32), channel_id=1, source_target_pairs={{0,2},{1,3},{2,4},{3,5},{4,6},{5,7},{6,0},{7,1},{8,10},{9,11},{10,... | collective-permute-start | bytes 466952 | tf_op jit(solution)/shard_map/ppermute | solution.py:99
  42.4 2.1 %collective-permute-start.12 = (s16[608,128]{1,0:T(8,128)(2,1)S(1)}, s16[608,128]{1,0:T(8,128)(2,1)S(1)}, u32[]{:S(2)}, u32[]{:S(2)}) collective-permute-start(s16[608,128]{1,0:T(8,128)(2,1)S(1)} %get-tuple-element.33), channel_id=1, source_target_pairs={{0,4},{1,5},{2,6},{3,7},{4,0},{5,1},{6,2},{7,3},{8,12},{9,13},{10,... | collective-permute-start | bytes 466952 | tf_op jit(solution)/shard_map/ppermute | solution.py:99
  44.5 0.9 %collective-permute-start.13 = (s16[608,128]{1,0:T(8,128)(2,1)S(1)}, s16[608,128]{1,0:T(8,128)(2,1)S(1)}, u32[]{:S(2)}, u32[]{:S(2)}) collective-permute-start(s16[608,128]{1,0:T(8,128)(2,1)S(1)} %get-tuple-element.34), channel_id=1, source_target_pairs={{0,6},{1,7},{2,0},{3,1},{4,2},{5,3},{6,4},{7,5},{8,14},{9,15},{10,... | collective-permute-start | bytes 466952 | tf_op jit(solution)/shard_map/ppermute | solution.py:99
  45.5 0.0 collective-permute-done.6.other_ref
  45.5 0.8 shard_map.58
  46.3 0.6 collective-permute-start.7
  46.9 0.9 %collective-permute-start.8 = (s16[464,128]{1,0:T(8,128)(2,1)S(1)}, s16[464,128]{1,0:T(8,128)(2,1)S(1)}, u32[]{:S(2)}, u32[]{:S(2)}) collective-permute-start(s16[464,128]{1,0:T(8,128)(2,1)S(1)} %get-tuple-element.27), channel_id=1, source_target_pairs={{0,4},{1,5},{2,6},{3,7},{4,0},{5,1},{6,2},{7,3},{8,12},{9,13},{10,... | collective-permute-start | bytes 356360 | tf_op jit(solution)/shard_map/ppermute | solution.py:99
  47.7 0.3 collective-permute-done.11.a_ref
  48.0 1.4 %collective-permute-start.9 = (s16[464,128]{1,0:T(8,128)(2,1)S(1)}, s16[464,128]{1,0:T(8,128)(2,1)S(1)}, u32[]{:S(2)}, u32[]{:S(2)}) collective-permute-start(s16[464,128]{1,0:T(8,128)(2,1)S(1)} %get-tuple-element.28), channel_id=1, source_target_pairs={{0,6},{1,7},{2,0},{3,1},{4,2},{5,3},{6,4},{7,5},{8,14},{9,15},{10,... | collective-permute-start | bytes 356360 | tf_op jit(solution)/shard_map/ppermute | solution.py:99
  49.3 2.7 %collective-permute-done.12.b_ref = s16[608,128]{1,0:T(8,128)(2,1)S(1)} collective-permute-done((s16[608,128]{1,0:T(8,128)(2,1)S(1)}, s16[608,128]{1,0:T(8,128)(2,1)S(1)}, u32[]{:S(2)}, u32[]{:S(2)}) %collective-permute-start.12) | collective-permute-done | bytes 155680 | tf_op jit(solution)/shard_map/ppermute | solution.py:99
  52.0 0.0 collective-permute-done.13.c_ref
  52.0 0.3 shard_map.61.refs_0_
  52.3 0.0 copy-start
  52.3 2.9 %collective-permute-done.7.a_ref = s16[464,128]{1,0:T(8,128)(2,1)S(1)} collective-permute-done((s16[464,128]{1,0:T(8,128)(2,1)S(1)}, s16[464,128]{1,0:T(8,128)(2,1)S(1)}, u32[]{:S(2)}, u32[]{:S(2)}) %collective-permute-start.7) | collective-permute-done | bytes 118816 | tf_op jit(solution)/shard_map/ppermute | solution.py:99
  55.2 1.9 %collective-permute-done.8.b_ref = s16[464,128]{1,0:T(8,128)(2,1)S(1)} collective-permute-done((s16[464,128]{1,0:T(8,128)(2,1)S(1)}, s16[464,128]{1,0:T(8,128)(2,1)S(1)}, u32[]{:S(2)}, u32[]{:S(2)}) %collective-permute-start.8) | collective-permute-done | bytes 118816 | tf_op jit(solution)/shard_map/ppermute | solution.py:99
  57.1 0.0 collective-permute-done.9.c_ref
  57.1 0.2 shard_map.62
  57.3 12.9 %all_to_all.10.in_ref = s16[16,80,128]{2,1,0:T(8,128)(2,1)S(1)} all-to-all(s16[16,80,128]{2,1,0:T(8,128)(2,1)S(1)} %shard_map.62), channel_id=1, replica_groups=mesh['occ'=16,'vir'=8] {'occ'}, dimensions={0} | all-to-all | bytes 655360 | tf_op jit(solution)/shard_map/all_to_all | solution.py:420
  70.2 0.0 copy-done
  70.2 0.8 shard_map.63
  71.0 13.8 %all_to_all.11.in_ref = s16[8,144,128]{2,1,0:T(8,128)(2,1)S(1)} all-to-all(s16[8,144,128]{2,1,0:T(8,128)(2,1)S(1)} %shard_map.63), channel_id=1, replica_groups=mesh['occ'=16,'vir'=8] {'vir'}, dimensions={0} | all-to-all | bytes 589824 | tf_op jit(solution)/shard_map/all_to_all | solution.py:422
  84.8 0.9 %shard_map.64 = f32[32,4096]{1,0:T(8,128)} custom-call(s16[8,144,128]{2,1,0:T(8,128)(2,1)S(1)} %all_to_all.11.in_ref), custom_call_target="tpu_custom_call" | custom-call | tf_op jit(solution)/shard_map/pallas_call | solution.py:393
  (1 shorter events, 0.0 us)
Async XLA Ops:
  1.0 6.8 %collective-permute-start.2 = (bf16[528,128]{1,0:T(8,128)(2,1)S(1)}, bf16[528,128]{1,0:T(8,128)(2,1)S(1)}, u32[]{:S(2)}, u32[]{:S(2)}) collective-permute-start(bf16[528,128]{1,0:T(8,128)(2,1)S(1)} %shard_map.55), channel_id=1, source_target_pairs={{0,24},{1,97},{2,26},{3,99},{4,28},{5,101},{6,30},{7,103},{8,0},{9... | collective-permute-start | bytes 405512 | tf_op jit(solution)/shard_map/ppermute | solution.py:99
  4.4 5.5 %collective-permute-start.1 = (bf16[528,128]{1,0:T(8,128)(2,1)S(1)}, bf16[528,128]{1,0:T(8,128)(2,1)S(1)}, u32[]{:S(2)}, u32[]{:S(2)}) collective-permute-start(bf16[528,128]{1,0:T(8,128)(2,1)S(1)} %shard_map.55), channel_id=1, source_target_pairs={{0,16},{1,65},{2,18},{3,67},{4,20},{5,69},{6,22},{7,71},{8,24},{9,... | collective-permute-start | bytes 405512 | tf_op jit(solution)/shard_map/ppermute | solution.py:99
  4.9 6.6 %collective-permute-start = (bf16[528,128]{1,0:T(8,128)(2,1)S(1)}, bf16[528,128]{1,0:T(8,128)(2,1)S(1)}, u32[]{:S(2)}, u32[]{:S(2)}) collective-permute-start(bf16[528,128]{1,0:T(8,128)(2,1)S(1)} %shard_map.55), channel_id=1, source_target_pairs={{0,8},{1,33},{2,10},{3,35},{4,12},{5,37},{6,14},{7,39},{8,16},{9,4... | collective-permute-start | bytes 405512 | tf_op jit(solution)/shard_map/ppermute | solution.py:99
  11.5 9.8 %collective-permute-start.3 = (bf16[2112,128]{1,0:T(8,128)(2,1)S(1)}, bf16[2112,128]{1,0:T(8,128)(2,1)S(1)}, u32[]{:S(2)}, u32[]{:S(2)}) collective-permute-start(bf16[2112,128]{1,0:T(8,128)(2,1)S(1)} %pad_maximum_fusion.after_ref.refs_0_), channel_id=1, source_target_pairs={{0,96},{1,25},{2,98},{3,27},{4,100},{5,29},{6,102},{7,31},{8,104},... | collective-permute-start | bytes 1622024 | tf_op jit(solution)/shard_map/ppermute | solution.py:99
  15.1 9.7 %collective-permute-start.4 = (bf16[2112,128]{1,0:T(8,128)(2,1)S(1)}, bf16[2112,128]{1,0:T(8,128)(2,1)S(1)}, u32[]{:S(2)}, u32[]{:S(2)}) collective-permute-start(bf16[2112,128]{1,0:T(8,128)(2,1)S(1)} %pad_maximum_fusion.after_ref.refs_0_), channel_id=1, source_target_pairs={{0,32},{1,9},{2,34},{3,11},{4,36},{5,13},{6,38},{7,15},{8,40},{9,1... | collective-permute-start | bytes 1622024 | tf_op jit(solution)/shard_map/ppermute | solution.py:99
  21.4 12.3 %collective-permute-start.5 = (bf16[2112,128]{1,0:T(8,128)(2,1)S(1)}, bf16[2112,128]{1,0:T(8,128)(2,1)S(1)}, u32[]{:S(2)}, u32[]{:S(2)}) collective-permute-start(bf16[2112,128]{1,0:T(8,128)(2,1)S(1)} %pad_maximum_fusion.after_ref.refs_0_), channel_id=1, source_target_pairs={{0,64},{1,17},{2,66},{3,19},{4,68},{5,21},{6,70},{7,23},{8,72},{9,... | collective-permute-start | bytes 1622024 | tf_op jit(solution)/shard_map/ppermute | solution.py:99
  28.7 11.4 %collective-permute-start.10 = (f32[4,576,128]{2,1,0:T(8,128)S(1)}, f32[4,576,128]{2,1,0:T(8,128)S(1)}, u32[]{:S(2)}, u32[]{:S(2)}) collective-permute-start(f32[4,576,128]{2,1,0:T(8,128)S(1)} %get-tuple-element.30), channel_id=1, source_target_pairs={{0,1},{1,0},{2,3},{3,2},{4,5},{5,4},{6,7},{7,6},{8,9},{9,8},{10,11... | collective-permute-start | bytes 3538952 | tf_op jit(solution)/shard_map/ppermute | solution.py:99
  37.2 8.3 %collective-permute-start.6 = (f32[4,448,128]{2,1,0:T(8,128)S(1)}, f32[4,448,128]{2,1,0:T(8,128)S(1)}, u32[]{:S(2)}, u32[]{:S(2)}) collective-permute-start(f32[4,448,128]{2,1,0:T(8,128)S(1)} %get-tuple-element.24), channel_id=1, source_target_pairs={{0,1},{1,0},{2,3},{3,2},{4,5},{5,4},{6,7},{7,6},{8,9},{9,8},{10,11... | collective-permute-start | bytes 2752520 | tf_op jit(solution)/shard_map/ppermute | solution.py:99
  41.1 6.9 %collective-permute-start.11 = (s16[608,128]{1,0:T(8,128)(2,1)S(1)}, s16[608,128]{1,0:T(8,128)(2,1)S(1)}, u32[]{:S(2)}, u32[]{:S(2)}) collective-permute-start(s16[608,128]{1,0:T(8,128)(2,1)S(1)} %get-tuple-element.32), channel_id=1, source_target_pairs={{0,2},{1,3},{2,4},{3,5},{4,6},{5,7},{6,0},{7,1},{8,10},{9,11},{10,... | collective-permute-start | bytes 466952 | tf_op jit(solution)/shard_map/ppermute | solution.py:99
  42.4 9.6 %collective-permute-start.12 = (s16[608,128]{1,0:T(8,128)(2,1)S(1)}, s16[608,128]{1,0:T(8,128)(2,1)S(1)}, u32[]{:S(2)}, u32[]{:S(2)}) collective-permute-start(s16[608,128]{1,0:T(8,128)(2,1)S(1)} %get-tuple-element.33), channel_id=1, source_target_pairs={{0,4},{1,5},{2,6},{3,7},{4,0},{5,1},{6,2},{7,3},{8,12},{9,13},{10,... | collective-permute-start | bytes 466952 | tf_op jit(solution)/shard_map/ppermute | solution.py:99
  44.5 7.5 %collective-permute-start.13 = (s16[608,128]{1,0:T(8,128)(2,1)S(1)}, s16[608,128]{1,0:T(8,128)(2,1)S(1)}, u32[]{:S(2)}, u32[]{:S(2)}) collective-permute-start(s16[608,128]{1,0:T(8,128)(2,1)S(1)} %get-tuple-element.34), channel_id=1, source_target_pairs={{0,6},{1,7},{2,0},{3,1},{4,2},{5,3},{6,4},{7,5},{8,14},{9,15},{10,... | collective-permute-start | bytes 466952 | tf_op jit(solution)/shard_map/ppermute | solution.py:99
  46.3 8.9 %collective-permute-start.7 = (s16[464,128]{1,0:T(8,128)(2,1)S(1)}, s16[464,128]{1,0:T(8,128)(2,1)S(1)}, u32[]{:S(2)}, u32[]{:S(2)}) collective-permute-start(s16[464,128]{1,0:T(8,128)(2,1)S(1)} %get-tuple-element.26), channel_id=1, source_target_pairs={{0,2},{1,3},{2,4},{3,5},{4,6},{5,7},{6,0},{7,1},{8,10},{9,11},{10,... | collective-permute-start | bytes 356360 | tf_op jit(solution)/shard_map/ppermute | solution.py:99
  46.9 10.3 %collective-permute-start.8 = (s16[464,128]{1,0:T(8,128)(2,1)S(1)}, s16[464,128]{1,0:T(8,128)(2,1)S(1)}, u32[]{:S(2)}, u32[]{:S(2)}) collective-permute-start(s16[464,128]{1,0:T(8,128)(2,1)S(1)} %get-tuple-element.27), channel_id=1, source_target_pairs={{0,4},{1,5},{2,6},{3,7},{4,0},{5,1},{6,2},{7,3},{8,12},{9,13},{10,... | collective-permute-start | bytes 356360 | tf_op jit(solution)/shard_map/ppermute | solution.py:99
  48.0 9.1 %collective-permute-start.9 = (s16[464,128]{1,0:T(8,128)(2,1)S(1)}, s16[464,128]{1,0:T(8,128)(2,1)S(1)}, u32[]{:S(2)}, u32[]{:S(2)}) collective-permute-start(s16[464,128]{1,0:T(8,128)(2,1)S(1)} %get-tuple-element.28), channel_id=1, source_target_pairs={{0,6},{1,7},{2,0},{3,1},{4,2},{5,3},{6,4},{7,5},{8,14},{9,15},{10,... | collective-permute-start | bytes 356360 | tf_op jit(solution)/shard_map/ppermute | solution.py:99
  52.3 17.9 %copy-start = (s32[32]{0:T(128)S(1)}, s32[32]{0:T(128)}, u32[]{:S(2)}) copy-start(s32[32]{0:T(128)} %owner_ref.1) | copy-start | bytes 388

commit v4 on v3

--- a/solution.py
+++ b/solution.py
@@ -115,40 +115,6 @@
     return shift(value, lambda x, z, y, c: (x, z, y, c + 1))
 
 
-def fetch_kernel(live_hbm, ints_hbm, after_ref, block_ref, live, sem, sems):
-    del after_ref
-    copy = pltpu.make_async_copy(live_hbm, live, sem)
-    copy.start()
-    copy.wait()
-
-    def fetch(r, c):
-        i = c * SLOTS + r
-        return pltpu.make_async_copy(ints_hbm.at[r, c], block_ref.at[i], sems.at[i])
-
-    for c in range(TILES):
-        for r in range(SLOTS):
-            pl.when(live[r, c] != 0)(lambda: fetch(r, c).start())
-    for c in range(TILES):
-        for r in range(SLOTS):
-            pl.when(live[r, c] != 0)(lambda: fetch(r, c).wait())
-
-
-def fetch_blocks(block_live, integrals, after):
-    return pl.pallas_call(
-        fetch_kernel,
-        out_shape=pltpu.VMEM((TILES * SLOTS, ENTRY, ENTRY), bf16),
-        in_specs=[HBM, HBM, ANY],
-        out_specs=VMEM,
-        scratch_shapes=[
-            pltpu.SMEM(block_live.shape, i32),
-            pltpu.SemaphoreType.DMA,
-            pltpu.SemaphoreType.DMA((TILES * SLOTS,)),
-        ],
-        compiler_params=params(2),
-        cost_estimate=pl.CostEstimate(flops=0, bytes_accessed=32 << 20, transcendentals=0),
-    )(*in_hbm(block_live, integrals), after)
-
-
 NEAR = (0, 1, 3)
 GROUPS = (
     [(e, d) for e in NEAR for d in NEAR],
@@ -156,27 +122,39 @@
 )
 
 
-def compute_kernel(group, shifts, live_hbm, block_ref, *refs):
-    amps = dict(zip(shifts, refs[: len(shifts)]))
-    theirs_ref, mine_ref, left, product, table_v, table, live, count, where, sem = refs[len(shifts) :]
+def compute_kernel(group, sources, fetches, live_hbm, ints_hbm, *refs):
+    count_in = max(at for at, _ in sources.values()) + 1
+    arrays = refs[:count_in]
+    refs = refs[count_in + (0 if fetches else 1) :]
+    theirs_ref, mine_ref, block_ref, left, product, table_v, table, live, count, where, sem, sems = refs
     core = position()[3]
     copy_live = pltpu.make_async_copy(live_hbm, live, sem.at[0])
     copy_live.start()
 
+    def fetch(i):
+        return pltpu.make_async_copy(ints_hbm.at[lax.rem(i, SLOTS), i // SLOTS], block_ref.at[i], sems.at[i])
+
+    def piece(a, b, row, rows):
+        at, base = sources[a, b]
+        return arrays[at][pl.ds(base + row, rows), :]
+
     lane = lax.broadcasted_iota(i32, (8, LANES), 1)
     entries = jnp.zeros((8, LANES), i32)
     for k, (a, b) in enumerate(group):
-        tag = amps[a][pl.ds(b * PIECE + TAG, META), :].astype(f32)[:8].astype(i32)
+        tag = piece(a, b, TAG, META).astype(f32)[:8].astype(i32)
         entries = jnp.where(lane == k, tag, entries)
     table_v[...] = entries
     copy_table = pltpu.make_async_copy(table_v, table, sem.at[1])
     copy_table.start()
 
+    copy_live.wait()
+    if fetches:
+        for i in range(TILES * SLOTS):
+            pl.when(live[i % SLOTS, i // SLOTS] != 0)(functools.partial(lambda i: fetch(i).start(), i))
     theirs_ref[...] = jnp.zeros_like(theirs_ref)
     mine_ref[...] = jnp.zeros_like(mine_ref)
     for c in range(TILES):
         count[c] = 0
-    copy_live.wait()
     copy_table.wait()
 
     for k, (a, b) in enumerate(group):
@@ -192,15 +170,17 @@
                 where[c * BLOCKS + at] = o
                 rows = pl.multiple_of(at * ROWS, ROWS)
                 for kb in range(KB):
-                    left[c, pl.ds(rows, ROWS), kb * LANES : (kb + 1) * LANES] = amps[a][
-                        pl.ds(b * PIECE + (kb * LIVE + slot) * ROWS, ROWS), :
-                    ]
+                    left[c, pl.ds(rows, ROWS), kb * LANES : (kb + 1) * LANES] = piece(
+                        a, b, (kb * LIVE + slot) * ROWS, ROWS
+                    )
 
     def one_block(i, carry):
         c, r = i // SLOTS, lax.rem(i, SLOTS)
 
         @pl.when(live[r, c] != 0)
         def _():
+            if fetches:
+                fetch(i).wait()
             n = count[c]
 
             def one_chunk(j, inner):
@@ -238,15 +218,18 @@
     lax.fori_loop(0, TILES * SLOTS, one_block, 0)
 
 
-def compute(which, block_live, blocks, amps):
+def compute(which, block_live, integrals, blocks, pieces):
     group = GROUPS[which]
-    shifts = sorted(amps)
+    fetches = blocks is None
+    sources = {ab: (i, k * PIECE) for i, (_, held) in enumerate(pieces) for k, ab in enumerate(held)}
     total = pltpu.VMEM((RING, len(group) * SLOTS * ROWS, LANES), f32)
-    return pl.pallas_call(
-        functools.partial(compute_kernel, group, shifts),
-        out_shape=(total, total),
-        in_specs=[HBM] + [VMEM] * (1 + len(shifts)),
-        out_specs=(VMEM,) * 2,
+    more = [] if fetches else in_vmem(blocks)
+    return pl.pallas_call(
+        functools.partial(compute_kernel, group, sources, fetches),
+        out_shape=(total, total, pltpu.VMEM((TILES * SLOTS, ENTRY, ENTRY), bf16)),
+        in_specs=[HBM, HBM] + [VMEM] * (len(pieces) + len(more)),
+        out_specs=(VMEM,) * 3,
+        input_output_aliases={} if fetches else {2 + len(pieces): 2},
         scratch_shapes=[
             pltpu.VMEM((TILES, 2 * CHUNK, ENTRY), bf16),
             pltpu.VMEM((CHUNK, ENTRY), f32),
@@ -256,10 +239,11 @@
             pltpu.SMEM((TILES,), i32),
             pltpu.SMEM((TILES * BLOCKS,), i32),
             pltpu.SemaphoreType.DMA((2,)),
+            pltpu.SemaphoreType.DMA((TILES * SLOTS,)),
         ],
         compiler_params=params(8),
         cost_estimate=pl.CostEstimate(flops=1 << 32, bytes_accessed=8 << 20, transcendentals=0),
-    )(*in_hbm(block_live), *in_vmem(blocks), *[amps[a] for a in shifts])
+    )(*in_hbm(block_live, integrals), *[array for array, _ in pieces], *more)
 
 
 def encode(value):
@@ -400,16 +384,22 @@
 
 
 def shards(amplitudes, tile_live, integrals, block_live, row_owner):
-    packed = pack(tile_live, amplitudes)
-    row = jnp.concatenate([packed] + [shift_first(packed, b) for b in range(1, RING)], 0)
-    amps = {0: row, 1: shift_second(row, 1), 3: shift_second(row, 3)}
-    blocks = fetch_blocks(block_live, integrals, row)
-    late, amps[3], blocks = lax.optimization_barrier((row, amps[3], blocks))
-    amps[2] = shift_second(late, 2)
-
-    theirs0, mine0 = compute(0, block_live, blocks, {a: amps[a] for a in NEAR})
+    own = pack(tile_live, amplitudes)
+    by1, by3, by2 = (shift_first(own, b) for b in (1, 3, 2))
+    at_once = {a: shift_second(own, a) for a in (1, 3)}
+    near = jnp.concatenate([by1, by3], 0)
+    nears = {a: shift_second(near, a) for a in (1, 3)}
+    row = jnp.concatenate([own, by1, by2, by3], 0)
+    row, nears[3] = lax.optimization_barrier((row, nears[3]))
+    first = [(own, [(0, 0)]), (by1, [(0, 1)]), (by3, [(0, 3)])]
+    for a in (1, 3):
+        first += [(at_once[a], [(a, 0)]), (nears[a], [(a, 1), (a, 3)])]
+    second = [(shift_second(row, 2), [(2, b) for b in range(RING)]), (by2, [(0, 2)])]
+    second += [(shift_second(by2, a), [(a, 2)]) for a in (1, 3)]
+
+    theirs0, mine0, blocks = compute(0, block_live, integrals, None, first)
     other0 = shift_core(theirs0)
-    theirs1, mine1 = compute(1, block_live, blocks, amps)
+    theirs1, mine1, _ = compute(1, block_live, integrals, blocks, second)
     other1 = shift_core(theirs1)
     own0, *sends0 = core_sum(mine0, other0)
     codes0 = [shift_y(sends0[d - 1], d) for d in range(1, RING)]

time: 86 us -> 82.6 us (0.960)
  waiting for transfers between devices: 17.2 us -> 11.1 us
  starting transfers between devices: 25.1 us -> 28 us
    ppermute x14 -> x18, waiting for transfers between devices: 17.2 us -> 11.1 us  [shift(): lax.ppermute(value, ('occ', 'vir'), [(index(*s), index(*place(*s))) for s...]
    ppermute x14 -> x18, starting transfers between devices: 25.1 us -> 28 us  [shift(): lax.ppermute(value, ('occ', 'vir'), [(index(*s), index(*place(*s))) for s...]
    all_to_all x1, blocking collectives: 12.9 us -> 14.1 us  [shards(): lax.all_to_all(parts, 'occ', split_axis=0, concat_axis=0, tiled=True)]
    pallas_call x3 -> x2, Pallas kernels: 11.6 us -> 10.7 us  [compute(): pl.pallas_call(functools.partial(compute_kernel, group, sources, fetches)...]
  transfers between devices with their start and end apart: 14 -> 18, of which waited for: 9 -> 5; matrix products, arithmetic and copies ran while one was open for 0% -> 0% of each run, Pallas kernels for 16% -> 16%
where the time goes in v4:
time: 82.6 us; the launch traced here: 82.3 us
  starting transfers between devices  28 us (34%)
  blocking collectives  27.3 us (33%)
  Pallas kernels  15.7 us (19%)
  waiting for transfers between devices  11.1 us (13%)
    ppermute x18, starting transfers between devices, shift(): lax.ppermute(value, ('occ', 'vir'), [(index(*s), index(*place(*s))) for s...  28 us
    all_to_all x1, blocking collectives, shards(): lax.all_to_all(parts, 'occ', split_axis=0, concat_axis=0, tiled=True)  14.1 us
    all_to_all x1, blocking collectives, shards(): lax.all_to_all(parts, 'vir', split_axis=0, concat_axis=0, tiled=True)  13.2 us
    ppermute x18, waiting for transfers between devices, shift(): lax.ppermute(value, ('occ', 'vir'), [(index(*s), index(*place(*s))) for s...  11.1 us
    pallas_call x2, Pallas kernels, compute(): pl.pallas_call(functools.partial(compute_kernel, group, sources, fetches)...  10.7 us
    pallas_call x2, Pallas kernels, core_sum(): pl.pallas_call(core_sum_kernel, out_shape=(shape((rows, LANES), f32), cod...  1.86 us
  transfers between devices with their start and end apart: 18, of which 5 were waited for; matrix products, arithmetic and copies ran while one was open for 0% of the time, Pallas kernels for 16%

profile of v4, /device:TPU:1, one launch (start us, length us, event | category | flops | bytes accessed | tf_op | source)
XLA Modules:
  0.0 82.3 jit_solution(7472669813170306011)
XLA Ops:
  0.0 1.0 %shard_map.55.refs_0_ = bf16[528,128]{1,0:T(8,128)(2,1)S(1)} custom-call(s32[1,4]{1,0:T(1,128)} %live_hbm.3, bf16[32,4096]{1,0:T(8,128)(2,1)} %amp_hbm.1), custom_call_target="tpu_custom_call" | custom-call | tf_op jit(solution)/shard_map/pallas_call | solution.py:80
  1.0 2.1 %collective-permute-start = (bf16[528,128]{1,0:T(8,128)(2,1)S(1)}, bf16[528,128]{1,0:T(8,128)(2,1)S(1)}, u32[]{:S(2)}, u32[]{:S(2)}) collective-permute-start(bf16[528,128]{1,0:T(8,128)(2,1)S(1)} %shard_map.55.refs_0_), channel_id=1, source_target_pairs={{0,8},{1,33},{2,10},{3,35},{4,12},{5,37},{6,14},{7,39},{8,16},{9,4... | collective-permute-start | bytes 405512 | tf_op jit(solution)/shard_map/ppermute | solution.py:99
  3.1 1.4 %collective-permute-start.2 = (bf16[528,128]{1,0:T(8,128)(2,1)S(1)}, bf16[528,128]{1,0:T(8,128)(2,1)S(1)}, u32[]{:S(2)}, u32[]{:S(2)}) collective-permute-start(bf16[528,128]{1,0:T(8,128)(2,1)S(1)} %shard_map.55.refs_0_), channel_id=1, source_target_pairs={{0,24},{1,97},{2,26},{3,99},{4,28},{5,101},{6,30},{7,103},{8,0},{9... | collective-permute-start | bytes 405512 | tf_op jit(solution)/shard_map/ppermute | solution.py:99
  4.5 1.6 %collective-permute-start.1 = (bf16[528,128]{1,0:T(8,128)(2,1)S(1)}, bf16[528,128]{1,0:T(8,128)(2,1)S(1)}, u32[]{:S(2)}, u32[]{:S(2)}) collective-permute-start(bf16[528,128]{1,0:T(8,128)(2,1)S(1)} %shard_map.55.refs_0_), channel_id=1, source_target_pairs={{0,16},{1,65},{2,18},{3,67},{4,20},{5,69},{6,22},{7,71},{8,24},{9,... | collective-permute-start | bytes 405512 | tf_op jit(solution)/shard_map/ppermute | solution.py:99
  6.1 1.6 %collective-permute-start.7 = (bf16[528,128]{1,0:T(8,128)(2,1)S(1)}, bf16[528,128]{1,0:T(8,128)(2,1)S(1)}, u32[]{:S(2)}, u32[]{:S(2)}) collective-permute-start(bf16[528,128]{1,0:T(8,128)(2,1)S(1)} %shard_map.55.refs_0_), channel_id=1, source_target_pairs={{0,32},{1,9},{2,34},{3,11},{4,36},{5,13},{6,38},{7,15},{8,40},{9,1... | collective-permute-start | bytes 405512 | tf_op jit(solution)/shard_map/ppermute | solution.py:99
  7.8 2.1 %collective-permute-start.9 = (bf16[528,128]{1,0:T(8,128)(2,1)S(1)}, bf16[528,128]{1,0:T(8,128)(2,1)S(1)}, u32[]{:S(2)}, u32[]{:S(2)}) collective-permute-start(bf16[528,128]{1,0:T(8,128)(2,1)S(1)} %shard_map.55.refs_0_), channel_id=1, source_target_pairs={{0,96},{1,25},{2,98},{3,27},{4,100},{5,29},{6,102},{7,31},{8,104},... | collective-permute-start | bytes 405512 | tf_op jit(solution)/shard_map/ppermute | solution.py:99
  9.9 0.0 collective-permute-done.refs_1_
  9.9 0.0 collective-permute-done.2.refs_2_
  9.9 1.5 %collective-permute-start.3 = (bf16[1056,128]{1,0:T(8,128)(2,1)S(1)}, bf16[1056,128]{1,0:T(8,128)(2,1)S(1)}, u32[]{:S(2)}, u32[]{:S(2)}) collective-permute-start(bf16[1056,128]{1,0:T(8,128)(2,1)S(1)} %constant_dynamic-update-slice_fusion), channel_id=1, source_target_pairs={{0,96},{1,25},{2,98},{3,27},{4,100},{5,29},{6,102},{7,31},{8,104},... | collective-permute-start | bytes 811016 | tf_op jit(solution)/shard_map/ppermute | solution.py:99
  11.5 0.0 collective-permute-start.8
  11.5 0.0 collective-permute-done.1.refs_1_
  11.5 4.9 %collective-permute-done.3.refs_6_ = bf16[1056,128]{1,0:T(8,128)(2,1)S(1)} collective-permute-done((bf16[1056,128]{1,0:T(8,128)(2,1)S(1)}, bf16[1056,128]{1,0:T(8,128)(2,1)S(1)}, u32[]{:S(2)}, u32[]{:S(2)}) %collective-permute-start.3) | collective-permute-done | bytes 270368 | tf_op jit(solution)/shard_map/ppermute | solution.py:99
  16.4 1.8 %collective-permute-start.4 = (bf16[2112,128]{1,0:T(8,128)(2,1)S(1)}, bf16[2112,128]{1,0:T(8,128)(2,1)S(1)}, u32[]{:S(2)}, u32[]{:S(2)}) collective-permute-start(bf16[2112,128]{1,0:T(8,128)(2,1)S(1)} %pad_maximum_fusion), channel_id=1, source_target_pairs={{0,64},{1,17},{2,66},{3,19},{4,68},{5,21},{6,70},{7,23},{8,72},{9,... | collective-permute-start | bytes 1622024 | tf_op jit(solution)/shard_map/ppermute | solution.py:99
  18.2 1.3 %collective-permute-start.5 = (bf16[528,128]{1,0:T(8,128)(2,1)S(1)}, bf16[528,128]{1,0:T(8,128)(2,1)S(1)}, u32[]{:S(2)}, u32[]{:S(2)}) collective-permute-start(bf16[528,128]{1,0:T(8,128)(2,1)S(1)} %collective-permute-done.1.refs_1_), channel_id=1, source_target_pairs={{0,32},{1,9},{2,34},{3,11},{4,36},{5,13},{6,38},{7,15},{8,40},{9,1... | collective-permute-start | bytes 405512 | tf_op jit(solution)/shard_map/ppermute | solution.py:99
  19.5 0.0 collective-permute-done.7.refs_3_
  19.5 1.4 %collective-permute-start.6 = (bf16[528,128]{1,0:T(8,128)(2,1)S(1)}, bf16[528,128]{1,0:T(8,128)(2,1)S(1)}, u32[]{:S(2)}, u32[]{:S(2)}) collective-permute-start(bf16[528,128]{1,0:T(8,128)(2,1)S(1)} %collective-permute-done.1.refs_1_), channel_id=1, source_target_pairs={{0,96},{1,25},{2,98},{3,27},{4,100},{5,29},{6,102},{7,31},{8,104},... | collective-permute-start | bytes 405512 | tf_op jit(solution)/shard_map/ppermute | solution.py:99
  20.9 0.0 collective-permute-done.9.refs_5_
  20.9 0.0 collective-permute-done.8.refs_4_
  20.9 6.1 %shard_map.56 = (f32[4,576,128]{2,1,0:T(8,128)S(1)}, f32[4,576,128]{2,1,0:T(8,128)S(1)}, bf16[8,1024,1024]{2,1,0:T(8,128)(2,1)S(1)}) custom-call(s32[2,4]{1,0:T(2,128)} %live_hbm.5, bf16[2,4,1024,1024]{3,2,1,0:T(8,128)(2,1)} %ints_hbm.3, bf16[528,128]{1,0:T(8,128)(2,1)S(1)} %shard_map.55.refs_0_, bf16[528,128]{1,0:T(8,128)(2,1)S(1)} %collective-permute-done.refs_1_, ...), custom_call_target="tpu_custom_call" | custom-call | flops 4294967296 | bytes 8388608 | tf_op jit(solution)/shard_map/pallas_call | solution.py:227
  27.0 3.2 %collective-permute-start.14 = (f32[4,576,128]{2,1,0:T(8,128)S(1)}, f32[4,576,128]{2,1,0:T(8,128)S(1)}, u32[]{:S(2)}, u32[]{:S(2)}) collective-permute-start(f32[4,576,128]{2,1,0:T(8,128)S(1)} %get-tuple-element.30), channel_id=1, source_target_pairs={{0,1},{1,0},{2,3},{3,2},{4,5},{5,4},{6,7},{7,6},{8,9},{9,8},{10,11... | collective-permute-start | bytes 3538952 | tf_op jit(solution)/shard_map/ppermute | solution.py:99
  30.2 0.0 collective-permute-done.5.refs_2_
  30.2 0.0 collective-permute-done.6.refs_3_
  30.2 0.0 collective-permute-done.4.refs_0_
  30.2 4.7 %shard_map.57 = (f32[4,448,128]{2,1,0:T(8,128)S(1)}, f32[4,448,128]{2,1,0:T(8,128)S(1)}, bf16[8,1024,1024]{2,1,0:T(8,128)(2,1)S(1)}) custom-call(s32[2,4]{1,0:T(2,128)} %live_hbm.5, bf16[2,4,1024,1024]{3,2,1,0:T(8,128)(2,1)} %ints_hbm.3, bf16[2112,128]{1,0:T(8,128)(2,1)S(1)} %collective-permute-done.4.refs_0_, ...), custom_call_target="tpu_custom_call", output_to_operand_aliasing={{2}: (6, {})} | custom-call | flops 4294967296 | bytes 8388608 | tf_op jit(solution)/shard_map/pallas_call | solution.py:227
  34.9 0.7 collective-permute-start.10
  35.5 0.0 collective-permute-done.14.other_ref
  35.5 1.0 %shard_map.59 = (f32[576,128]{1,0:T(8,128)S(1)}, s16[608,128]{1,0:T(8,128)(2,1)S(1)}, s16[608,128]{1,0:T(8,128)(2,1)S(1)}, s16[608,128]{1,0:T(8,128)(2,1)S(1)}) custom-call(f32[4,576,128]{2,1,0:T(8,128)S(1)} %get-tuple-element.29.mine_ref, f32[4,576,128]{2,1,0:T(8,128)S(1)} %collective-permute-done.14.other_ref), custom_call_target="tpu_custom_call" | custom-call | tf_op jit(solution)/shard_map/pallas_call | solution.py:288
  36.6 4.1 %collective-permute-start.15 = (s16[608,128]{1,0:T(8,128)(2,1)S(1)}, s16[608,128]{1,0:T(8,128)(2,1)S(1)}, u32[]{:S(2)}, u32[]{:S(2)}) collective-permute-start(s16[608,128]{1,0:T(8,128)(2,1)S(1)} %get-tuple-element.32), channel_id=1, source_target_pairs={{0,2},{1,3},{2,4},{3,5},{4,6},{5,7},{6,0},{7,1},{8,10},{9,11},{10,... | collective-permute-start | bytes 466952 | tf_op jit(solution)/shard_map/ppermute | solution.py:99
  40.6 0.0 collective-permute-start.16
  40.6 2.5 %collective-permute-start.17 = (s16[608,128]{1,0:T(8,128)(2,1)S(1)}, s16[608,128]{1,0:T(8,128)(2,1)S(1)}, u32[]{:S(2)}, u32[]{:S(2)}) collective-permute-start(s16[608,128]{1,0:T(8,128)(2,1)S(1)} %get-tuple-element.34), channel_id=1, source_target_pairs={{0,6},{1,7},{2,0},{3,1},{4,2},{5,3},{6,4},{7,5},{8,14},{9,15},{10,... | collective-permute-start | bytes 466952 | tf_op jit(solution)/shard_map/ppermute | solution.py:99
  43.1 0.0 collective-permute-done.10.other_ref
  43.1 0.8 %shard_map.58 = (f32[448,128]{1,0:T(8,128)S(1)}, s16[464,128]{1,0:T(8,128)(2,1)S(1)}, s16[464,128]{1,0:T(8,128)(2,1)S(1)}, s16[464,128]{1,0:T(8,128)(2,1)S(1)}) custom-call(f32[4,448,128]{2,1,0:T(8,128)S(1)} %get-tuple-element.23.mine_ref, f32[4,448,128]{2,1,0:T(8,128)S(1)} %collective-permute-done.10.other_ref), custom_call_target="tpu_custom_call" | custom-call | tf_op jit(solution)/shard_map/pallas_call | solution.py:288
  44.0 0.1 collective-permute-start.11
  44.1 1.9 %collective-permute-start.12 = (s16[464,128]{1,0:T(8,128)(2,1)S(1)}, s16[464,128]{1,0:T(8,128)(2,1)S(1)}, u32[]{:S(2)}, u32[]{:S(2)}) collective-permute-start(s16[464,128]{1,0:T(8,128)(2,1)S(1)} %get-tuple-element.27), channel_id=1, source_target_pairs={{0,4},{1,5},{2,6},{3,7},{4,0},{5,1},{6,2},{7,3},{8,12},{9,13},{10,... | collective-permute-start | bytes 356360 | tf_op jit(solution)/shard_map/ppermute | solution.py:99
  46.0 0.0 collective-permute-done.15.a_ref
  46.0 0.7 collective-permute-start.13
  46.7 1.3 %collective-permute-done.16.b_ref = s16[608,128]{1,0:T(8,128)(2,1)S(1)} collective-permute-done((s16[608,128]{1,0:T(8,128)(2,1)S(1)}, s16[608,128]{1,0:T(8,128)(2,1)S(1)}, u32[]{:S(2)}, u32[]{:S(2)}) %collective-permute-start.16) | collective-permute-done | bytes 155680 | tf_op jit(solution)/shard_map/ppermute | solution.py:99
  48.1 0.4 collective-permute-done.17.c_ref
  48.4 0.3 shard_map.60.refs_0_
  48.7 0.0 copy-start
  48.7 1.8 %collective-permute-done.11.a_ref = s16[464,128]{1,0:T(8,128)(2,1)S(1)} collective-permute-done((s16[464,128]{1,0:T(8,128)(2,1)S(1)}, s16[464,128]{1,0:T(8,128)(2,1)S(1)}, u32[]{:S(2)}, u32[]{:S(2)}) %collective-permute-start.11) | collective-permute-done | bytes 118816 | tf_op jit(solution)/shard_map/ppermute | solution.py:99
  50.5 2.6 %collective-permute-done.12.b_ref = s16[464,128]{1,0:T(8,128)(2,1)S(1)} collective-permute-done((s16[464,128]{1,0:T(8,128)(2,1)S(1)}, s16[464,128]{1,0:T(8,128)(2,1)S(1)}, u32[]{:S(2)}, u32[]{:S(2)}) %collective-permute-start.12) | collective-permute-done | bytes 118816 | tf_op jit(solution)/shard_map/ppermute | solution.py:99
  53.2 0.0 collective-permute-done.13.c_ref
  53.2 0.2 shard_map.61
  53.4 14.1 %all_to_all.10.in_ref = s16[16,80,128]{2,1,0:T(8,128)(2,1)S(1)} all-to-all(s16[16,80,128]{2,1,0:T(8,128)(2,1)S(1)} %shard_map.61), channel_id=1, replica_groups=mesh['occ'=16,'vir'=8] {'occ'}, dimensions={0} | all-to-all | bytes 655360 | tf_op jit(solution)/shard_map/all_to_all | solution.py:410
  67.4 0.0 copy-done
  67.4 0.8 shard_map.62
  68.2 13.2 %all_to_all.11.in_ref = s16[8,144,128]{2,1,0:T(8,128)(2,1)S(1)} all-to-all(s16[8,144,128]{2,1,0:T(8,128)(2,1)S(1)} %shard_map.62), channel_id=1, replica_groups=mesh['occ'=16,'vir'=8] {'vir'}, dimensions={0} | all-to-all | bytes 589824 | tf_op jit(solution)/shard_map/all_to_all | solution.py:412
  81.4 0.9 %shard_map.63 = f32[32,4096]{1,0:T(8,128)} custom-call(s16[8,144,128]{2,1,0:T(8,128)(2,1)S(1)} %all_to_all.11.in_ref), custom_call_target="tpu_custom_call" | custom-call | tf_op jit(solution)/shard_map/pallas_call | solution.py:377
  (3 shorter events, 0.1 us)
Async XLA Ops:
  1.0 8.9 %collective-permute-start = (bf16[528,128]{1,0:T(8,128)(2,1)S(1)}, bf16[528,128]{1,0:T(8,128)(2,1)S(1)}, u32[]{:S(2)}, u32[]{:S(2)}) collective-permute-start(bf16[528,128]{1,0:T(8,128)(2,1)S(1)} %shard_map.55.refs_0_), channel_id=1, source_target_pairs={{0,8},{1,33},{2,10},{3,35},{4,12},{5,37},{6,14},{7,39},{8,16},{9,4... | collective-permute-start | bytes 405512 | tf_op jit(solution)/shard_map/ppermute | solution.py:99
  3.1 6.8 %collective-permute-start.2 = (bf16[528,128]{1,0:T(8,128)(2,1)S(1)}, bf16[528,128]{1,0:T(8,128)(2,1)S(1)}, u32[]{:S(2)}, u32[]{:S(2)}) collective-permute-start(bf16[528,128]{1,0:T(8,128)(2,1)S(1)} %shard_map.55.refs_0_), channel_id=1, source_target_pairs={{0,24},{1,97},{2,26},{3,99},{4,28},{5,101},{6,30},{7,103},{8,0},{9... | collective-permute-start | bytes 405512 | tf_op jit(solution)/shard_map/ppermute | solution.py:99
  4.5 7.0 %collective-permute-start.1 = (bf16[528,128]{1,0:T(8,128)(2,1)S(1)}, bf16[528,128]{1,0:T(8,128)(2,1)S(1)}, u32[]{:S(2)}, u32[]{:S(2)}) collective-permute-start(bf16[528,128]{1,0:T(8,128)(2,1)S(1)} %shard_map.55.refs_0_), channel_id=1, source_target_pairs={{0,16},{1,65},{2,18},{3,67},{4,20},{5,69},{6,22},{7,71},{8,24},{9,... | collective-permute-start | bytes 405512 | tf_op jit(solution)/shard_map/ppermute | solution.py:99
  6.1 13.4 %collective-permute-start.7 = (bf16[528,128]{1,0:T(8,128)(2,1)S(1)}, bf16[528,128]{1,0:T(8,128)(2,1)S(1)}, u32[]{:S(2)}, u32[]{:S(2)}) collective-permute-start(bf16[528,128]{1,0:T(8,128)(2,1)S(1)} %shard_map.55.refs_0_), channel_id=1, source_target_pairs={{0,32},{1,9},{2,34},{3,11},{4,36},{5,13},{6,38},{7,15},{8,40},{9,1... | collective-permute-start | bytes 405512 | tf_op jit(solution)/shard_map/ppermute | solution.py:99
  7.8 13.1 %collective-permute-start.9 = (bf16[528,128]{1,0:T(8,128)(2,1)S(1)}, bf16[528,128]{1,0:T(8,128)(2,1)S(1)}, u32[]{:S(2)}, u32[]{:S(2)}) collective-permute-start(bf16[528,128]{1,0:T(8,128)(2,1)S(1)} %shard_map.55.refs_0_), channel_id=1, source_target_pairs={{0,96},{1,25},{2,98},{3,27},{4,100},{5,29},{6,102},{7,31},{8,104},... | collective-permute-start | bytes 405512 | tf_op jit(solution)/shard_map/ppermute | solution.py:99
  9.9 6.5 %collective-permute-start.3 = (bf16[1056,128]{1,0:T(8,128)(2,1)S(1)}, bf16[1056,128]{1,0:T(8,128)(2,1)S(1)}, u32[]{:S(2)}, u32[]{:S(2)}) collective-permute-start(bf16[1056,128]{1,0:T(8,128)(2,1)S(1)} %constant_dynamic-update-slice_fusion), channel_id=1, source_target_pairs={{0,96},{1,25},{2,98},{3,27},{4,100},{5,29},{6,102},{7,31},{8,104},... | collective-permute-start | bytes 811016 | tf_op jit(solution)/shard_map/ppermute | solution.py:99
  11.5 9.4 %collective-permute-start.8 = (bf16[1056,128]{1,0:T(8,128)(2,1)S(1)}, bf16[1056,128]{1,0:T(8,128)(2,1)S(1)}, u32[]{:S(2)}, u32[]{:S(2)}) collective-permute-start(bf16[1056,128]{1,0:T(8,128)(2,1)S(1)} %constant_dynamic-update-slice_fusion), channel_id=1, source_target_pairs={{0,32},{1,9},{2,34},{3,11},{4,36},{5,13},{6,38},{7,15},{8,40},{9,1... | collective-permute-start | bytes 811016 | tf_op jit(solution)/shard_map/ppermute | solution.py:99
  16.4 13.8 %collective-permute-start.4 = (bf16[2112,128]{1,0:T(8,128)(2,1)S(1)}, bf16[2112,128]{1,0:T(8,128)(2,1)S(1)}, u32[]{:S(2)}, u32[]{:S(2)}) collective-permute-start(bf16[2112,128]{1,0:T(8,128)(2,1)S(1)} %pad_maximum_fusion), channel_id=1, source_target_pairs={{0,64},{1,17},{2,66},{3,19},{4,68},{5,21},{6,70},{7,23},{8,72},{9,... | collective-permute-start | bytes 1622024 | tf_op jit(solution)/shard_map/ppermute | solution.py:99
  18.2 12.0 %collective-permute-start.5 = (bf16[528,128]{1,0:T(8,128)(2,1)S(1)}, bf16[528,128]{1,0:T(8,128)(2,1)S(1)}, u32[]{:S(2)}, u32[]{:S(2)}) collective-permute-start(bf16[528,128]{1,0:T(8,128)(2,1)S(1)} %collective-permute-done.1.refs_1_), channel_id=1, source_target_pairs={{0,32},{1,9},{2,34},{3,11},{4,36},{5,13},{6,38},{7,15},{8,40},{9,1... | collective-permute-start | bytes 405512 | tf_op jit(solution)/shard_map/ppermute | solution.py:99
  19.5 10.7 %collective-permute-start.6 = (bf16[528,128]{1,0:T(8,128)(2,1)S(1)}, bf16[528,128]{1,0:T(8,128)(2,1)S(1)}, u32[]{:S(2)}, u32[]{:S(2)}) collective-permute-start(bf16[528,128]{1,0:T(8,128)(2,1)S(1)} %collective-permute-done.1.refs_1_), channel_id=1, source_target_pairs={{0,96},{1,25},{2,98},{3,27},{4,100},{5,29},{6,102},{7,31},{8,104},... | collective-permute-start | bytes 405512 | tf_op jit(solution)/shard_map/ppermute | solution.py:99
  27.0 8.6 %collective-permute-start.14 = (f32[4,576,128]{2,1,0:T(8,128)S(1)}, f32[4,576,128]{2,1,0:T(8,128)S(1)}, u32[]{:S(2)}, u32[]{:S(2)}) collective-permute-start(f32[4,576,128]{2,1,0:T(8,128)S(1)} %get-tuple-element.30), channel_id=1, source_target_pairs={{0,1},{1,0},{2,3},{3,2},{4,5},{5,4},{6,7},{7,6},{8,9},{9,8},{10,11... | collective-permute-start | bytes 3538952 | tf_op jit(solution)/shard_map/ppermute | solution.py:99
  34.9 8.3 %collective-permute-start.10 = (f32[4,448,128]{2,1,0:T(8,128)S(1)}, f32[4,448,128]{2,1,0:T(8,128)S(1)}, u32[]{:S(2)}, u32[]{:S(2)}) collective-permute-start(f32[4,448,128]{2,1,0:T(8,128)S(1)} %get-tuple-element.24), channel_id=1, source_target_pairs={{0,1},{1,0},{2,3},{3,2},{4,5},{5,4},{6,7},{7,6},{8,9},{9,8},{10,11... | collective-permute-start | bytes 2752520 | tf_op jit(solution)/shard_map/ppermute | solution.py:99
  36.6 9.4 %collective-permute-start.15 = (s16[608,128]{1,0:T(8,128)(2,1)S(1)}, s16[608,128]{1,0:T(8,128)(2,1)S(1)}, u32[]{:S(2)}, u32[]{:S(2)}) collective-permute-start(s16[608,128]{1,0:T(8,128)(2,1)S(1)} %get-tuple-element.32), channel_id=1, source_target_pairs={{0,2},{1,3},{2,4},{3,5},{4,6},{5,7},{6,0},{7,1},{8,10},{9,11},{10,... | collective-permute-start | bytes 466952 | tf_op jit(solution)/shard_map/ppermute | solution.py:99
  40.6 7.4 %collective-permute-start.16 = (s16[608,128]{1,0:T(8,128)(2,1)S(1)}, s16[608,128]{1,0:T(8,128)(2,1)S(1)}, u32[]{:S(2)}, u32[]{:S(2)}) collective-permute-start(s16[608,128]{1,0:T(8,128)(2,1)S(1)} %get-tuple-element.33), channel_id=1, source_target_pairs={{0,4},{1,5},{2,6},{3,7},{4,0},{5,1},{6,2},{7,3},{8,12},{9,13},{10,... | collective-permute-start | bytes 466952 | tf_op jit(solution)/shard_map/ppermute | solution.py:99
  40.6 7.8 %collective-permute-start.17 = (s16[608,128]{1,0:T(8,128)(2,1)S(1)}, s16[608,128]{1,0:T(8,128)(2,1)S(1)}, u32[]{:S(2)}, u32[]{:S(2)}) collective-permute-start(s16[608,128]{1,0:T(8,128)(2,1)S(1)} %get-tuple-element.34), channel_id=1, source_target_pairs={{0,6},{1,7},{2,0},{3,1},{4,2},{5,3},{6,4},{7,5},{8,14},{9,15},{10,... | collective-permute-start | bytes 466952 | tf_op jit(solution)/shard_map/ppermute | solution.py:99
  44.0 6.6 %collective-permute-start.11 = (s16[464,128]{1,0:T(8,128)(2,1)S(1)}, s16[464,128]{1,0:T(8,128)(2,1)S(1)}, u32[]{:S(2)}, u32[]{:S(2)}) collective-permute-start(s16[464,128]{1,0:T(8,128)(2,1)S(1)} %get-tuple-element.26), channel_id=1, source_target_pairs={{0,2},{1,3},{2,4},{3,5},{4,6},{5,7},{6,0},{7,1},{8,10},{9,11},{10,... | collective-permute-start | bytes 356360 | tf_op jit(solution)/shard_map/ppermute | solution.py:99
  44.1 9.1 %collective-permute-start.12 = (s16[464,128]{1,0:T(8,128)(2,1)S(1)}, s16[464,128]{1,0:T(8,128)(2,1)S(1)}, u32[]{:S(2)}, u32[]{:S(2)}) collective-permute-start(s16[464,128]{1,0:T(8,128)(2,1)S(1)} %get-tuple-element.27), channel_id=1, source_target_pairs={{0,4},{1,5},{2,6},{3,7},{4,0},{5,1},{6,2},{7,3},{8,12},{9,13},{10,... | collective-permute-start | bytes 356360 | tf_op jit(solution)/shard_map/ppermute | solution.py:99
  46.0 7.2 %collective-permute-start.13 = (s16[464,128]{1,0:T(8,128)(2,1)S(1)}, s16[464,128]{1,0:T(8,128)(2,1)S(1)}, u32[]{:S(2)}, u32[]{:S(2)}) collective-permute-start(s16[464,128]{1,0:T(8,128)(2,1)S(1)} %get-tuple-element.28), channel_id=1, source_target_pairs={{0,6},{1,7},{2,0},{3,1},{4,2},{5,3},{6,4},{7,5},{8,14},{9,15},{10,... | collective-permute-start | bytes 356360 | tf_op jit(solution)/shard_map/ppermute | solution.py:99
  48.7 18.7 %copy-start = (s32[32]{0:T(128)S(1)}, s32[32]{0:T(128)}, u32[]{:S(2)}) copy-start(s32[32]{0:T(128)} %owner_ref.1) | copy-start | bytes 388

commit v5 on v4

--- a/solution.py
+++ b/solution.py
@@ -22,6 +22,7 @@
 HALF = ENTRY // 2
 CHUNK = 256
 SIZES = (64, 128, CHUNK)
+EARLY = 4
 CODE = 32700.0
 TINY = 1e-33
 
@@ -115,6 +116,37 @@
     return shift(value, lambda x, z, y, c: (x, z, y, c + 1))
 
 
+def fetch_kernel(live_hbm, ints_hbm, after_ref, block_ref, live, sem, sems):
+    del after_ref
+    copy = pltpu.make_async_copy(live_hbm, live, sem)
+    copy.start()
+    copy.wait()
+
+    def fetch(i):
+        return pltpu.make_async_copy(ints_hbm.at[i % SLOTS, i // SLOTS], block_ref.at[i], sems.at[i])
+
+    for i in range(EARLY):
+        pl.when(live[i % SLOTS, i // SLOTS] != 0)(functools.partial(lambda i: fetch(i).start(), i))
+    for i in range(EARLY):
+        pl.when(live[i % SLOTS, i // SLOTS] != 0)(functools.partial(lambda i: fetch(i).wait(), i))
+
+
+def fetch_blocks(block_live, integrals, after):
+    return pl.pallas_call(
+        fetch_kernel,
+        out_shape=pltpu.VMEM((TILES * SLOTS, ENTRY, ENTRY), bf16),
+        in_specs=[HBM, HBM, ANY],
+        out_specs=VMEM,
+        scratch_shapes=[
+            pltpu.SMEM(block_live.shape, i32),
+            pltpu.SemaphoreType.DMA,
+            pltpu.SemaphoreType.DMA((EARLY,)),
+        ],
+        compiler_params=params(2),
+        cost_estimate=pl.CostEstimate(flops=0, bytes_accessed=16 << 20, transcendentals=0),
+    )(*in_hbm(block_live, integrals), after)
+
+
 NEAR = (0, 1, 3)
 GROUPS = (
     [(e, d) for e in NEAR for d in NEAR],
@@ -125,7 +157,7 @@
 def compute_kernel(group, sources, fetches, live_hbm, ints_hbm, *refs):
     count_in = max(at for at, _ in sources.values()) + 1
     arrays = refs[:count_in]
-    refs = refs[count_in + (0 if fetches else 1) :]
+    refs = refs[count_in + 1 :]
     theirs_ref, mine_ref, block_ref, left, product, table_v, table, live, count, where, sem, sems = refs
     core = position()[3]
     copy_live = pltpu.make_async_copy(live_hbm, live, sem.at[0])
@@ -149,7 +181,7 @@
 
     copy_live.wait()
     if fetches:
-        for i in range(TILES * SLOTS):
+        for i in range(EARLY, TILES * SLOTS):
             pl.when(live[i % SLOTS, i // SLOTS] != 0)(functools.partial(lambda i: fetch(i).start(), i))
     theirs_ref[...] = jnp.zeros_like(theirs_ref)
     mine_ref[...] = jnp.zeros_like(mine_ref)
@@ -180,7 +212,7 @@
         @pl.when(live[r, c] != 0)
         def _():
             if fetches:
-                fetch(i).wait()
+                pl.when(i >= EARLY)(lambda: fetch(i).wait())
             n = count[c]
 
             def one_chunk(j, inner):
@@ -220,16 +252,16 @@
 
 def compute(which, block_live, integrals, blocks, pieces):
     group = GROUPS[which]
-    fetches = blocks is None
+    fetches = which == 0
     sources = {ab: (i, k * PIECE) for i, (_, held) in enumerate(pieces) for k, ab in enumerate(held)}
     total = pltpu.VMEM((RING, len(group) * SLOTS * ROWS, LANES), f32)
-    more = [] if fetches else in_vmem(blocks)
+    more = in_vmem(blocks)
     return pl.pallas_call(
         functools.partial(compute_kernel, group, sources, fetches),
         out_shape=(total, total, pltpu.VMEM((TILES * SLOTS, ENTRY, ENTRY), bf16)),
         in_specs=[HBM, HBM] + [VMEM] * (len(pieces) + len(more)),
         out_specs=(VMEM,) * 3,
-        input_output_aliases={} if fetches else {2 + len(pieces): 2},
+        input_output_aliases={2 + len(pieces): 2},
         scratch_shapes=[
             pltpu.VMEM((TILES, 2 * CHUNK, ENTRY), bf16),
             pltpu.VMEM((CHUNK, ENTRY), f32),
@@ -270,14 +302,11 @@
     for d in range(1, RING):
         q = lax.rem(y + d, RING)
 
-        def group(g, carry):
-            at = pl.ds(pl.multiple_of(g * ROWS, ROWS), ROWS)
+        for g in range(rows // ROWS):
+            at = pl.ds(g * ROWS, ROWS)
             codes, exponent = encode(mine_ref[q, at, :] + other_ref[q, at, :])
             sends[d - 1][at, :] = codes
-            exps[pl.ds(g, 1), :] = exponent
-            return carry
-
-        lax.fori_loop(0, rows // ROWS, group, 0, unroll=2)
+            exps[g : g + 1, :] = exponent
         sends[d - 1][pl.ds(rows, exps.shape[0]), :] = exps[...].astype(i32).astype(i16)
 
 
@@ -341,13 +370,14 @@
 
 
 def reorder_kernel(owner_ref, in_ref, out_ref, exps):
-    for s in range(BLOCKS * SLOTS):
-        owner, r = divmod(s, SLOTS)
-        p = owner_ref[s]
-        v, t = p // TILES, lax.rem(p, TILES)
-        out_ref[v, pl.ds(pl.multiple_of(t * ROWS, ROWS), ROWS), :] = in_ref[owner, r * ROWS : (r + 1) * ROWS, :]
+    for owner in range(BLOCKS):
         tags = in_ref[owner, SLOTS * ROWS : PART, :].astype(i32).astype(f32)
-        exps[pl.ds(v * META + t, 1), :] = tags[r : r + 1, :]
+        for r in range(SLOTS):
+            p = owner_ref[owner * SLOTS + r]
+            v, t = p // TILES, lax.rem(p, TILES)
+            rows = pl.ds(pl.multiple_of(t * ROWS, ROWS), ROWS)
+            out_ref[v, rows, :] = in_ref[owner, r * ROWS : (r + 1) * ROWS, :]
+            exps[pl.ds(v * META + t, 1), :] = tags[r : r + 1, :]
     for v in range(RANGES):
         out_ref[v, TILES * ROWS : DEST, :] = exps[v * META : (v + 1) * META, :].astype(i32).astype(i16)
 
@@ -389,15 +419,17 @@
     at_once = {a: shift_second(own, a) for a in (1, 3)}
     near = jnp.concatenate([by1, by3], 0)
     nears = {a: shift_second(near, a) for a in (1, 3)}
+    far = shift_first(jnp.concatenate([at_once[1], at_once[3]], 0), 2)
     row = jnp.concatenate([own, by1, by2, by3], 0)
-    row, nears[3] = lax.optimization_barrier((row, nears[3]))
+    blocks = fetch_blocks(block_live, integrals, near)
+    row, blocks = lax.optimization_barrier((row, blocks))
     first = [(own, [(0, 0)]), (by1, [(0, 1)]), (by3, [(0, 3)])]
     for a in (1, 3):
         first += [(at_once[a], [(a, 0)]), (nears[a], [(a, 1), (a, 3)])]
     second = [(shift_second(row, 2), [(2, b) for b in range(RING)]), (by2, [(0, 2)])]
-    second += [(shift_second(by2, a), [(a, 2)]) for a in (1, 3)]
-
-    theirs0, mine0, blocks = compute(0, block_live, integrals, None, first)
+    second += [(far, [(1, 2), (3, 2)])]
+
+    theirs0, mine0, blocks = compute(0, block_live, integrals, blocks, first)
     other0 = shift_core(theirs0)
     theirs1, mine1, _ = compute(1, block_live, integrals, blocks, second)
     other1 = shift_core(theirs1)

time: 82.6 us -> 80.9 us (0.979)
  waiting for transfers between devices: 11.1 us -> 8.63 us
  blocking collectives: 27.3 us -> 25.1 us
  starting transfers between devices: 28 us -> 29.9 us
  Pallas kernels: 15.7 us -> 16.8 us
    pallas_call x0 -> x1, Pallas kernels: none -> 3.6 us  [fetch_blocks(): pl.pallas_call(fetch_kernel, out_shape=pltpu.VMEM((TILES * SLOTS, ENTRY,...]
    all_to_all x1, blocking collectives: 14.1 us -> 11.2 us  [shards(): lax.all_to_all(parts, 'occ', split_axis=0, concat_axis=0, tiled=True)]
    ppermute x18 -> x17, waiting for transfers between devices: 11.1 us -> 8.63 us  [shift(): lax.ppermute(value, ('occ', 'vir'), [(index(*s), index(*place(*s))) for s...]
    ppermute x18 -> x17, starting transfers between devices: 28 us -> 29.9 us  [shift(): lax.ppermute(value, ('occ', 'vir'), [(index(*s), index(*place(*s))) for s...]
    pallas_call x2, Pallas kernels: 10.7 us -> 9.45 us  [compute(): pl.pallas_call(functools.partial(compute_kernel, group, sources, fetches)...]
    pallas_call x2, Pallas kernels: 1.86 us -> 0.61 us  [core_sum(): pl.pallas_call(core_sum_kernel, out_shape=(shape((rows, LANES), f32), cod...]
  transfers between devices with their start and end apart: 18 -> 17, of which waited for: 5 -> 4; matrix products, arithmetic and copies ran while one was open for 0% -> 0% of each run, Pallas kernels for 16% -> 17%
where the time goes in v5:
time: 80.9 us; the launch traced here: 80.6 us
  starting transfers between devices  29.9 us (37%)
  blocking collectives  25.1 us (31%)
  Pallas kernels  16.8 us (21%)
  waiting for transfers between devices  8.63 us (11%)
    ppermute x17, starting transfers between devices, shift(): lax.ppermute(value, ('occ', 'vir'), [(index(*s), index(*place(*s))) for s...  29.9 us
    all_to_all x1, blocking collectives, shards(): lax.all_to_all(parts, 'vir', split_axis=0, concat_axis=0, tiled=True)  13.9 us
    all_to_all x1, blocking collectives, shards(): lax.all_to_all(parts, 'occ', split_axis=0, concat_axis=0, tiled=True)  11.2 us
    pallas_call x2, Pallas kernels, compute(): pl.pallas_call(functools.partial(compute_kernel, group, sources, fetches)...  9.45 us
    ppermute x17, waiting for transfers between devices, shift(): lax.ppermute(value, ('occ', 'vir'), [(index(*s), index(*place(*s))) for s...  8.63 us
    pallas_call x1, Pallas kernels, fetch_blocks(): pl.pallas_call(fetch_kernel, out_shape=pltpu.VMEM((TILES * SLOTS, ENTRY,...  3.6 us
  transfers between devices with their start and end apart: 17, of which 4 were waited for; matrix products, arithmetic and copies ran while one was open for 0% of the time, Pallas kernels for 17%

profile of v5, /device:TPU:1, one launch (start us, length us, event | category | flops | bytes accessed | tf_op | source)
XLA Modules:
  0.0 80.6 jit_solution(11005816620615179620)
XLA Ops:
  0.0 1.0 %shard_map.55.refs_0_ = bf16[528,128]{1,0:T(8,128)(2,1)S(1)} custom-call(s32[1,4]{1,0:T(1,128)} %live_hbm.4, bf16[32,4096]{1,0:T(8,128)(2,1)} %amp_hbm.1), custom_call_target="tpu_custom_call" | custom-call | tf_op jit(solution)/shard_map/pallas_call | solution.py:81
  1.0 2.1 %collective-permute-start = (bf16[528,128]{1,0:T(8,128)(2,1)S(1)}, bf16[528,128]{1,0:T(8,128)(2,1)S(1)}, u32[]{:S(2)}, u32[]{:S(2)}) collective-permute-start(bf16[528,128]{1,0:T(8,128)(2,1)S(1)} %shard_map.55.refs_0_), channel_id=1, source_target_pairs={{0,8},{1,33},{2,10},{3,35},{4,12},{5,37},{6,14},{7,39},{8,16},{9,4... | collective-permute-start | bytes 405512 | tf_op jit(solution)/shard_map/ppermute | solution.py:100
  3.1 1.4 %collective-permute-start.2 = (bf16[528,128]{1,0:T(8,128)(2,1)S(1)}, bf16[528,128]{1,0:T(8,128)(2,1)S(1)}, u32[]{:S(2)}, u32[]{:S(2)}) collective-permute-start(bf16[528,128]{1,0:T(8,128)(2,1)S(1)} %shard_map.55.refs_0_), channel_id=1, source_target_pairs={{0,24},{1,97},{2,26},{3,99},{4,28},{5,101},{6,30},{7,103},{8,0},{9... | collective-permute-start | bytes 405512 | tf_op jit(solution)/shard_map/ppermute | solution.py:100
  4.5 1.6 %collective-permute-start.1 = (bf16[528,128]{1,0:T(8,128)(2,1)S(1)}, bf16[528,128]{1,0:T(8,128)(2,1)S(1)}, u32[]{:S(2)}, u32[]{:S(2)}) collective-permute-start(bf16[528,128]{1,0:T(8,128)(2,1)S(1)} %shard_map.55.refs_0_), channel_id=1, source_target_pairs={{0,16},{1,65},{2,18},{3,67},{4,20},{5,69},{6,22},{7,71},{8,24},{9,... | collective-permute-start | bytes 405512 | tf_op jit(solution)/shard_map/ppermute | solution.py:100
  6.1 1.6 %collective-permute-start.4 = (bf16[528,128]{1,0:T(8,128)(2,1)S(1)}, bf16[528,128]{1,0:T(8,128)(2,1)S(1)}, u32[]{:S(2)}, u32[]{:S(2)}) collective-permute-start(bf16[528,128]{1,0:T(8,128)(2,1)S(1)} %shard_map.55.refs_0_), channel_id=1, source_target_pairs={{0,32},{1,9},{2,34},{3,11},{4,36},{5,13},{6,38},{7,15},{8,40},{9,1... | collective-permute-start | bytes 405512 | tf_op jit(solution)/shard_map/ppermute | solution.py:100
  7.8 2.1 %collective-permute-start.5 = (bf16[528,128]{1,0:T(8,128)(2,1)S(1)}, bf16[528,128]{1,0:T(8,128)(2,1)S(1)}, u32[]{:S(2)}, u32[]{:S(2)}) collective-permute-start(bf16[528,128]{1,0:T(8,128)(2,1)S(1)} %shard_map.55.refs_0_), channel_id=1, source_target_pairs={{0,96},{1,25},{2,98},{3,27},{4,100},{5,29},{6,102},{7,31},{8,104},... | collective-permute-start | bytes 405512 | tf_op jit(solution)/shard_map/ppermute | solution.py:100
  9.9 0.0 collective-permute-done.refs_1_
  9.9 0.0 collective-permute-done.2.refs_2_
  9.9 0.1 collective-permute-start.7
  10.0 2.7 %collective-permute-start.8 = (bf16[1056,128]{1,0:T(8,128)(2,1)S(1)}, bf16[1056,128]{1,0:T(8,128)(2,1)S(1)}, u32[]{:S(2)}, u32[]{:S(2)}) collective-permute-start(bf16[1056,128]{1,0:T(8,128)(2,1)S(1)} %constant_dynamic-update-slice_fusion.after_ref), channel_id=1, source_target_pairs={{0,96},{1,25},{2,98},{3,27},{4,100},{5,29},{6,102},{7,31},{8,104},... | collective-permute-start | bytes 811016 | tf_op jit(solution)/shard_map/ppermute | solution.py:100
  12.7 0.0 collective-permute-done.1.refs_1_
  12.7 3.6 %shard_map.56.refs_7_ = bf16[8,1024,1024]{2,1,0:T(8,128)(2,1)S(1)} custom-call(s32[2,4]{1,0:T(2,128)} %live_hbm.7, bf16[2,4,1024,1024]{3,2,1,0:T(8,128)(2,1)} %ints_hbm.5, bf16[1056,128]{1,0:T(8,128)(2,1)S(1)} %constant_dynamic-update-slice_fusion.after_ref), custom_call_target="tpu_custom_call" | custom-call | bytes 16777216 | tf_op jit(solution)/shard_map/pallas_call | solution.py:135
  16.3 1.6 %collective-permute-start.3 = (bf16[2112,128]{1,0:T(8,128)(2,1)S(1)}, bf16[2112,128]{1,0:T(8,128)(2,1)S(1)}, u32[]{:S(2)}, u32[]{:S(2)}) collective-permute-start(bf16[2112,128]{1,0:T(8,128)(2,1)S(1)} %pad_maximum_fusion), channel_id=1, source_target_pairs={{0,64},{1,17},{2,66},{3,19},{4,68},{5,21},{6,70},{7,23},{8,72},{9,... | collective-permute-start | bytes 1622024 | tf_op jit(solution)/shard_map/ppermute | solution.py:100
  17.9 0.0 collective-permute-done.4.refs_3_
  17.9 0.0 collective-permute-done.5.refs_5_
  17.9 1.6 %collective-permute-start.6 = (bf16[1056,128]{1,0:T(8,128)(2,1)S(1)}, bf16[1056,128]{1,0:T(8,128)(2,1)S(1)}, u32[]{:S(2)}, u32[]{:S(2)}) collective-permute-start(bf16[1056,128]{1,0:T(8,128)(2,1)S(1)} %pad_maximum_fusion.1), channel_id=1, source_target_pairs={{0,16},{1,65},{2,18},{3,67},{4,20},{5,69},{6,22},{7,71},{8,24},{9,... | collective-permute-start | bytes 811016 | tf_op jit(solution)/shard_map/ppermute | solution.py:100
  19.5 0.0 collective-permute-done.7.refs_4_
  19.5 0.0 collective-permute-done.8.refs_6_
  19.5 4.8 %shard_map.57 = (f32[4,576,128]{2,1,0:T(8,128)S(1)}, f32[4,576,128]{2,1,0:T(8,128)S(1)}, bf16[8,1024,1024]{2,1,0:T(8,128)(2,1)S(1)}) custom-call(s32[2,4]{1,0:T(2,128)} %live_hbm.7, bf16[2,4,1024,1024]{3,2,1,0:T(8,128)(2,1)} %ints_hbm.5, bf16[528,128]{1,0:T(8,128)(2,1)S(1)} %shard_map.55.refs_0_, ...), custom_call_target="tpu_custom_call", output_to_operand_aliasing={{2}: (9, {})} | custom-call | flops 4294967296 | bytes 8388608 | tf_op jit(solution)/shard_map/pallas_call | solution.py:259
  24.4 3.8 %collective-permute-start.13 = (f32[4,576,128]{2,1,0:T(8,128)S(1)}, f32[4,576,128]{2,1,0:T(8,128)S(1)}, u32[]{:S(2)}, u32[]{:S(2)}) collective-permute-start(f32[4,576,128]{2,1,0:T(8,128)S(1)} %get-tuple-element.30), channel_id=1, source_target_pairs={{0,1},{1,0},{2,3},{3,2},{4,5},{5,4},{6,7},{7,6},{8,9},{9,8},{10,11... | collective-permute-start | bytes 3538952 | tf_op jit(solution)/shard_map/ppermute | solution.py:100
  28.2 0.0 collective-permute-done.6.refs_2_
  28.2 0.0 collective-permute-done.3.refs_0_
  28.2 4.6 %shard_map.58 = (f32[4,448,128]{2,1,0:T(8,128)S(1)}, f32[4,448,128]{2,1,0:T(8,128)S(1)}, bf16[8,1024,1024]{2,1,0:T(8,128)(2,1)S(1)}) custom-call(s32[2,4]{1,0:T(2,128)} %live_hbm.7, bf16[2,4,1024,1024]{3,2,1,0:T(8,128)(2,1)} %ints_hbm.5, bf16[2112,128]{1,0:T(8,128)(2,1)S(1)} %collective-permute-done.3.refs_0_, ...), custom_call_target="tpu_custom_call", output_to_operand_aliasing={{2}: (5, {})} | custom-call | flops 4294967296 | bytes 8388608 | tf_op jit(solution)/shard_map/pallas_call | solution.py:259
  32.8 3.3 %collective-permute-start.9 = (f32[4,448,128]{2,1,0:T(8,128)S(1)}, f32[4,448,128]{2,1,0:T(8,128)S(1)}, u32[]{:S(2)}, u32[]{:S(2)}) collective-permute-start(f32[4,448,128]{2,1,0:T(8,128)S(1)} %get-tuple-element.24), channel_id=1, source_target_pairs={{0,1},{1,0},{2,3},{3,2},{4,5},{5,4},{6,7},{7,6},{8,9},{9,8},{10,11... | collective-permute-start | bytes 2752520 | tf_op jit(solution)/shard_map/ppermute | solution.py:100
  36.1 0.0 collective-permute-done.13.other_ref
  36.1 0.3 shard_map.60
  36.4 0.1 collective-permute-start.14
  36.5 4.5 %collective-permute-start.15 = (s16[608,128]{1,0:T(8,128)(2,1)S(1)}, s16[608,128]{1,0:T(8,128)(2,1)S(1)}, u32[]{:S(2)}, u32[]{:S(2)}) collective-permute-start(s16[608,128]{1,0:T(8,128)(2,1)S(1)} %get-tuple-element.33), channel_id=1, source_target_pairs={{0,4},{1,5},{2,6},{3,7},{4,0},{5,1},{6,2},{7,3},{8,12},{9,13},{10,... | collective-permute-start | bytes 466952 | tf_op jit(solution)/shard_map/ppermute | solution.py:100
  41.0 1.0 %collective-permute-start.16 = (s16[608,128]{1,0:T(8,128)(2,1)S(1)}, s16[608,128]{1,0:T(8,128)(2,1)S(1)}, u32[]{:S(2)}, u32[]{:S(2)}) collective-permute-start(s16[608,128]{1,0:T(8,128)(2,1)S(1)} %get-tuple-element.34), channel_id=1, source_target_pairs={{0,6},{1,7},{2,0},{3,1},{4,2},{5,3},{6,4},{7,5},{8,14},{9,15},{10,... | collective-permute-start | bytes 466952 | tf_op jit(solution)/shard_map/ppermute | solution.py:100
  41.9 0.0 collective-permute-done.9.other_ref
  42.0 0.3 shard_map.59
  42.2 0.6 collective-permute-start.10
  42.8 0.7 collective-permute-start.11
  43.5 0.7 collective-permute-done.14.a_ref
  44.2 1.3 %collective-permute-start.12 = (s16[464,128]{1,0:T(8,128)(2,1)S(1)}, s16[464,128]{1,0:T(8,128)(2,1)S(1)}, u32[]{:S(2)}, u32[]{:S(2)}) collective-permute-start(s16[464,128]{1,0:T(8,128)(2,1)S(1)} %get-tuple-element.28), channel_id=1, source_target_pairs={{0,6},{1,7},{2,0},{3,1},{4,2},{5,3},{6,4},{7,5},{8,14},{9,15},{10,... | collective-permute-start | bytes 356360 | tf_op jit(solution)/shard_map/ppermute | solution.py:100
  45.4 3.1 %collective-permute-done.15.b_ref = s16[608,128]{1,0:T(8,128)(2,1)S(1)} collective-permute-done((s16[608,128]{1,0:T(8,128)(2,1)S(1)}, s16[608,128]{1,0:T(8,128)(2,1)S(1)}, u32[]{:S(2)}, u32[]{:S(2)}) %collective-permute-start.15) | collective-permute-done | bytes 155680 | tf_op jit(solution)/shard_map/ppermute | solution.py:100
  48.5 0.0 collective-permute-done.16.c_ref
  48.5 0.3 shard_map.61.refs_0_
  48.8 0.0 copy-start
  48.8 2.8 %collective-permute-done.10.a_ref = s16[464,128]{1,0:T(8,128)(2,1)S(1)} collective-permute-done((s16[464,128]{1,0:T(8,128)(2,1)S(1)}, s16[464,128]{1,0:T(8,128)(2,1)S(1)}, u32[]{:S(2)}, u32[]{:S(2)}) %collective-permute-start.10) | collective-permute-done | bytes 118816 | tf_op jit(solution)/shard_map/ppermute | solution.py:100
  51.6 2.0 %collective-permute-done.11.b_ref = s16[464,128]{1,0:T(8,128)(2,1)S(1)} collective-permute-done((s16[464,128]{1,0:T(8,128)(2,1)S(1)}, s16[464,128]{1,0:T(8,128)(2,1)S(1)}, u32[]{:S(2)}, u32[]{:S(2)}) %collective-permute-start.11) | collective-permute-done | bytes 118816 | tf_op jit(solution)/shard_map/ppermute | solution.py:100
  53.6 0.0 collective-permute-done.12.c_ref
  53.6 0.2 shard_map.62
  53.8 11.2 %all_to_all.10.in_ref = s16[16,80,128]{2,1,0:T(8,128)(2,1)S(1)} all-to-all(s16[16,80,128]{2,1,0:T(8,128)(2,1)S(1)} %shard_map.62), channel_id=1, replica_groups=mesh['occ'=16,'vir'=8] {'occ'}, dimensions={0} | all-to-all | bytes 655360 | tf_op jit(solution)/shard_map/all_to_all | solution.py:442
  65.0 0.0 copy-done
  65.0 0.8 shard_map.63
  65.8 13.9 %all_to_all.11.in_ref = s16[8,144,128]{2,1,0:T(8,128)(2,1)S(1)} all-to-all(s16[8,144,128]{2,1,0:T(8,128)(2,1)S(1)} %shard_map.63), channel_id=1, replica_groups=mesh['occ'=16,'vir'=8] {'vir'}, dimensions={0} | all-to-all | bytes 589824 | tf_op jit(solution)/shard_map/all_to_all | solution.py:444
  79.7 0.9 %shard_map.64 = f32[32,4096]{1,0:T(8,128)} custom-call(s16[8,144,128]{2,1,0:T(8,128)(2,1)S(1)} %all_to_all.11.in_ref), custom_call_target="tpu_custom_call" | custom-call | tf_op jit(solution)/shard_map/pallas_call | solution.py:407
  (4 shorter events, 0.1 us)
Async XLA Ops:
  1.0 8.9 %collective-permute-start = (bf16[528,128]{1,0:T(8,128)(2,1)S(1)}, bf16[528,128]{1,0:T(8,128)(2,1)S(1)}, u32[]{:S(2)}, u32[]{:S(2)}) collective-permute-start(bf16[528,128]{1,0:T(8,128)(2,1)S(1)} %shard_map.55.refs_0_), channel_id=1, source_target_pairs={{0,8},{1,33},{2,10},{3,35},{4,12},{5,37},{6,14},{7,39},{8,16},{9,4... | collective-permute-start | bytes 405512 | tf_op jit(solution)/shard_map/ppermute | solution.py:100
  3.1 6.8 %collective-permute-start.2 = (bf16[528,128]{1,0:T(8,128)(2,1)S(1)}, bf16[528,128]{1,0:T(8,128)(2,1)S(1)}, u32[]{:S(2)}, u32[]{:S(2)}) collective-permute-start(bf16[528,128]{1,0:T(8,128)(2,1)S(1)} %shard_map.55.refs_0_), channel_id=1, source_target_pairs={{0,24},{1,97},{2,26},{3,99},{4,28},{5,101},{6,30},{7,103},{8,0},{9... | collective-permute-start | bytes 405512 | tf_op jit(solution)/shard_map/ppermute | solution.py:100
  4.5 8.2 %collective-permute-start.1 = (bf16[528,128]{1,0:T(8,128)(2,1)S(1)}, bf16[528,128]{1,0:T(8,128)(2,1)S(1)}, u32[]{:S(2)}, u32[]{:S(2)}) collective-permute-start(bf16[528,128]{1,0:T(8,128)(2,1)S(1)} %shard_map.55.refs_0_), channel_id=1, source_target_pairs={{0,16},{1,65},{2,18},{3,67},{4,20},{5,69},{6,22},{7,71},{8,24},{9,... | collective-permute-start | bytes 405512 | tf_op jit(solution)/shard_map/ppermute | solution.py:100
  6.1 11.8 %collective-permute-start.4 = (bf16[528,128]{1,0:T(8,128)(2,1)S(1)}, bf16[528,128]{1,0:T(8,128)(2,1)S(1)}, u32[]{:S(2)}, u32[]{:S(2)}) collective-permute-start(bf16[528,128]{1,0:T(8,128)(2,1)S(1)} %shard_map.55.refs_0_), channel_id=1, source_target_pairs={{0,32},{1,9},{2,34},{3,11},{4,36},{5,13},{6,38},{7,15},{8,40},{9,1... | collective-permute-start | bytes 405512 | tf_op jit(solution)/shard_map/ppermute | solution.py:100
  7.8 10.1 %collective-permute-start.5 = (bf16[528,128]{1,0:T(8,128)(2,1)S(1)}, bf16[528,128]{1,0:T(8,128)(2,1)S(1)}, u32[]{:S(2)}, u32[]{:S(2)}) collective-permute-start(bf16[528,128]{1,0:T(8,128)(2,1)S(1)} %shard_map.55.refs_0_), channel_id=1, source_target_pairs={{0,96},{1,25},{2,98},{3,27},{4,100},{5,29},{6,102},{7,31},{8,104},... | collective-permute-start | bytes 405512 | tf_op jit(solution)/shard_map/ppermute | solution.py:100
  9.9 9.6 %collective-permute-start.7 = (bf16[1056,128]{1,0:T(8,128)(2,1)S(1)}, bf16[1056,128]{1,0:T(8,128)(2,1)S(1)}, u32[]{:S(2)}, u32[]{:S(2)}) collective-permute-start(bf16[1056,128]{1,0:T(8,128)(2,1)S(1)} %constant_dynamic-update-slice_fusion.after_ref), channel_id=1, source_target_pairs={{0,32},{1,9},{2,34},{3,11},{4,36},{5,13},{6,38},{7,15},{8,40},{9,1... | collective-permute-start | bytes 811016 | tf_op jit(solution)/shard_map/ppermute | solution.py:100
  10.0 9.5 %collective-permute-start.8 = (bf16[1056,128]{1,0:T(8,128)(2,1)S(1)}, bf16[1056,128]{1,0:T(8,128)(2,1)S(1)}, u32[]{:S(2)}, u32[]{:S(2)}) collective-permute-start(bf16[1056,128]{1,0:T(8,128)(2,1)S(1)} %constant_dynamic-update-slice_fusion.after_ref), channel_id=1, source_target_pairs={{0,96},{1,25},{2,98},{3,27},{4,100},{5,29},{6,102},{7,31},{8,104},... | collective-permute-start | bytes 811016 | tf_op jit(solution)/shard_map/ppermute | solution.py:100
  16.3 11.9 %collective-permute-start.3 = (bf16[2112,128]{1,0:T(8,128)(2,1)S(1)}, bf16[2112,128]{1,0:T(8,128)(2,1)S(1)}, u32[]{:S(2)}, u32[]{:S(2)}) collective-permute-start(bf16[2112,128]{1,0:T(8,128)(2,1)S(1)} %pad_maximum_fusion), channel_id=1, source_target_pairs={{0,64},{1,17},{2,66},{3,19},{4,68},{5,21},{6,70},{7,23},{8,72},{9,... | collective-permute-start | bytes 1622024 | tf_op jit(solution)/shard_map/ppermute | solution.py:100
  17.9 10.3 %collective-permute-start.6 = (bf16[1056,128]{1,0:T(8,128)(2,1)S(1)}, bf16[1056,128]{1,0:T(8,128)(2,1)S(1)}, u32[]{:S(2)}, u32[]{:S(2)}) collective-permute-start(bf16[1056,128]{1,0:T(8,128)(2,1)S(1)} %pad_maximum_fusion.1), channel_id=1, source_target_pairs={{0,16},{1,65},{2,18},{3,67},{4,20},{5,69},{6,22},{7,71},{8,24},{9,... | collective-permute-start | bytes 811016 | tf_op jit(solution)/shard_map/ppermute | solution.py:100
  24.4 11.7 %collective-permute-start.13 = (f32[4,576,128]{2,1,0:T(8,128)S(1)}, f32[4,576,128]{2,1,0:T(8,128)S(1)}, u32[]{:S(2)}, u32[]{:S(2)}) collective-permute-start(f32[4,576,128]{2,1,0:T(8,128)S(1)} %get-tuple-element.30), channel_id=1, source_target_pairs={{0,1},{1,0},{2,3},{3,2},{4,5},{5,4},{6,7},{7,6},{8,9},{9,8},{10,11... | collective-permute-start | bytes 3538952 | tf_op jit(solution)/shard_map/ppermute | solution.py:100
  32.8 9.1 %collective-permute-start.9 = (f32[4,448,128]{2,1,0:T(8,128)S(1)}, f32[4,448,128]{2,1,0:T(8,128)S(1)}, u32[]{:S(2)}, u32[]{:S(2)}) collective-permute-start(f32[4,448,128]{2,1,0:T(8,128)S(1)} %get-tuple-element.24), channel_id=1, source_target_pairs={{0,1},{1,0},{2,3},{3,2},{4,5},{5,4},{6,7},{7,6},{8,9},{9,8},{10,11... | collective-permute-start | bytes 2752520 | tf_op jit(solution)/shard_map/ppermute | solution.py:100
  36.4 7.8 %collective-permute-start.14 = (s16[608,128]{1,0:T(8,128)(2,1)S(1)}, s16[608,128]{1,0:T(8,128)(2,1)S(1)}, u32[]{:S(2)}, u32[]{:S(2)}) collective-permute-start(s16[608,128]{1,0:T(8,128)(2,1)S(1)} %get-tuple-element.32), channel_id=1, source_target_pairs={{0,2},{1,3},{2,4},{3,5},{4,6},{5,7},{6,0},{7,1},{8,10},{9,11},{10,... | collective-permute-start | bytes 466952 | tf_op jit(solution)/shard_map/ppermute | solution.py:100
  36.5 12.0 %collective-permute-start.15 = (s16[608,128]{1,0:T(8,128)(2,1)S(1)}, s16[608,128]{1,0:T(8,128)(2,1)S(1)}, u32[]{:S(2)}, u32[]{:S(2)}) collective-permute-start(s16[608,128]{1,0:T(8,128)(2,1)S(1)} %get-tuple-element.33), channel_id=1, source_target_pairs={{0,4},{1,5},{2,6},{3,7},{4,0},{5,1},{6,2},{7,3},{8,12},{9,13},{10,... | collective-permute-start | bytes 466952 | tf_op jit(solution)/shard_map/ppermute | solution.py:100
  41.0 7.5 %collective-permute-start.16 = (s16[608,128]{1,0:T(8,128)(2,1)S(1)}, s16[608,128]{1,0:T(8,128)(2,1)S(1)}, u32[]{:S(2)}, u32[]{:S(2)}) collective-permute-start(s16[608,128]{1,0:T(8,128)(2,1)S(1)} %get-tuple-element.34), channel_id=1, source_target_pairs={{0,6},{1,7},{2,0},{3,1},{4,2},{5,3},{6,4},{7,5},{8,14},{9,15},{10,... | collective-permute-start | bytes 466952 | tf_op jit(solution)/shard_map/ppermute | solution.py:100
  42.2 9.4 %collective-permute-start.10 = (s16[464,128]{1,0:T(8,128)(2,1)S(1)}, s16[464,128]{1,0:T(8,128)(2,1)S(1)}, u32[]{:S(2)}, u32[]{:S(2)}) collective-permute-start(s16[464,128]{1,0:T(8,128)(2,1)S(1)} %get-tuple-element.26), channel_id=1, source_target_pairs={{0,2},{1,3},{2,4},{3,5},{4,6},{5,7},{6,0},{7,1},{8,10},{9,11},{10,... | collective-permute-start | bytes 356360 | tf_op jit(solution)/shard_map/ppermute | solution.py:100
  42.8 10.8 %collective-permute-start.11 = (s16[464,128]{1,0:T(8,128)(2,1)S(1)}, s16[464,128]{1,0:T(8,128)(2,1)S(1)}, u32[]{:S(2)}, u32[]{:S(2)}) collective-permute-start(s16[464,128]{1,0:T(8,128)(2,1)S(1)} %get-tuple-element.27), channel_id=1, source_target_pairs={{0,4},{1,5},{2,6},{3,7},{4,0},{5,1},{6,2},{7,3},{8,12},{9,13},{10,... | collective-permute-start | bytes 356360 | tf_op jit(solution)/shard_map/ppermute | solution.py:100
  44.2 9.4 %collective-permute-start.12 = (s16[464,128]{1,0:T(8,128)(2,1)S(1)}, s16[464,128]{1,0:T(8,128)(2,1)S(1)}, u32[]{:S(2)}, u32[]{:S(2)}) collective-permute-start(s16[464,128]{1,0:T(8,128)(2,1)S(1)} %get-tuple-element.28), channel_id=1, source_target_pairs={{0,6},{1,7},{2,0},{3,1},{4,2},{5,3},{6,4},{7,5},{8,14},{9,15},{10,... | collective-permute-start | bytes 356360 | tf_op jit(solution)/shard_map/ppermute | solution.py:100
  48.8 16.2 %copy-start = (s32[32]{0:T(128)S(1)}, s32[32]{0:T(128)}, u32[]{:S(2)}) copy-start(s32[32]{0:T(128)} %owner_ref.1) | copy-start | bytes 388

commit v6 on v5

--- a/solution.py
+++ b/solution.py
@@ -22,6 +22,7 @@
 HALF = ENTRY // 2
 CHUNK = 256
 SIZES = (64, 128, CHUNK)
+WIDE = 512
 EARLY = 4
 CODE = 32700.0
 TINY = 1e-33
@@ -116,10 +117,12 @@
     return shift(value, lambda x, z, y, c: (x, z, y, c + 1))
 
 
-def fetch_kernel(live_hbm, ints_hbm, after_ref, block_ref, live, sem, sems):
+def fetch_kernel(live_hbm, ints_hbm, owner_hbm, after_ref, block_ref, owner_ref, live, sem, sems):
     del after_ref
-    copy = pltpu.make_async_copy(live_hbm, live, sem)
+    copy = pltpu.make_async_copy(live_hbm, live, sem.at[0])
     copy.start()
+    copy_owner = pltpu.make_async_copy(owner_hbm, owner_ref, sem.at[1])
+    copy_owner.start()
     copy.wait()
 
     def fetch(i):
@@ -129,22 +132,23 @@
         pl.when(live[i % SLOTS, i // SLOTS] != 0)(functools.partial(lambda i: fetch(i).start(), i))
     for i in range(EARLY):
         pl.when(live[i % SLOTS, i // SLOTS] != 0)(functools.partial(lambda i: fetch(i).wait(), i))
-
-
-def fetch_blocks(block_live, integrals, after):
+    copy_owner.wait()
+
+
+def fetch_blocks(block_live, integrals, row_owner, after):
     return pl.pallas_call(
         fetch_kernel,
-        out_shape=pltpu.VMEM((TILES * SLOTS, ENTRY, ENTRY), bf16),
-        in_specs=[HBM, HBM, ANY],
-        out_specs=VMEM,
+        out_shape=(pltpu.VMEM((TILES * SLOTS, ENTRY, ENTRY), bf16), pltpu.SMEM(row_owner.shape, i32)),
+        in_specs=[HBM, HBM, HBM, ANY],
+        out_specs=(VMEM, SMEM),
         scratch_shapes=[
             pltpu.SMEM(block_live.shape, i32),
-            pltpu.SemaphoreType.DMA,
+            pltpu.SemaphoreType.DMA((2,)),
             pltpu.SemaphoreType.DMA((EARLY,)),
         ],
         compiler_params=params(2),
         cost_estimate=pl.CostEstimate(flops=0, bytes_accessed=16 << 20, transcendentals=0),
-    )(*in_hbm(block_live, integrals), after)
+    )(*in_hbm(block_live, integrals, row_owner), after)
 
 
 NEAR = (0, 1, 3)
@@ -158,7 +162,7 @@
     count_in = max(at for at, _ in sources.values()) + 1
     arrays = refs[:count_in]
     refs = refs[count_in + 1 :]
-    theirs_ref, mine_ref, block_ref, left, product, table_v, table, live, count, where, sem, sems = refs
+    theirs_ref, mine_ref, block_ref, left, table_v, table, live, count, where, sem, sems = refs
     core = position()[3]
     copy_live = pltpu.make_async_copy(live_hbm, live, sem.at[0])
     copy_live.start()
@@ -215,35 +219,27 @@
                 pl.when(i >= EARLY)(lambda: fetch(i).wait())
             n = count[c]
 
-            def one_chunk(j, inner):
-                rest = n - j * (CHUNK // ROWS)
-                start = pl.multiple_of(j * CHUNK, CHUNK)
-
-                def multiply(rows):
-                    product[:rows, :] = jnp.dot(
-                        left[c, pl.ds(start, rows), :], block_ref[i], preferred_element_type=f32
-                    )
-
-                low = 0
-                for rows in SIZES:
-                    tiles = rows // ROWS
-                    pl.when((rest > low) & ((rest <= tiles) | (rows == CHUNK)))(functools.partial(multiply, rows))
-                    low = tiles
-
-                def add(t, last):
-                    o = where[c * BLOCKS + j * (CHUNK // ROWS) + t]
-                    rows = pl.ds(pl.multiple_of(t * ROWS, ROWS), ROWS)
-                    at = pl.ds(pl.multiple_of((o * SLOTS + r) * ROWS, ROWS), ROWS)
-                    for part, ref in enumerate((mine_ref, theirs_ref)):
-                        start = pl.multiple_of(jnp.where(core == 0, part, 1 - part) * HALF, HALF)
-                        for q in range(RING):
-                            ref[q, at, :] += product[rows, pl.ds(start + q * LANES, LANES)]
-                    return last
-
-                lax.fori_loop(0, jnp.minimum(rest, CHUNK // ROWS), add, 0)
-                return inner
-
-            lax.fori_loop(0, pl.cdiv(n * ROWS, CHUNK), one_chunk, 0)
+            def multiply(rows, first):
+                here = left[c, pl.ds(pl.multiple_of(first * ROWS, ROWS), rows), :]
+                for part, ref in enumerate((mine_ref, theirs_ref)):
+                    half = jnp.where(core == 0, part, 1 - part) * HALF
+                    for k in range(HALF // WIDE):
+                        start = pl.multiple_of(half + k * WIDE, WIDE)
+                        product = jnp.dot(here, block_ref[i, :, pl.ds(start, WIDE)], preferred_element_type=f32)
+                        for t in range(rows // ROWS):
+                            valid = first + t < n
+                            o = jnp.where(valid, where[c * BLOCKS + first + t], 0)
+                            at = pl.ds(pl.multiple_of((o * SLOTS + r) * ROWS, ROWS), ROWS)
+                            for m in range(WIDE // LANES):
+                                term = product[t * ROWS : (t + 1) * ROWS, m * LANES : (m + 1) * LANES]
+                                ref[k * (WIDE // LANES) + m, at, :] += jnp.where(valid, term, 0.0)
+
+            low = 0
+            for rows in SIZES:
+                tiles = rows // ROWS
+                pl.when((n > low) & ((n <= tiles) | (rows == CHUNK)))(functools.partial(multiply, rows, 0))
+                low = tiles
+            pl.when(n > low)(functools.partial(multiply, CHUNK, low))
 
         return carry
 
@@ -264,7 +260,6 @@
         input_output_aliases={2 + len(pieces): 2},
         scratch_shapes=[
             pltpu.VMEM((TILES, 2 * CHUNK, ENTRY), bf16),
-            pltpu.VMEM((CHUNK, ENTRY), f32),
             pltpu.VMEM((8, LANES), i32),
             pltpu.SMEM((8, LANES), i32),
             pltpu.SMEM(block_live.shape, i32),
@@ -390,17 +385,25 @@
         out_specs=VMEM,
         scratch_shapes=[pltpu.VMEM((RANGES * META, LANES), f32)],
         compiler_params=params(),
-    )(row_owner, parts)
-
-
-def finish_kernel(in_ref, out_ref):
+    )(pltpu.with_memory_space_constraint(row_owner, pltpu.SMEM), parts)
+
+
+def finish_kernel(in_ref, out_hbm, tiles, scales, sems):
     for v in range(RANGES):
-        y, core = divmod(v, 2)
-        scale = scale_of(in_ref[v, TILES * ROWS : DEST, :].astype(i32).astype(f32))
-        for t in range(TILES):
-            column = t * ENTRY + core * HALF + y * LANES
+        scales[v * META : (v + 1) * META, :] = scale_of(in_ref[v, TILES * ROWS : DEST, :].astype(i32).astype(f32))
+    copies = []
+    for t in range(TILES):
+        for v in range(RANGES):
+            y, core = divmod(v, 2)
+            column = core * HALF + y * LANES
             value = in_ref[v, t * ROWS : (t + 1) * ROWS, :].astype(i32).astype(f32)
-            out_ref[:, column : column + LANES] = value * scale[t : t + 1, :]
+            tiles[t, :, column : column + LANES] = value * scales[v * META + t : v * META + t + 1, :]
+        copies.append(
+            pltpu.make_async_copy(tiles.at[t], out_hbm.at[:, pl.ds(t * ENTRY, ENTRY)], sems.at[t])
+        )
+        copies[-1].start()
+    for copy in copies:
+        copy.wait()
 
 
 def finish(parts):
@@ -408,7 +411,12 @@
         finish_kernel,
         out_shape=shape((ROWS, TILES * ENTRY), f32),
         in_specs=[VMEM],
-        out_specs=VMEM,
+        out_specs=HBM,
+        scratch_shapes=[
+            pltpu.VMEM((TILES, ROWS, ENTRY), f32),
+            pltpu.VMEM((RANGES * META, LANES), f32),
+            pltpu.SemaphoreType.DMA((TILES,)),
+        ],
         compiler_params=params(),
     )(parts)
 
@@ -416,18 +424,16 @@
 def shards(amplitudes, tile_live, integrals, block_live, row_owner):
     own = pack(tile_live, amplitudes)
     by1, by3, by2 = (shift_first(own, b) for b in (1, 3, 2))
-    at_once = {a: shift_second(own, a) for a in (1, 3)}
-    near = jnp.concatenate([by1, by3], 0)
+    near = jnp.concatenate([own, by1, by3], 0)
     nears = {a: shift_second(near, a) for a in (1, 3)}
-    far = shift_first(jnp.concatenate([at_once[1], at_once[3]], 0), 2)
+    first = [(own, [(0, 0)]), (by1, [(0, 1)]), (by3, [(0, 3)])]
+    first += [(nears[a], [(a, b) for b in (0, 1, 3)]) for a in (1, 3)]
     row = jnp.concatenate([own, by1, by2, by3], 0)
-    blocks = fetch_blocks(block_live, integrals, near)
+    blocks, owners = fetch_blocks(block_live, integrals, row_owner, near)
     row, blocks = lax.optimization_barrier((row, blocks))
-    first = [(own, [(0, 0)]), (by1, [(0, 1)]), (by3, [(0, 3)])]
-    for a in (1, 3):
-        first += [(at_once[a], [(a, 0)]), (nears[a], [(a, 1), (a, 3)])]
+    fars = {a: shift_second(by2, a) for a in (1, 3)}
     second = [(shift_second(row, 2), [(2, b) for b in range(RING)]), (by2, [(0, 2)])]
-    second += [(far, [(1, 2), (3, 2)])]
+    second += [(fars[a], [(a, 2)]) for a in (1, 3)]
 
     theirs0, mine0, blocks = compute(0, block_live, integrals, blocks, first)
     other0 = shift_core(theirs0)
@@ -440,7 +446,7 @@
     parts = ring_sum(0, own0, codes0)
     parts = ring_sum(1, own1, codes1, parts)
     parts = lax.all_to_all(parts, "occ", split_axis=0, concat_axis=0, tiled=True)
-    parts = reorder(row_owner, parts)
+    parts = reorder(owners, parts)
     parts = lax.all_to_all(parts, "vir", split_axis=0, concat_axis=0, tiled=True)
     return finish(parts)
 

time: 80.9 us -> 80.1 us (level)
  starting transfers between devices: 29.9 us -> 26.4 us
  blocking collectives: 25.1 us -> 26.6 us
  waiting for transfers between devices: 8.63 us -> 9.73 us
    ppermute x17 -> x16, starting transfers between devices: 29.9 us -> 26.4 us  [shift(): lax.ppermute(value, ('occ', 'vir'), [(index(*s), index(*place(*s))) for s...]
    all_to_all x1, blocking collectives: 11.2 us -> 12.7 us  [shards(): lax.all_to_all(parts, 'occ', split_axis=0, concat_axis=0, tiled=True)]
    ppermute x17 -> x16, waiting for transfers between devices: 8.63 us -> 9.73 us  [shift(): lax.ppermute(value, ('occ', 'vir'), [(index(*s), index(*place(*s))) for s...]
  transfers between devices with their start and end apart: 17 -> 16, of which waited for: 4 -> 7; matrix products, arithmetic and copies ran while one was open for 0% -> 0% of each run, Pallas kernels for 17% -> 19%
where the time goes in v6:
time: 80.1 us
  blocking collectives  26.6 us (33%)
  starting transfers between devices  26.4 us (33%)
  Pallas kernels  17.3 us (22%)
  waiting for transfers between devices  9.73 us (12%)
    ppermute x16, starting transfers between devices, shift(): lax.ppermute(value, ('occ', 'vir'), [(index(*s), index(*place(*s))) for s...  26.4 us
    all_to_all x1, blocking collectives, shards(): lax.all_to_all(parts, 'vir', split_axis=0, concat_axis=0, tiled=True)  13.9 us
    all_to_all x1, blocking collectives, shards(): lax.all_to_all(parts, 'occ', split_axis=0, concat_axis=0, tiled=True)  12.7 us
    pallas_call x2, Pallas kernels, compute(): pl.pallas_call(functools.partial(compute_kernel, group, sources, fetches)...  9.9 us
    ppermute x16, waiting for transfers between devices, shift(): lax.ppermute(value, ('occ', 'vir'), [(index(*s), index(*place(*s))) for s...  9.73 us
    pallas_call x1, Pallas kernels, fetch_blocks(): pl.pallas_call(fetch_kernel, out_shape=(pltpu.VMEM((TILES * SLOTS, ENTRY,...  4.21 us
  transfers between devices with their start and end apart: 16, of which 7 were waited for; matrix products, arithmetic and copies ran while one was open for 0% of the time, Pallas kernels for 19%

profile of v6, /device:TPU:1, one launch (start us, length us, event | category | flops | bytes accessed | tf_op | source)
XLA Modules:
  0.0 80.1 jit_solution(16403647843557778359)
XLA Ops:
  0.0 1.0 %shard_map.55.refs_0_ = bf16[528,128]{1,0:T(8,128)(2,1)S(1)} custom-call(s32[1,4]{1,0:T(1,128)} %live_hbm.4, bf16[32,4096]{1,0:T(8,128)(2,1)} %amp_hbm.1), custom_call_target="tpu_custom_call" | custom-call | tf_op jit(solution)/shard_map/pallas_call | solution.py:82
  1.0 2.1 %collective-permute-start = (bf16[528,128]{1,0:T(8,128)(2,1)S(1)}, bf16[528,128]{1,0:T(8,128)(2,1)S(1)}, u32[]{:S(2)}, u32[]{:S(2)}) collective-permute-start(bf16[528,128]{1,0:T(8,128)(2,1)S(1)} %shard_map.55.refs_0_), channel_id=1, source_target_pairs={{0,8},{1,33},{2,10},{3,35},{4,12},{5,37},{6,14},{7,39},{8,16},{9,4... | collective-permute-start | bytes 405512 | tf_op jit(solution)/shard_map/ppermute | solution.py:101
  3.1 1.4 %collective-permute-start.1 = (bf16[528,128]{1,0:T(8,128)(2,1)S(1)}, bf16[528,128]{1,0:T(8,128)(2,1)S(1)}, u32[]{:S(2)}, u32[]{:S(2)}) collective-permute-start(bf16[528,128]{1,0:T(8,128)(2,1)S(1)} %shard_map.55.refs_0_), channel_id=1, source_target_pairs={{0,24},{1,97},{2,26},{3,99},{4,28},{5,101},{6,30},{7,103},{8,0},{9... | collective-permute-start | bytes 405512 | tf_op jit(solution)/shard_map/ppermute | solution.py:101
  4.5 1.6 %collective-permute-start.2 = (bf16[528,128]{1,0:T(8,128)(2,1)S(1)}, bf16[528,128]{1,0:T(8,128)(2,1)S(1)}, u32[]{:S(2)}, u32[]{:S(2)}) collective-permute-start(bf16[528,128]{1,0:T(8,128)(2,1)S(1)} %shard_map.55.refs_0_), channel_id=1, source_target_pairs={{0,16},{1,65},{2,18},{3,67},{4,20},{5,69},{6,22},{7,71},{8,24},{9,... | collective-permute-start | bytes 405512 | tf_op jit(solution)/shard_map/ppermute | solution.py:101
  6.1 0.7 collective-permute-done.refs_1_
  6.8 0.2 collective-permute-done.1.refs_2_
  7.0 1.9 %collective-permute-start.6 = (bf16[1584,128]{1,0:T(8,128)(2,1)S(1)}, bf16[1584,128]{1,0:T(8,128)(2,1)S(1)}, u32[]{:S(2)}, u32[]{:S(2)}) collective-permute-start(bf16[1584,128]{1,0:T(8,128)(2,1)S(1)} %pad_maximum_fusion.1.after_ref), channel_id=1, source_target_pairs={{0,32},{1,9},{2,34},{3,11},{4,36},{5,13},{6,38},{7,15},{8,40},{9,1... | collective-permute-start | bytes 1216520 | tf_op jit(solution)/shard_map/ppermute | solution.py:101
  8.9 2.3 %collective-permute-start.7 = (bf16[1584,128]{1,0:T(8,128)(2,1)S(1)}, bf16[1584,128]{1,0:T(8,128)(2,1)S(1)}, u32[]{:S(2)}, u32[]{:S(2)}) collective-permute-start(bf16[1584,128]{1,0:T(8,128)(2,1)S(1)} %pad_maximum_fusion.1.after_ref), channel_id=1, source_target_pairs={{0,96},{1,25},{2,98},{3,27},{4,100},{5,29},{6,102},{7,31},{8,104},... | collective-permute-start | bytes 1216520 | tf_op jit(solution)/shard_map/ppermute | solution.py:101
  11.2 4.2 %shard_map.56 = (bf16[8,1024,1024]{2,1,0:T(8,128)(2,1)S(1)}, s32[32]{0:T(128)S(4)}) custom-call(s32[2,4]{1,0:T(2,128)} %live_hbm.7, bf16[2,4,1024,1024]{3,2,1,0:T(8,128)(2,1)} %ints_hbm.5, s32[32]{0:T(128)} %owner_hbm.1, bf16[1584,128]{1,0:T(8,128)(2,1)S(1)} %pad_maximum_fusion.1.after_ref), custom_call_target="tpu_custom_call" | custom-call | bytes 16777216 | tf_op jit(solution)/shard_map/pallas_call | solution.py:139
  15.4 0.0 collective-permute-done.2.refs_1_
  15.5 0.1 collective-permute-start.3
  15.6 0.1 collective-permute-start.4
  15.7 2.7 %collective-permute-start.5 = (bf16[528,128]{1,0:T(8,128)(2,1)S(1)}, bf16[528,128]{1,0:T(8,128)(2,1)S(1)}, u32[]{:S(2)}, u32[]{:S(2)}) collective-permute-start(bf16[528,128]{1,0:T(8,128)(2,1)S(1)} %collective-permute-done.2.refs_1_), channel_id=1, source_target_pairs={{0,96},{1,25},{2,98},{3,27},{4,100},{5,29},{6,102},{7,31},{8,104},... | collective-permute-start | bytes 405512 | tf_op jit(solution)/shard_map/ppermute | solution.py:101
  18.3 0.0 collective-permute-done.6.refs_3_
  18.3 0.0 collective-permute-done.7.refs_4_
  18.3 5.2 %shard_map.57 = (f32[4,576,128]{2,1,0:T(8,128)S(1)}, f32[4,576,128]{2,1,0:T(8,128)S(1)}, bf16[8,1024,1024]{2,1,0:T(8,128)(2,1)S(1)}) custom-call(s32[2,4]{1,0:T(2,128)} %live_hbm.7, bf16[2,4,1024,1024]{3,2,1,0:T(8,128)(2,1)} %ints_hbm.5, bf16[528,128]{1,0:T(8,128)(2,1)S(1)} %shard_map.55.refs_0_, ...), custom_call_target="tpu_custom_call", output_to_operand_aliasing={{2}: (7, {})} | custom-call | flops 4294967296 | bytes 8388608 | tf_op jit(solution)/shard_map/pallas_call | solution.py:255
  23.5 2.9 %collective-permute-start.12 = (f32[4,576,128]{2,1,0:T(8,128)S(1)}, f32[4,576,128]{2,1,0:T(8,128)S(1)}, u32[]{:S(2)}, u32[]{:S(2)}) collective-permute-start(f32[4,576,128]{2,1,0:T(8,128)S(1)} %get-tuple-element.34), channel_id=1, source_target_pairs={{0,1},{1,0},{2,3},{3,2},{4,5},{5,4},{6,7},{7,6},{8,9},{9,8},{10,11... | collective-permute-start | bytes 3538952 | tf_op jit(solution)/shard_map/ppermute | solution.py:101
  26.4 0.4 collective-permute-done.4.refs_2_
  26.8 0.0 collective-permute-done.5.refs_3_
  26.8 0.0 collective-permute-done.3.refs_0_
  26.8 4.7 %shard_map.58 = (f32[4,448,128]{2,1,0:T(8,128)S(1)}, f32[4,448,128]{2,1,0:T(8,128)S(1)}, bf16[8,1024,1024]{2,1,0:T(8,128)(2,1)S(1)}) custom-call(s32[2,4]{1,0:T(2,128)} %live_hbm.7, bf16[2,4,1024,1024]{3,2,1,0:T(8,128)(2,1)} %ints_hbm.5, bf16[2112,128]{1,0:T(8,128)(2,1)S(1)} %collective-permute-done.3.refs_0_, ...), custom_call_target="tpu_custom_call", output_to_operand_aliasing={{2}: (6, {})} | custom-call | flops 4294967296 | bytes 8388608 | tf_op jit(solution)/shard_map/pallas_call | solution.py:255
  31.6 0.8 %collective-permute-start.8 = (f32[4,448,128]{2,1,0:T(8,128)S(1)}, f32[4,448,128]{2,1,0:T(8,128)S(1)}, u32[]{:S(2)}, u32[]{:S(2)}) collective-permute-start(f32[4,448,128]{2,1,0:T(8,128)S(1)} %get-tuple-element.28), channel_id=1, source_target_pairs={{0,1},{1,0},{2,3},{3,2},{4,5},{5,4},{6,7},{7,6},{8,9},{9,8},{10,11... | collective-permute-start | bytes 2752520 | tf_op jit(solution)/shard_map/ppermute | solution.py:101
  32.4 0.0 collective-permute-done.12.other_ref
  32.4 0.3 shard_map.60
  32.8 3.1 %collective-permute-start.13 = (s16[608,128]{1,0:T(8,128)(2,1)S(1)}, s16[608,128]{1,0:T(8,128)(2,1)S(1)}, u32[]{:S(2)}, u32[]{:S(2)}) collective-permute-start(s16[608,128]{1,0:T(8,128)(2,1)S(1)} %get-tuple-element.36), channel_id=1, source_target_pairs={{0,2},{1,3},{2,4},{3,5},{4,6},{5,7},{6,0},{7,1},{8,10},{9,11},{10,... | collective-permute-start | bytes 466952 | tf_op jit(solution)/shard_map/ppermute | solution.py:101
  35.9 3.4 %collective-permute-start.14 = (s16[608,128]{1,0:T(8,128)(2,1)S(1)}, s16[608,128]{1,0:T(8,128)(2,1)S(1)}, u32[]{:S(2)}, u32[]{:S(2)}) collective-permute-start(s16[608,128]{1,0:T(8,128)(2,1)S(1)} %get-tuple-element.37), channel_id=1, source_target_pairs={{0,4},{1,5},{2,6},{3,7},{4,0},{5,1},{6,2},{7,3},{8,12},{9,13},{10,... | collective-permute-start | bytes 466952 | tf_op jit(solution)/shard_map/ppermute | solution.py:101
  39.3 0.0 collective-permute-start.15
  39.3 0.0 collective-permute-done.8.other_ref
  39.3 0.3 shard_map.59
  39.6 1.4 %collective-permute-start.10 = (s16[464,128]{1,0:T(8,128)(2,1)S(1)}, s16[464,128]{1,0:T(8,128)(2,1)S(1)}, u32[]{:S(2)}, u32[]{:S(2)}) collective-permute-start(s16[464,128]{1,0:T(8,128)(2,1)S(1)} %get-tuple-element.31), channel_id=1, source_target_pairs={{0,4},{1,5},{2,6},{3,7},{4,0},{5,1},{6,2},{7,3},{8,12},{9,13},{10,... | collective-permute-start | bytes 356360 | tf_op jit(solution)/shard_map/ppermute | solution.py:101
  41.0 2.6 %collective-permute-start.11 = (s16[464,128]{1,0:T(8,128)(2,1)S(1)}, s16[464,128]{1,0:T(8,128)(2,1)S(1)}, u32[]{:S(2)}, u32[]{:S(2)}) collective-permute-start(s16[464,128]{1,0:T(8,128)(2,1)S(1)} %get-tuple-element.32), channel_id=1, source_target_pairs={{0,6},{1,7},{2,0},{3,1},{4,2},{5,3},{6,4},{7,5},{8,14},{9,15},{10,... | collective-permute-start | bytes 356360 | tf_op jit(solution)/shard_map/ppermute | solution.py:101
  43.5 0.0 collective-permute-done.13.a_ref
  43.6 0.0 collective-permute-start.9
  43.6 3.3 %collective-permute-done.14.b_ref = s16[608,128]{1,0:T(8,128)(2,1)S(1)} collective-permute-done((s16[608,128]{1,0:T(8,128)(2,1)S(1)}, s16[608,128]{1,0:T(8,128)(2,1)S(1)}, u32[]{:S(2)}, u32[]{:S(2)}) %collective-permute-start.14) | collective-permute-done | bytes 155680 | tf_op jit(solution)/shard_map/ppermute | solution.py:101
  46.8 0.0 collective-permute-done.15.c_ref
  46.8 0.3 shard_map.61.refs_0_
  47.1 2.3 %collective-permute-done.10.b_ref = s16[464,128]{1,0:T(8,128)(2,1)S(1)} collective-permute-done((s16[464,128]{1,0:T(8,128)(2,1)S(1)}, s16[464,128]{1,0:T(8,128)(2,1)S(1)}, u32[]{:S(2)}, u32[]{:S(2)}) %collective-permute-start.10) | collective-permute-done | bytes 118816 | tf_op jit(solution)/shard_map/ppermute | solution.py:101
  49.4 2.1 %collective-permute-done.11.c_ref = s16[464,128]{1,0:T(8,128)(2,1)S(1)} collective-permute-done((s16[464,128]{1,0:T(8,128)(2,1)S(1)}, s16[464,128]{1,0:T(8,128)(2,1)S(1)}, u32[]{:S(2)}, u32[]{:S(2)}) %collective-permute-start.11) | collective-permute-done | bytes 118816 | tf_op jit(solution)/shard_map/ppermute | solution.py:101
  51.5 0.7 collective-permute-done.9.a_ref
  52.2 0.2 shard_map.62
  52.4 12.7 %all_to_all.10.in_ref = s16[16,80,128]{2,1,0:T(8,128)(2,1)S(1)} all-to-all(s16[16,80,128]{2,1,0:T(8,128)(2,1)S(1)} %shard_map.62), channel_id=1, replica_groups=mesh['occ'=16,'vir'=8] {'occ'}, dimensions={0} | all-to-all | bytes 655360 | tf_op jit(solution)/shard_map/all_to_all | solution.py:448
  65.1 0.2 shard_map.63
  65.4 13.9 %all_to_all.11.in_ref = s16[8,144,128]{2,1,0:T(8,128)(2,1)S(1)} all-to-all(s16[8,144,128]{2,1,0:T(8,128)(2,1)S(1)} %shard_map.63), channel_id=1, replica_groups=mesh['occ'=16,'vir'=8] {'vir'}, dimensions={0} | all-to-all | bytes 589824 | tf_op jit(solution)/shard_map/all_to_all | solution.py:450
  79.3 0.8 %shard_map.64 = f32[32,4096]{1,0:T(8,128)} custom-call(s16[8,144,128]{2,1,0:T(8,128)(2,1)S(1)} %all_to_all.11.in_ref), custom_call_target="tpu_custom_call" | custom-call | tf_op jit(solution)/shard_map/pallas_call | solution.py:410
  (2 shorter events, 0.1 us)
Async XLA Ops:
  1.0 5.8 %collective-permute-start = (bf16[528,128]{1,0:T(8,128)(2,1)S(1)}, bf16[528,128]{1,0:T(8,128)(2,1)S(1)}, u32[]{:S(2)}, u32[]{:S(2)}) collective-permute-start(bf16[528,128]{1,0:T(8,128)(2,1)S(1)} %shard_map.55.refs_0_), channel_id=1, source_target_pairs={{0,8},{1,33},{2,10},{3,35},{4,12},{5,37},{6,14},{7,39},{8,16},{9,4... | collective-permute-start | bytes 405512 | tf_op jit(solution)/shard_map/ppermute | solution.py:101
  3.1 3.9 %collective-permute-start.1 = (bf16[528,128]{1,0:T(8,128)(2,1)S(1)}, bf16[528,128]{1,0:T(8,128)(2,1)S(1)}, u32[]{:S(2)}, u32[]{:S(2)}) collective-permute-start(bf16[528,128]{1,0:T(8,128)(2,1)S(1)} %shard_map.55.refs_0_), channel_id=1, source_target_pairs={{0,24},{1,97},{2,26},{3,99},{4,28},{5,101},{6,30},{7,103},{8,0},{9... | collective-permute-start | bytes 405512 | tf_op jit(solution)/shard_map/ppermute | solution.py:101
  4.5 11.0 %collective-permute-start.2 = (bf16[528,128]{1,0:T(8,128)(2,1)S(1)}, bf16[528,128]{1,0:T(8,128)(2,1)S(1)}, u32[]{:S(2)}, u32[]{:S(2)}) collective-permute-start(bf16[528,128]{1,0:T(8,128)(2,1)S(1)} %shard_map.55.refs_0_), channel_id=1, source_target_pairs={{0,16},{1,65},{2,18},{3,67},{4,20},{5,69},{6,22},{7,71},{8,24},{9,... | collective-permute-start | bytes 405512 | tf_op jit(solution)/shard_map/ppermute | solution.py:101
  7.0 11.3 %collective-permute-start.6 = (bf16[1584,128]{1,0:T(8,128)(2,1)S(1)}, bf16[1584,128]{1,0:T(8,128)(2,1)S(1)}, u32[]{:S(2)}, u32[]{:S(2)}) collective-permute-start(bf16[1584,128]{1,0:T(8,128)(2,1)S(1)} %pad_maximum_fusion.1.after_ref), channel_id=1, source_target_pairs={{0,32},{1,9},{2,34},{3,11},{4,36},{5,13},{6,38},{7,15},{8,40},{9,1... | collective-permute-start | bytes 1216520 | tf_op jit(solution)/shard_map/ppermute | solution.py:101
  8.9 9.4 %collective-permute-start.7 = (bf16[1584,128]{1,0:T(8,128)(2,1)S(1)}, bf16[1584,128]{1,0:T(8,128)(2,1)S(1)}, u32[]{:S(2)}, u32[]{:S(2)}) collective-permute-start(bf16[1584,128]{1,0:T(8,128)(2,1)S(1)} %pad_maximum_fusion.1.after_ref), channel_id=1, source_target_pairs={{0,96},{1,25},{2,98},{3,27},{4,100},{5,29},{6,102},{7,31},{8,104},... | collective-permute-start | bytes 1216520 | tf_op jit(solution)/shard_map/ppermute | solution.py:101
  15.5 11.3 %collective-permute-start.3 = (bf16[2112,128]{1,0:T(8,128)(2,1)S(1)}, bf16[2112,128]{1,0:T(8,128)(2,1)S(1)}, u32[]{:S(2)}, u32[]{:S(2)}) collective-permute-start(bf16[2112,128]{1,0:T(8,128)(2,1)S(1)} %pad_maximum_fusion), channel_id=1, source_target_pairs={{0,64},{1,17},{2,66},{3,19},{4,68},{5,21},{6,70},{7,23},{8,72},{9,... | collective-permute-start | bytes 1622024 | tf_op jit(solution)/shard_map/ppermute | solution.py:101
  15.6 11.2 %collective-permute-start.4 = (bf16[528,128]{1,0:T(8,128)(2,1)S(1)}, bf16[528,128]{1,0:T(8,128)(2,1)S(1)}, u32[]{:S(2)}, u32[]{:S(2)}) collective-permute-start(bf16[528,128]{1,0:T(8,128)(2,1)S(1)} %collective-permute-done.2.refs_1_), channel_id=1, source_target_pairs={{0,32},{1,9},{2,34},{3,11},{4,36},{5,13},{6,38},{7,15},{8,40},{9,1... | collective-permute-start | bytes 405512 | tf_op jit(solution)/shard_map/ppermute | solution.py:101
  15.7 11.2 %collective-permute-start.5 = (bf16[528,128]{1,0:T(8,128)(2,1)S(1)}, bf16[528,128]{1,0:T(8,128)(2,1)S(1)}, u32[]{:S(2)}, u32[]{:S(2)}) collective-permute-start(bf16[528,128]{1,0:T(8,128)(2,1)S(1)} %collective-permute-done.2.refs_1_), channel_id=1, source_target_pairs={{0,96},{1,25},{2,98},{3,27},{4,100},{5,29},{6,102},{7,31},{8,104},... | collective-permute-start | bytes 405512 | tf_op jit(solution)/shard_map/ppermute | solution.py:101
  23.5 8.9 %collective-permute-start.12 = (f32[4,576,128]{2,1,0:T(8,128)S(1)}, f32[4,576,128]{2,1,0:T(8,128)S(1)}, u32[]{:S(2)}, u32[]{:S(2)}) collective-permute-start(f32[4,576,128]{2,1,0:T(8,128)S(1)} %get-tuple-element.34), channel_id=1, source_target_pairs={{0,1},{1,0},{2,3},{3,2},{4,5},{5,4},{6,7},{7,6},{8,9},{9,8},{10,11... | collective-permute-start | bytes 3538952 | tf_op jit(solution)/shard_map/ppermute | solution.py:101
  31.6 7.7 %collective-permute-start.8 = (f32[4,448,128]{2,1,0:T(8,128)S(1)}, f32[4,448,128]{2,1,0:T(8,128)S(1)}, u32[]{:S(2)}, u32[]{:S(2)}) collective-permute-start(f32[4,448,128]{2,1,0:T(8,128)S(1)} %get-tuple-element.28), channel_id=1, source_target_pairs={{0,1},{1,0},{2,3},{3,2},{4,5},{5,4},{6,7},{7,6},{8,9},{9,8},{10,11... | collective-permute-start | bytes 2752520 | tf_op jit(solution)/shard_map/ppermute | solution.py:101
  32.8 10.8 %collective-permute-start.13 = (s16[608,128]{1,0:T(8,128)(2,1)S(1)}, s16[608,128]{1,0:T(8,128)(2,1)S(1)}, u32[]{:S(2)}, u32[]{:S(2)}) collective-permute-start(s16[608,128]{1,0:T(8,128)(2,1)S(1)} %get-tuple-element.36), channel_id=1, source_target_pairs={{0,2},{1,3},{2,4},{3,5},{4,6},{5,7},{6,0},{7,1},{8,10},{9,11},{10,... | collective-permute-start | bytes 466952 | tf_op jit(solution)/shard_map/ppermute | solution.py:101
  35.9 10.9 %collective-permute-start.14 = (s16[608,128]{1,0:T(8,128)(2,1)S(1)}, s16[608,128]{1,0:T(8,128)(2,1)S(1)}, u32[]{:S(2)}, u32[]{:S(2)}) collective-permute-start(s16[608,128]{1,0:T(8,128)(2,1)S(1)} %get-tuple-element.37), channel_id=1, source_target_pairs={{0,4},{1,5},{2,6},{3,7},{4,0},{5,1},{6,2},{7,3},{8,12},{9,13},{10,... | collective-permute-start | bytes 466952 | tf_op jit(solution)/shard_map/ppermute | solution.py:101
  39.3 7.5 %collective-permute-start.15 = (s16[608,128]{1,0:T(8,128)(2,1)S(1)}, s16[608,128]{1,0:T(8,128)(2,1)S(1)}, u32[]{:S(2)}, u32[]{:S(2)}) collective-permute-start(s16[608,128]{1,0:T(8,128)(2,1)S(1)} %get-tuple-element.38), channel_id=1, source_target_pairs={{0,6},{1,7},{2,0},{3,1},{4,2},{5,3},{6,4},{7,5},{8,14},{9,15},{10,... | collective-permute-start | bytes 466952 | tf_op jit(solution)/shard_map/ppermute | solution.py:101
  39.6 9.8 %collective-permute-start.10 = (s16[464,128]{1,0:T(8,128)(2,1)S(1)}, s16[464,128]{1,0:T(8,128)(2,1)S(1)}, u32[]{:S(2)}, u32[]{:S(2)}) collective-permute-start(s16[464,128]{1,0:T(8,128)(2,1)S(1)} %get-tuple-element.31), channel_id=1, source_target_pairs={{0,4},{1,5},{2,6},{3,7},{4,0},{5,1},{6,2},{7,3},{8,12},{9,13},{10,... | collective-permute-start | bytes 356360 | tf_op jit(solution)/shard_map/ppermute | solution.py:101
  41.0 10.5 %collective-permute-start.11 = (s16[464,128]{1,0:T(8,128)(2,1)S(1)}, s16[464,128]{1,0:T(8,128)(2,1)S(1)}, u32[]{:S(2)}, u32[]{:S(2)}) collective-permute-start(s16[464,128]{1,0:T(8,128)(2,1)S(1)} %get-tuple-element.32), channel_id=1, source_target_pairs={{0,6},{1,7},{2,0},{3,1},{4,2},{5,3},{6,4},{7,5},{8,14},{9,15},{10,... | collective-permute-start | bytes 356360 | tf_op jit(solution)/shard_map/ppermute | solution.py:101
  43.6 8.7 %collective-permute-start.9 = (s16[464,128]{1,0:T(8,128)(2,1)S(1)}, s16[464,128]{1,0:T(8,128)(2,1)S(1)}, u32[]{:S(2)}, u32[]{:S(2)}) collective-permute-start(s16[464,128]{1,0:T(8,128)(2,1)S(1)} %get-tuple-element.30), channel_id=1, source_target_pairs={{0,2},{1,3},{2,4},{3,5},{4,6},{5,7},{6,0},{7,1},{8,10},{9,11},{10,... | collective-permute-start | bytes 356360 | tf_op jit(solution)/shard_map/ppermute | solution.py:101

commit v7 on v6

--- a/solution.py
+++ b/solution.py
@@ -23,7 +23,7 @@
 CHUNK = 256
 SIZES = (64, 128, CHUNK)
 WIDE = 512
-EARLY = 4
+EARLY = 3
 CODE = 32700.0
 TINY = 1e-33
 

time: 80.1 us -> 79.7 us (level)
  Pallas kernels: 17.3 us -> 15.5 us
  blocking collectives: 26.6 us -> 27.7 us
    pallas_call x1, Pallas kernels: 4.21 us -> 2.33 us  [fetch_blocks(): pl.pallas_call(fetch_kernel, out_shape=(pltpu.VMEM((TILES * SLOTS, ENTRY,...]
    all_to_all x1, blocking collectives: 12.7 us -> 14.4 us  [shards(): lax.all_to_all(parts, 'occ', split_axis=0, concat_axis=0, tiled=True)]
  transfers between devices with their start and end apart: 16 -> 16, of which waited for: 7 -> 7; matrix products, arithmetic and copies ran while one was open for 0% -> 0% of each run, Pallas kernels for 19% -> 17%
where the time goes in v7:
time: 79.7 us; the launch traced here: 79.3 us
  blocking collectives  27.7 us (35%)
  starting transfers between devices  26.3 us (33%)
  Pallas kernels  15.5 us (19%)
  waiting for transfers between devices  9.63 us (12%)
    ppermute x16, starting transfers between devices, shift(): lax.ppermute(value, ('occ', 'vir'), [(index(*s), index(*place(*s))) for s...  26.3 us
    all_to_all x1, blocking collectives, shards(): lax.all_to_all(parts, 'occ', split_axis=0, concat_axis=0, tiled=True)  14.4 us
    all_to_all x1, blocking collectives, shards(): lax.all_to_all(parts, 'vir', split_axis=0, concat_axis=0, tiled=True)  13.3 us
    pallas_call x2, Pallas kernels, compute(): pl.pallas_call(functools.partial(compute_kernel, group, sources, fetches)...  10 us
    ppermute x16, waiting for transfers between devices, shift(): lax.ppermute(value, ('occ', 'vir'), [(index(*s), index(*place(*s))) for s...  9.63 us
    pallas_call x1, Pallas kernels, fetch_blocks(): pl.pallas_call(fetch_kernel, out_shape=(pltpu.VMEM((TILES * SLOTS, ENTRY,...  2.33 us
  transfers between devices with their start and end apart: 16, of which 7 were waited for; matrix products, arithmetic and copies ran while one was open for 0% of the time, Pallas kernels for 17%

profile of v7, /device:TPU:1, one launch (start us, length us, event | category | flops | bytes accessed | tf_op | source)
XLA Modules:
  0.0 79.3 jit_solution(2222351090189905533)
XLA Ops:
  0.0 1.0 %shard_map.55.refs_0_ = bf16[528,128]{1,0:T(8,128)(2,1)S(1)} custom-call(s32[1,4]{1,0:T(1,128)} %live_hbm.4, bf16[32,4096]{1,0:T(8,128)(2,1)} %amp_hbm.1), custom_call_target="tpu_custom_call" | custom-call | tf_op jit(solution)/shard_map/pallas_call | solution.py:82
  1.0 2.1 %collective-permute-start = (bf16[528,128]{1,0:T(8,128)(2,1)S(1)}, bf16[528,128]{1,0:T(8,128)(2,1)S(1)}, u32[]{:S(2)}, u32[]{:S(2)}) collective-permute-start(bf16[528,128]{1,0:T(8,128)(2,1)S(1)} %shard_map.55.refs_0_), channel_id=1, source_target_pairs={{0,8},{1,33},{2,10},{3,35},{4,12},{5,37},{6,14},{7,39},{8,16},{9,4... | collective-permute-start | bytes 405512 | tf_op jit(solution)/shard_map/ppermute | solution.py:101
  3.1 1.4 %collective-permute-start.1 = (bf16[528,128]{1,0:T(8,128)(2,1)S(1)}, bf16[528,128]{1,0:T(8,128)(2,1)S(1)}, u32[]{:S(2)}, u32[]{:S(2)}) collective-permute-start(bf16[528,128]{1,0:T(8,128)(2,1)S(1)} %shard_map.55.refs_0_), channel_id=1, source_target_pairs={{0,24},{1,97},{2,26},{3,99},{4,28},{5,101},{6,30},{7,103},{8,0},{9... | collective-permute-start | bytes 405512 | tf_op jit(solution)/shard_map/ppermute | solution.py:101
  4.5 1.6 %collective-permute-start.2 = (bf16[528,128]{1,0:T(8,128)(2,1)S(1)}, bf16[528,128]{1,0:T(8,128)(2,1)S(1)}, u32[]{:S(2)}, u32[]{:S(2)}) collective-permute-start(bf16[528,128]{1,0:T(8,128)(2,1)S(1)} %shard_map.55.refs_0_), channel_id=1, source_target_pairs={{0,16},{1,65},{2,18},{3,67},{4,20},{5,69},{6,22},{7,71},{8,24},{9,... | collective-permute-start | bytes 405512 | tf_op jit(solution)/shard_map/ppermute | solution.py:101
  6.1 0.7 collective-permute-done.refs_1_
  6.8 0.2 collective-permute-done.1.refs_2_
  7.0 1.9 %collective-permute-start.6 = (bf16[1584,128]{1,0:T(8,128)(2,1)S(1)}, bf16[1584,128]{1,0:T(8,128)(2,1)S(1)}, u32[]{:S(2)}, u32[]{:S(2)}) collective-permute-start(bf16[1584,128]{1,0:T(8,128)(2,1)S(1)} %pad_maximum_fusion.1.after_ref), channel_id=1, source_target_pairs={{0,32},{1,9},{2,34},{3,11},{4,36},{5,13},{6,38},{7,15},{8,40},{9,1... | collective-permute-start | bytes 1216520 | tf_op jit(solution)/shard_map/ppermute | solution.py:101
  8.9 2.3 %collective-permute-start.7 = (bf16[1584,128]{1,0:T(8,128)(2,1)S(1)}, bf16[1584,128]{1,0:T(8,128)(2,1)S(1)}, u32[]{:S(2)}, u32[]{:S(2)}) collective-permute-start(bf16[1584,128]{1,0:T(8,128)(2,1)S(1)} %pad_maximum_fusion.1.after_ref), channel_id=1, source_target_pairs={{0,96},{1,25},{2,98},{3,27},{4,100},{5,29},{6,102},{7,31},{8,104},... | collective-permute-start | bytes 1216520 | tf_op jit(solution)/shard_map/ppermute | solution.py:101
  11.2 2.3 %shard_map.56 = (bf16[8,1024,1024]{2,1,0:T(8,128)(2,1)S(1)}, s32[32]{0:T(128)S(4)}) custom-call(s32[2,4]{1,0:T(2,128)} %live_hbm.7, bf16[2,4,1024,1024]{3,2,1,0:T(8,128)(2,1)} %ints_hbm.5, s32[32]{0:T(128)} %owner_hbm.1, bf16[1584,128]{1,0:T(8,128)(2,1)S(1)} %pad_maximum_fusion.1.after_ref), custom_call_target="tpu_custom_call" | custom-call | bytes 16777216 | tf_op jit(solution)/shard_map/pallas_call | solution.py:139
  13.6 0.0 collective-permute-done.2.refs_1_
  13.6 1.9 %collective-permute-start.3 = (bf16[2112,128]{1,0:T(8,128)(2,1)S(1)}, bf16[2112,128]{1,0:T(8,128)(2,1)S(1)}, u32[]{:S(2)}, u32[]{:S(2)}) collective-permute-start(bf16[2112,128]{1,0:T(8,128)(2,1)S(1)} %pad_maximum_fusion), channel_id=1, source_target_pairs={{0,64},{1,17},{2,66},{3,19},{4,68},{5,21},{6,70},{7,23},{8,72},{9,... | collective-permute-start | bytes 1622024 | tf_op jit(solution)/shard_map/ppermute | solution.py:101
  15.5 0.8 %collective-permute-start.4 = (bf16[528,128]{1,0:T(8,128)(2,1)S(1)}, bf16[528,128]{1,0:T(8,128)(2,1)S(1)}, u32[]{:S(2)}, u32[]{:S(2)}) collective-permute-start(bf16[528,128]{1,0:T(8,128)(2,1)S(1)} %collective-permute-done.2.refs_1_), channel_id=1, source_target_pairs={{0,32},{1,9},{2,34},{3,11},{4,36},{5,13},{6,38},{7,15},{8,40},{9,1... | collective-permute-start | bytes 405512 | tf_op jit(solution)/shard_map/ppermute | solution.py:101
  16.3 1.9 %collective-permute-start.5 = (bf16[528,128]{1,0:T(8,128)(2,1)S(1)}, bf16[528,128]{1,0:T(8,128)(2,1)S(1)}, u32[]{:S(2)}, u32[]{:S(2)}) collective-permute-start(bf16[528,128]{1,0:T(8,128)(2,1)S(1)} %collective-permute-done.2.refs_1_), channel_id=1, source_target_pairs={{0,96},{1,25},{2,98},{3,27},{4,100},{5,29},{6,102},{7,31},{8,104},... | collective-permute-start | bytes 405512 | tf_op jit(solution)/shard_map/ppermute | solution.py:101
  18.1 0.0 collective-permute-done.6.refs_3_
  18.2 0.0 collective-permute-done.7.refs_4_
  18.2 5.7 %shard_map.57 = (f32[4,576,128]{2,1,0:T(8,128)S(1)}, f32[4,576,128]{2,1,0:T(8,128)S(1)}, bf16[8,1024,1024]{2,1,0:T(8,128)(2,1)S(1)}) custom-call(s32[2,4]{1,0:T(2,128)} %live_hbm.7, bf16[2,4,1024,1024]{3,2,1,0:T(8,128)(2,1)} %ints_hbm.5, bf16[528,128]{1,0:T(8,128)(2,1)S(1)} %shard_map.55.refs_0_, ...), custom_call_target="tpu_custom_call", output_to_operand_aliasing={{2}: (7, {})} | custom-call | flops 4294967296 | bytes 8388608 | tf_op jit(solution)/shard_map/pallas_call | solution.py:255
  23.9 3.3 %collective-permute-start.12 = (f32[4,576,128]{2,1,0:T(8,128)S(1)}, f32[4,576,128]{2,1,0:T(8,128)S(1)}, u32[]{:S(2)}, u32[]{:S(2)}) collective-permute-start(f32[4,576,128]{2,1,0:T(8,128)S(1)} %get-tuple-element.34), channel_id=1, source_target_pairs={{0,1},{1,0},{2,3},{3,2},{4,5},{5,4},{6,7},{7,6},{8,9},{9,8},{10,11... | collective-permute-start | bytes 3538952 | tf_op jit(solution)/shard_map/ppermute | solution.py:101
  27.3 0.0 collective-permute-done.4.refs_2_
  27.3 0.0 collective-permute-done.5.refs_3_
  27.3 0.0 collective-permute-done.3.refs_0_
  27.3 4.3 %shard_map.58 = (f32[4,448,128]{2,1,0:T(8,128)S(1)}, f32[4,448,128]{2,1,0:T(8,128)S(1)}, bf16[8,1024,1024]{2,1,0:T(8,128)(2,1)S(1)}) custom-call(s32[2,4]{1,0:T(2,128)} %live_hbm.7, bf16[2,4,1024,1024]{3,2,1,0:T(8,128)(2,1)} %ints_hbm.5, bf16[2112,128]{1,0:T(8,128)(2,1)S(1)} %collective-permute-done.3.refs_0_, ...), custom_call_target="tpu_custom_call", output_to_operand_aliasing={{2}: (6, {})} | custom-call | flops 4294967296 | bytes 8388608 | tf_op jit(solution)/shard_map/pallas_call | solution.py:255
  31.6 2.8 %collective-permute-start.8 = (f32[4,448,128]{2,1,0:T(8,128)S(1)}, f32[4,448,128]{2,1,0:T(8,128)S(1)}, u32[]{:S(2)}, u32[]{:S(2)}) collective-permute-start(f32[4,448,128]{2,1,0:T(8,128)S(1)} %get-tuple-element.28), channel_id=1, source_target_pairs={{0,1},{1,0},{2,3},{3,2},{4,5},{5,4},{6,7},{7,6},{8,9},{9,8},{10,11... | collective-permute-start | bytes 2752520 | tf_op jit(solution)/shard_map/ppermute | solution.py:101
  34.4 0.0 collective-permute-done.12.other_ref
  34.4 0.3 shard_map.60
  34.7 0.9 %collective-permute-start.13 = (s16[608,128]{1,0:T(8,128)(2,1)S(1)}, s16[608,128]{1,0:T(8,128)(2,1)S(1)}, u32[]{:S(2)}, u32[]{:S(2)}) collective-permute-start(s16[608,128]{1,0:T(8,128)(2,1)S(1)} %get-tuple-element.36), channel_id=1, source_target_pairs={{0,2},{1,3},{2,4},{3,5},{4,6},{5,7},{6,0},{7,1},{8,10},{9,11},{10,... | collective-permute-start | bytes 466952 | tf_op jit(solution)/shard_map/ppermute | solution.py:101
  35.6 1.5 %collective-permute-start.14 = (s16[608,128]{1,0:T(8,128)(2,1)S(1)}, s16[608,128]{1,0:T(8,128)(2,1)S(1)}, u32[]{:S(2)}, u32[]{:S(2)}) collective-permute-start(s16[608,128]{1,0:T(8,128)(2,1)S(1)} %get-tuple-element.37), channel_id=1, source_target_pairs={{0,4},{1,5},{2,6},{3,7},{4,0},{5,1},{6,2},{7,3},{8,12},{9,13},{10,... | collective-permute-start | bytes 466952 | tf_op jit(solution)/shard_map/ppermute | solution.py:101
  37.1 2.0 %collective-permute-start.15 = (s16[608,128]{1,0:T(8,128)(2,1)S(1)}, s16[608,128]{1,0:T(8,128)(2,1)S(1)}, u32[]{:S(2)}, u32[]{:S(2)}) collective-permute-start(s16[608,128]{1,0:T(8,128)(2,1)S(1)} %get-tuple-element.38), channel_id=1, source_target_pairs={{0,6},{1,7},{2,0},{3,1},{4,2},{5,3},{6,4},{7,5},{8,14},{9,15},{10,... | collective-permute-start | bytes 466952 | tf_op jit(solution)/shard_map/ppermute | solution.py:101
  39.1 0.0 collective-permute-done.8.other_ref
  39.1 0.3 shard_map.59
  39.4 0.8 %collective-permute-start.10 = (s16[464,128]{1,0:T(8,128)(2,1)S(1)}, s16[464,128]{1,0:T(8,128)(2,1)S(1)}, u32[]{:S(2)}, u32[]{:S(2)}) collective-permute-start(s16[464,128]{1,0:T(8,128)(2,1)S(1)} %get-tuple-element.31), channel_id=1, source_target_pairs={{0,4},{1,5},{2,6},{3,7},{4,0},{5,1},{6,2},{7,3},{8,12},{9,13},{10,... | collective-permute-start | bytes 356360 | tf_op jit(solution)/shard_map/ppermute | solution.py:101
  40.2 1.1 %collective-permute-start.11 = (s16[464,128]{1,0:T(8,128)(2,1)S(1)}, s16[464,128]{1,0:T(8,128)(2,1)S(1)}, u32[]{:S(2)}, u32[]{:S(2)}) collective-permute-start(s16[464,128]{1,0:T(8,128)(2,1)S(1)} %get-tuple-element.32), channel_id=1, source_target_pairs={{0,6},{1,7},{2,0},{3,1},{4,2},{5,3},{6,4},{7,5},{8,14},{9,15},{10,... | collective-permute-start | bytes 356360 | tf_op jit(solution)/shard_map/ppermute | solution.py:101
  41.3 0.5 collective-permute-done.13.a_ref
  41.8 0.0 collective-permute-start.9
  41.8 2.9 %collective-permute-done.14.b_ref = s16[608,128]{1,0:T(8,128)(2,1)S(1)} collective-permute-done((s16[608,128]{1,0:T(8,128)(2,1)S(1)}, s16[608,128]{1,0:T(8,128)(2,1)S(1)}, u32[]{:S(2)}, u32[]{:S(2)}) %collective-permute-start.14) | collective-permute-done | bytes 155680 | tf_op jit(solution)/shard_map/ppermute | solution.py:101
  44.8 0.4 collective-permute-done.15.c_ref
  45.2 0.3 shard_map.61.refs_0_
  45.5 1.8 %collective-permute-done.10.b_ref = s16[464,128]{1,0:T(8,128)(2,1)S(1)} collective-permute-done((s16[464,128]{1,0:T(8,128)(2,1)S(1)}, s16[464,128]{1,0:T(8,128)(2,1)S(1)}, u32[]{:S(2)}, u32[]{:S(2)}) %collective-permute-start.10) | collective-permute-done | bytes 118816 | tf_op jit(solution)/shard_map/ppermute | solution.py:101
  47.3 3.0 %collective-permute-done.11.c_ref = s16[464,128]{1,0:T(8,128)(2,1)S(1)} collective-permute-done((s16[464,128]{1,0:T(8,128)(2,1)S(1)}, s16[464,128]{1,0:T(8,128)(2,1)S(1)}, u32[]{:S(2)}, u32[]{:S(2)}) %collective-permute-start.11) | collective-permute-done | bytes 118816 | tf_op jit(solution)/shard_map/ppermute | solution.py:101
  50.3 0.0 collective-permute-done.9.a_ref
  50.3 0.2 shard_map.62
  50.5 14.4 %all_to_all.10.in_ref = s16[16,80,128]{2,1,0:T(8,128)(2,1)S(1)} all-to-all(s16[16,80,128]{2,1,0:T(8,128)(2,1)S(1)} %shard_map.62), channel_id=1, replica_groups=mesh['occ'=16,'vir'=8] {'occ'}, dimensions={0} | all-to-all | bytes 655360 | tf_op jit(solution)/shard_map/all_to_all | solution.py:448
  64.9 0.2 shard_map.63
  65.1 13.3 %all_to_all.11.in_ref = s16[8,144,128]{2,1,0:T(8,128)(2,1)S(1)} all-to-all(s16[8,144,128]{2,1,0:T(8,128)(2,1)S(1)} %shard_map.63), channel_id=1, replica_groups=mesh['occ'=16,'vir'=8] {'vir'}, dimensions={0} | all-to-all | bytes 589824 | tf_op jit(solution)/shard_map/all_to_all | solution.py:450
  78.5 0.8 %shard_map.64 = f32[32,4096]{1,0:T(8,128)} custom-call(s16[8,144,128]{2,1,0:T(8,128)(2,1)S(1)} %all_to_all.11.in_ref), custom_call_target="tpu_custom_call" | custom-call | tf_op jit(solution)/shard_map/pallas_call | solution.py:410
  (2 shorter events, 0.1 us)
Async XLA Ops:
  1.0 5.8 %collective-permute-start = (bf16[528,128]{1,0:T(8,128)(2,1)S(1)}, bf16[528,128]{1,0:T(8,128)(2,1)S(1)}, u32[]{:S(2)}, u32[]{:S(2)}) collective-permute-start(bf16[528,128]{1,0:T(8,128)(2,1)S(1)} %shard_map.55.refs_0_), channel_id=1, source_target_pairs={{0,8},{1,33},{2,10},{3,35},{4,12},{5,37},{6,14},{7,39},{8,16},{9,4... | collective-permute-start | bytes 405512 | tf_op jit(solution)/shard_map/ppermute | solution.py:101
  3.1 3.9 %collective-permute-start.1 = (bf16[528,128]{1,0:T(8,128)(2,1)S(1)}, bf16[528,128]{1,0:T(8,128)(2,1)S(1)}, u32[]{:S(2)}, u32[]{:S(2)}) collective-permute-start(bf16[528,128]{1,0:T(8,128)(2,1)S(1)} %shard_map.55.refs_0_), channel_id=1, source_target_pairs={{0,24},{1,97},{2,26},{3,99},{4,28},{5,101},{6,30},{7,103},{8,0},{9... | collective-permute-start | bytes 405512 | tf_op jit(solution)/shard_map/ppermute | solution.py:101
  4.5 9.1 %collective-permute-start.2 = (bf16[528,128]{1,0:T(8,128)(2,1)S(1)}, bf16[528,128]{1,0:T(8,128)(2,1)S(1)}, u32[]{:S(2)}, u32[]{:S(2)}) collective-permute-start(bf16[528,128]{1,0:T(8,128)(2,1)S(1)} %shard_map.55.refs_0_), channel_id=1, source_target_pairs={{0,16},{1,65},{2,18},{3,67},{4,20},{5,69},{6,22},{7,71},{8,24},{9,... | collective-permute-start | bytes 405512 | tf_op jit(solution)/shard_map/ppermute | solution.py:101
  7.0 11.1 %collective-permute-start.6 = (bf16[1584,128]{1,0:T(8,128)(2,1)S(1)}, bf16[1584,128]{1,0:T(8,128)(2,1)S(1)}, u32[]{:S(2)}, u32[]{:S(2)}) collective-permute-start(bf16[1584,128]{1,0:T(8,128)(2,1)S(1)} %pad_maximum_fusion.1.after_ref), channel_id=1, source_target_pairs={{0,32},{1,9},{2,34},{3,11},{4,36},{5,13},{6,38},{7,15},{8,40},{9,1... | collective-permute-start | bytes 1216520 | tf_op jit(solution)/shard_map/ppermute | solution.py:101
  8.9 9.2 %collective-permute-start.7 = (bf16[1584,128]{1,0:T(8,128)(2,1)S(1)}, bf16[1584,128]{1,0:T(8,128)(2,1)S(1)}, u32[]{:S(2)}, u32[]{:S(2)}) collective-permute-start(bf16[1584,128]{1,0:T(8,128)(2,1)S(1)} %pad_maximum_fusion.1.after_ref), channel_id=1, source_target_pairs={{0,96},{1,25},{2,98},{3,27},{4,100},{5,29},{6,102},{7,31},{8,104},... | collective-permute-start | bytes 1216520 | tf_op jit(solution)/shard_map/ppermute | solution.py:101
  13.6 13.7 %collective-permute-start.3 = (bf16[2112,128]{1,0:T(8,128)(2,1)S(1)}, bf16[2112,128]{1,0:T(8,128)(2,1)S(1)}, u32[]{:S(2)}, u32[]{:S(2)}) collective-permute-start(bf16[2112,128]{1,0:T(8,128)(2,1)S(1)} %pad_maximum_fusion), channel_id=1, source_target_pairs={{0,64},{1,17},{2,66},{3,19},{4,68},{5,21},{6,70},{7,23},{8,72},{9,... | collective-permute-start | bytes 1622024 | tf_op jit(solution)/shard_map/ppermute | solution.py:101
  15.5 11.8 %collective-permute-start.4 = (bf16[528,128]{1,0:T(8,128)(2,1)S(1)}, bf16[528,128]{1,0:T(8,128)(2,1)S(1)}, u32[]{:S(2)}, u32[]{:S(2)}) collective-permute-start(bf16[528,128]{1,0:T(8,128)(2,1)S(1)} %collective-permute-done.2.refs_1_), channel_id=1, source_target_pairs={{0,32},{1,9},{2,34},{3,11},{4,36},{5,13},{6,38},{7,15},{8,40},{9,1... | collective-permute-start | bytes 405512 | tf_op jit(solution)/shard_map/ppermute | solution.py:101
  16.3 11.0 %collective-permute-start.5 = (bf16[528,128]{1,0:T(8,128)(2,1)S(1)}, bf16[528,128]{1,0:T(8,128)(2,1)S(1)}, u32[]{:S(2)}, u32[]{:S(2)}) collective-permute-start(bf16[528,128]{1,0:T(8,128)(2,1)S(1)} %collective-permute-done.2.refs_1_), channel_id=1, source_target_pairs={{0,96},{1,25},{2,98},{3,27},{4,100},{5,29},{6,102},{7,31},{8,104},... | collective-permute-start | bytes 405512 | tf_op jit(solution)/shard_map/ppermute | solution.py:101
  23.9 10.5 %collective-permute-start.12 = (f32[4,576,128]{2,1,0:T(8,128)S(1)}, f32[4,576,128]{2,1,0:T(8,128)S(1)}, u32[]{:S(2)}, u32[]{:S(2)}) collective-permute-start(f32[4,576,128]{2,1,0:T(8,128)S(1)} %get-tuple-element.34), channel_id=1, source_target_pairs={{0,1},{1,0},{2,3},{3,2},{4,5},{5,4},{6,7},{7,6},{8,9},{9,8},{10,11... | collective-permute-start | bytes 3538952 | tf_op jit(solution)/shard_map/ppermute | solution.py:101
  31.6 7.5 %collective-permute-start.8 = (f32[4,448,128]{2,1,0:T(8,128)S(1)}, f32[4,448,128]{2,1,0:T(8,128)S(1)}, u32[]{:S(2)}, u32[]{:S(2)}) collective-permute-start(f32[4,448,128]{2,1,0:T(8,128)S(1)} %get-tuple-element.28), channel_id=1, source_target_pairs={{0,1},{1,0},{2,3},{3,2},{4,5},{5,4},{6,7},{7,6},{8,9},{9,8},{10,11... | collective-permute-start | bytes 2752520 | tf_op jit(solution)/shard_map/ppermute | solution.py:101
  34.7 7.1 %collective-permute-start.13 = (s16[608,128]{1,0:T(8,128)(2,1)S(1)}, s16[608,128]{1,0:T(8,128)(2,1)S(1)}, u32[]{:S(2)}, u32[]{:S(2)}) collective-permute-start(s16[608,128]{1,0:T(8,128)(2,1)S(1)} %get-tuple-element.36), channel_id=1, source_target_pairs={{0,2},{1,3},{2,4},{3,5},{4,6},{5,7},{6,0},{7,1},{8,10},{9,11},{10,... | collective-permute-start | bytes 466952 | tf_op jit(solution)/shard_map/ppermute | solution.py:101
  35.6 9.2 %collective-permute-start.14 = (s16[608,128]{1,0:T(8,128)(2,1)S(1)}, s16[608,128]{1,0:T(8,128)(2,1)S(1)}, u32[]{:S(2)}, u32[]{:S(2)}) collective-permute-start(s16[608,128]{1,0:T(8,128)(2,1)S(1)} %get-tuple-element.37), channel_id=1, source_target_pairs={{0,4},{1,5},{2,6},{3,7},{4,0},{5,1},{6,2},{7,3},{8,12},{9,13},{10,... | collective-permute-start | bytes 466952 | tf_op jit(solution)/shard_map/ppermute | solution.py:101
  37.1 8.1 %collective-permute-start.15 = (s16[608,128]{1,0:T(8,128)(2,1)S(1)}, s16[608,128]{1,0:T(8,128)(2,1)S(1)}, u32[]{:S(2)}, u32[]{:S(2)}) collective-permute-start(s16[608,128]{1,0:T(8,128)(2,1)S(1)} %get-tuple-element.38), channel_id=1, source_target_pairs={{0,6},{1,7},{2,0},{3,1},{4,2},{5,3},{6,4},{7,5},{8,14},{9,15},{10,... | collective-permute-start | bytes 466952 | tf_op jit(solution)/shard_map/ppermute | solution.py:101
  39.4 7.9 %collective-permute-start.10 = (s16[464,128]{1,0:T(8,128)(2,1)S(1)}, s16[464,128]{1,0:T(8,128)(2,1)S(1)}, u32[]{:S(2)}, u32[]{:S(2)}) collective-permute-start(s16[464,128]{1,0:T(8,128)(2,1)S(1)} %get-tuple-element.31), channel_id=1, source_target_pairs={{0,4},{1,5},{2,6},{3,7},{4,0},{5,1},{6,2},{7,3},{8,12},{9,13},{10,... | collective-permute-start | bytes 356360 | tf_op jit(solution)/shard_map/ppermute | solution.py:101
  40.2 10.1 %collective-permute-start.11 = (s16[464,128]{1,0:T(8,128)(2,1)S(1)}, s16[464,128]{1,0:T(8,128)(2,1)S(1)}, u32[]{:S(2)}, u32[]{:S(2)}) collective-permute-start(s16[464,128]{1,0:T(8,128)(2,1)S(1)} %get-tuple-element.32), channel_id=1, source_target_pairs={{0,6},{1,7},{2,0},{3,1},{4,2},{5,3},{6,4},{7,5},{8,14},{9,15},{10,... | collective-permute-start | bytes 356360 | tf_op jit(solution)/shard_map/ppermute | solution.py:101
  41.8 8.5 %collective-permute-start.9 = (s16[464,128]{1,0:T(8,128)(2,1)S(1)}, s16[464,128]{1,0:T(8,128)(2,1)S(1)}, u32[]{:S(2)}, u32[]{:S(2)}) collective-permute-start(s16[464,128]{1,0:T(8,128)(2,1)S(1)} %get-tuple-element.30), channel_id=1, source_target_pairs={{0,2},{1,3},{2,4},{3,5},{4,6},{5,7},{6,0},{7,1},{8,10},{9,11},{10,... | collective-permute-start | bytes 356360 | tf_op jit(solution)/shard_map/ppermute | solution.py:101

commit v8 on v7

--- a/solution.py
+++ b/solution.py
@@ -45,6 +45,10 @@
 
 def in_hbm(*arrays):
     return [pltpu.with_memory_space_constraint(a, pltpu.HBM) for a in arrays]
+
+
+def in_smem(array):
+    return pltpu.with_memory_space_constraint(array, pltpu.SMEM)
 
 
 def in_vmem(*arrays):
@@ -138,11 +142,10 @@
 def fetch_blocks(block_live, integrals, row_owner, after):
     return pl.pallas_call(
         fetch_kernel,
-        out_shape=(pltpu.VMEM((TILES * SLOTS, ENTRY, ENTRY), bf16), pltpu.SMEM(row_owner.shape, i32)),
+        out_shape=(pltpu.VMEM((TILES * SLOTS, ENTRY, ENTRY), bf16), pltpu.SMEM(row_owner.shape, i32), pltpu.SMEM(block_live.shape, i32)),
         in_specs=[HBM, HBM, HBM, ANY],
-        out_specs=(VMEM, SMEM),
+        out_specs=(VMEM, SMEM, SMEM),
         scratch_shapes=[
-            pltpu.SMEM(block_live.shape, i32),
             pltpu.SemaphoreType.DMA((2,)),
             pltpu.SemaphoreType.DMA((EARLY,)),
         ],
@@ -158,14 +161,12 @@
 )
 
 
-def compute_kernel(group, sources, fetches, live_hbm, ints_hbm, *refs):
+def compute_kernel(group, sources, fetches, live, ints_hbm, *refs):
     count_in = max(at for at, _ in sources.values()) + 1
     arrays = refs[:count_in]
     refs = refs[count_in + 1 :]
-    theirs_ref, mine_ref, block_ref, left, table_v, table, live, count, where, sem, sems = refs
+    theirs_ref, mine_ref, block_ref, left, table_v, table, count, where, sem, sems = refs
     core = position()[3]
-    copy_live = pltpu.make_async_copy(live_hbm, live, sem.at[0])
-    copy_live.start()
 
     def fetch(i):
         return pltpu.make_async_copy(ints_hbm.at[lax.rem(i, SLOTS), i // SLOTS], block_ref.at[i], sems.at[i])
@@ -173,6 +174,10 @@
     def piece(a, b, row, rows):
         at, base = sources[a, b]
         return arrays[at][pl.ds(base + row, rows), :]
+
+    if fetches:
+        for i in range(EARLY, TILES * SLOTS):
+            pl.when(live[i % SLOTS, i // SLOTS] != 0)(functools.partial(lambda i: fetch(i).start(), i))
 
     lane = lax.broadcasted_iota(i32, (8, LANES), 1)
     entries = jnp.zeros((8, LANES), i32)
@@ -180,13 +185,9 @@
         tag = piece(a, b, TAG, META).astype(f32)[:8].astype(i32)
         entries = jnp.where(lane == k, tag, entries)
     table_v[...] = entries
-    copy_table = pltpu.make_async_copy(table_v, table, sem.at[1])
+    copy_table = pltpu.make_async_copy(table_v, table, sem)
     copy_table.start()
 
-    copy_live.wait()
-    if fetches:
-        for i in range(EARLY, TILES * SLOTS):
-            pl.when(live[i % SLOTS, i // SLOTS] != 0)(functools.partial(lambda i: fetch(i).start(), i))
     theirs_ref[...] = jnp.zeros_like(theirs_ref)
     mine_ref[...] = jnp.zeros_like(mine_ref)
     for c in range(TILES):
@@ -246,7 +247,7 @@
     lax.fori_loop(0, TILES * SLOTS, one_block, 0)
 
 
-def compute(which, block_live, integrals, blocks, pieces):
+def compute(which, flags, integrals, blocks, pieces):
     group = GROUPS[which]
     fetches = which == 0
     sources = {ab: (i, k * PIECE) for i, (_, held) in enumerate(pieces) for k, ab in enumerate(held)}
@@ -255,22 +256,21 @@
     return pl.pallas_call(
         functools.partial(compute_kernel, group, sources, fetches),
         out_shape=(total, total, pltpu.VMEM((TILES * SLOTS, ENTRY, ENTRY), bf16)),
-        in_specs=[HBM, HBM] + [VMEM] * (len(pieces) + len(more)),
+        in_specs=[SMEM, HBM] + [VMEM] * (len(pieces) + len(more)),
         out_specs=(VMEM,) * 3,
         input_output_aliases={2 + len(pieces): 2},
         scratch_shapes=[
             pltpu.VMEM((TILES, 2 * CHUNK, ENTRY), bf16),
             pltpu.VMEM((8, LANES), i32),
             pltpu.SMEM((8, LANES), i32),
-            pltpu.SMEM(block_live.shape, i32),
             pltpu.SMEM((TILES,), i32),
             pltpu.SMEM((TILES * BLOCKS,), i32),
-            pltpu.SemaphoreType.DMA((2,)),
+            pltpu.SemaphoreType.DMA,
             pltpu.SemaphoreType.DMA((TILES * SLOTS,)),
         ],
         compiler_params=params(8),
         cost_estimate=pl.CostEstimate(flops=1 << 32, bytes_accessed=8 << 20, transcendentals=0),
-    )(*in_hbm(block_live, integrals), *[array for array, _ in pieces], *more)
+    )(in_smem(flags), *in_hbm(integrals), *[array for array, _ in pieces], *more)
 
 
 def encode(value):
@@ -385,7 +385,7 @@
         out_specs=VMEM,
         scratch_shapes=[pltpu.VMEM((RANGES * META, LANES), f32)],
         compiler_params=params(),
-    )(pltpu.with_memory_space_constraint(row_owner, pltpu.SMEM), parts)
+    )(in_smem(row_owner), parts)
 
 
 def finish_kernel(in_ref, out_hbm, tiles, scales, sems):
@@ -429,15 +429,15 @@
     first = [(own, [(0, 0)]), (by1, [(0, 1)]), (by3, [(0, 3)])]
     first += [(nears[a], [(a, b) for b in (0, 1, 3)]) for a in (1, 3)]
     row = jnp.concatenate([own, by1, by2, by3], 0)
-    blocks, owners = fetch_blocks(block_live, integrals, row_owner, near)
+    blocks, owners, flags = fetch_blocks(block_live, integrals, row_owner, near)
     row, blocks = lax.optimization_barrier((row, blocks))
     fars = {a: shift_second(by2, a) for a in (1, 3)}
     second = [(shift_second(row, 2), [(2, b) for b in range(RING)]), (by2, [(0, 2)])]
     second += [(fars[a], [(a, 2)]) for a in (1, 3)]
 
-    theirs0, mine0, blocks = compute(0, block_live, integrals, blocks, first)
+    theirs0, mine0, blocks = compute(0, flags, integrals, blocks, first)
     other0 = shift_core(theirs0)
-    theirs1, mine1, _ = compute(1, block_live, integrals, blocks, second)
+    theirs1, mine1, _ = compute(1, flags, integrals, blocks, second)
     other1 = shift_core(theirs1)
     own0, *sends0 = core_sum(mine0, other0)
     codes0 = [shift_y(sends0[d - 1], d) for d in range(1, RING)]

time: 79.7 us -> 79.3 us (level)
  blocking collectives: 27.7 us -> 26.5 us
    pallas_call x1, Pallas kernels: 2.33 us -> 3.6 us  [fetch_blocks(): pl.pallas_call(fetch_kernel, out_shape=(pltpu.VMEM((TILES * SLOTS, ENTRY,...]
    all_to_all x1, blocking collectives: 14.4 us -> 13.4 us  [shards(): lax.all_to_all(parts, 'occ', split_axis=0, concat_axis=0, tiled=True)]
  transfers between devices with their start and end apart: 16 -> 16, of which waited for: 7 -> 7; matrix products, arithmetic and copies ran while one was open for 0% -> 0% of each run, Pallas kernels for 17% -> 18%
where the time goes in v8:
time: 79.3 us; the launch traced here: 78.8 us
  blocking collectives  26.5 us (33%)
  starting transfers between devices  25.9 us (33%)
  Pallas kernels  16.2 us (20%)
  waiting for transfers between devices  10 us (13%)
    ppermute x16, starting transfers between devices, shift(): lax.ppermute(value, ('occ', 'vir'), [(index(*s), index(*place(*s))) for s...  25.9 us
    all_to_all x1, blocking collectives, shards(): lax.all_to_all(parts, 'occ', split_axis=0, concat_axis=0, tiled=True)  13.4 us
    all_to_all x1, blocking collectives, shards(): lax.all_to_all(parts, 'vir', split_axis=0, concat_axis=0, tiled=True)  13.1 us
    ppermute x16, waiting for transfers between devices, shift(): lax.ppermute(value, ('occ', 'vir'), [(index(*s), index(*place(*s))) for s...  10 us
    pallas_call x2, Pallas kernels, compute(): pl.pallas_call(functools.partial(compute_kernel, group, sources, fetches)...  9.48 us
    pallas_call x1, Pallas kernels, fetch_blocks(): pl.pallas_call(fetch_kernel, out_shape=(pltpu.VMEM((TILES * SLOTS, ENTRY,...  3.6 us
  transfers between devices with their start and end apart: 16, of which 7 were waited for; matrix products, arithmetic and copies ran while one was open for 0% of the time, Pallas kernels for 18%

profile of v8, /device:TPU:1, one launch (start us, length us, event | category | flops | bytes accessed | tf_op | source)
XLA Modules:
  0.0 78.8 jit_solution(4487967573560967544)
XLA Ops:
  0.0 1.0 %shard_map.55.refs_0_ = bf16[528,128]{1,0:T(8,128)(2,1)S(1)} custom-call(s32[1,4]{1,0:T(1,128)} %live_hbm.2, bf16[32,4096]{1,0:T(8,128)(2,1)} %amp_hbm.1), custom_call_target="tpu_custom_call" | custom-call | tf_op jit(solution)/shard_map/pallas_call | solution.py:86
  1.0 2.1 %collective-permute-start = (bf16[528,128]{1,0:T(8,128)(2,1)S(1)}, bf16[528,128]{1,0:T(8,128)(2,1)S(1)}, u32[]{:S(2)}, u32[]{:S(2)}) collective-permute-start(bf16[528,128]{1,0:T(8,128)(2,1)S(1)} %shard_map.55.refs_0_), channel_id=1, source_target_pairs={{0,8},{1,33},{2,10},{3,35},{4,12},{5,37},{6,14},{7,39},{8,16},{9,4... | collective-permute-start | bytes 405512 | tf_op jit(solution)/shard_map/ppermute | solution.py:105
  3.1 1.4 %collective-permute-start.1 = (bf16[528,128]{1,0:T(8,128)(2,1)S(1)}, bf16[528,128]{1,0:T(8,128)(2,1)S(1)}, u32[]{:S(2)}, u32[]{:S(2)}) collective-permute-start(bf16[528,128]{1,0:T(8,128)(2,1)S(1)} %shard_map.55.refs_0_), channel_id=1, source_target_pairs={{0,24},{1,97},{2,26},{3,99},{4,28},{5,101},{6,30},{7,103},{8,0},{9... | collective-permute-start | bytes 405512 | tf_op jit(solution)/shard_map/ppermute | solution.py:105
  4.5 1.6 %collective-permute-start.2 = (bf16[528,128]{1,0:T(8,128)(2,1)S(1)}, bf16[528,128]{1,0:T(8,128)(2,1)S(1)}, u32[]{:S(2)}, u32[]{:S(2)}) collective-permute-start(bf16[528,128]{1,0:T(8,128)(2,1)S(1)} %shard_map.55.refs_0_), channel_id=1, source_target_pairs={{0,16},{1,65},{2,18},{3,67},{4,20},{5,69},{6,22},{7,71},{8,24},{9,... | collective-permute-start | bytes 405512 | tf_op jit(solution)/shard_map/ppermute | solution.py:105
  6.1 0.7 collective-permute-done.refs_1_
  6.8 0.2 collective-permute-done.1.refs_2_
  7.0 1.9 %collective-permute-start.6 = (bf16[1584,128]{1,0:T(8,128)(2,1)S(1)}, bf16[1584,128]{1,0:T(8,128)(2,1)S(1)}, u32[]{:S(2)}, u32[]{:S(2)}) collective-permute-start(bf16[1584,128]{1,0:T(8,128)(2,1)S(1)} %pad_maximum_fusion.1.after_ref), channel_id=1, source_target_pairs={{0,32},{1,9},{2,34},{3,11},{4,36},{5,13},{6,38},{7,15},{8,40},{9,1... | collective-permute-start | bytes 1216520 | tf_op jit(solution)/shard_map/ppermute | solution.py:105
  8.9 2.3 %collective-permute-start.7 = (bf16[1584,128]{1,0:T(8,128)(2,1)S(1)}, bf16[1584,128]{1,0:T(8,128)(2,1)S(1)}, u32[]{:S(2)}, u32[]{:S(2)}) collective-permute-start(bf16[1584,128]{1,0:T(8,128)(2,1)S(1)} %pad_maximum_fusion.1.after_ref), channel_id=1, source_target_pairs={{0,96},{1,25},{2,98},{3,27},{4,100},{5,29},{6,102},{7,31},{8,104},... | collective-permute-start | bytes 1216520 | tf_op jit(solution)/shard_map/ppermute | solution.py:105
  11.2 3.6 %shard_map.56 = (bf16[8,1024,1024]{2,1,0:T(8,128)(2,1)S(1)}, s32[32]{0:T(128)S(4)}, s32[2,4]{1,0:T(2,128)S(4)}) custom-call(s32[2,4]{1,0:T(2,128)} %live_hbm.3, bf16[2,4,1024,1024]{3,2,1,0:T(8,128)(2,1)} %ints_hbm.5, s32[32]{0:T(128)} %owner_hbm.1, bf16[1584,128]{1,0:T(8,128)(2,1)S(1)} %pad_maximum_fusion.1.after_ref), custom_call_target="tpu_custom_call" | custom-call | bytes 16777216 | tf_op jit(solution)/shard_map/pallas_call | solution.py:143
  14.8 0.0 collective-permute-done.2.refs_1_
  14.9 0.1 collective-permute-start.3
  15.0 1.9 %collective-permute-start.4 = (bf16[528,128]{1,0:T(8,128)(2,1)S(1)}, bf16[528,128]{1,0:T(8,128)(2,1)S(1)}, u32[]{:S(2)}, u32[]{:S(2)}) collective-permute-start(bf16[528,128]{1,0:T(8,128)(2,1)S(1)} %collective-permute-done.2.refs_1_), channel_id=1, source_target_pairs={{0,32},{1,9},{2,34},{3,11},{4,36},{5,13},{6,38},{7,15},{8,40},{9,1... | collective-permute-start | bytes 405512 | tf_op jit(solution)/shard_map/ppermute | solution.py:105
  16.9 0.8 %collective-permute-start.5 = (bf16[528,128]{1,0:T(8,128)(2,1)S(1)}, bf16[528,128]{1,0:T(8,128)(2,1)S(1)}, u32[]{:S(2)}, u32[]{:S(2)}) collective-permute-start(bf16[528,128]{1,0:T(8,128)(2,1)S(1)} %collective-permute-done.2.refs_1_), channel_id=1, source_target_pairs={{0,96},{1,25},{2,98},{3,27},{4,100},{5,29},{6,102},{7,31},{8,104},... | collective-permute-start | bytes 405512 | tf_op jit(solution)/shard_map/ppermute | solution.py:105
  17.7 0.0 collective-permute-done.6.refs_3_
  17.7 0.0 collective-permute-done.7.refs_4_
  17.7 5.8 %shard_map.57 = (f32[4,576,128]{2,1,0:T(8,128)S(1)}, f32[4,576,128]{2,1,0:T(8,128)S(1)}, bf16[8,1024,1024]{2,1,0:T(8,128)(2,1)S(1)}) custom-call(s32[2,4]{1,0:T(2,128)S(4)} %get-tuple-element.24.live, bf16[2,4,1024,1024]{3,2,1,0:T(8,128)(2,1)} %ints_hbm.5, bf16[528,128]{1,0:T(8,128)(2,1)S(1)} %shard_map.55.refs_0_, ...), custom_call_target="tpu_custom_call", output_to_operand_aliasing={{2}: (7, {})} | custom-call | flops 4294967296 | bytes 8388608 | tf_op jit(solution)/shard_map/pallas_call | solution.py:256
  23.6 1.9 %collective-permute-start.12 = (f32[4,576,128]{2,1,0:T(8,128)S(1)}, f32[4,576,128]{2,1,0:T(8,128)S(1)}, u32[]{:S(2)}, u32[]{:S(2)}) collective-permute-start(f32[4,576,128]{2,1,0:T(8,128)S(1)} %get-tuple-element.36), channel_id=1, source_target_pairs={{0,1},{1,0},{2,3},{3,2},{4,5},{5,4},{6,7},{7,6},{8,9},{9,8},{10,11... | collective-permute-start | bytes 3538952 | tf_op jit(solution)/shard_map/ppermute | solution.py:105
  25.5 0.7 collective-permute-done.4.refs_2_
  26.2 0.0 collective-permute-done.5.refs_3_
  26.2 0.0 collective-permute-done.3.refs_0_
  26.2 3.7 %shard_map.58 = (f32[4,448,128]{2,1,0:T(8,128)S(1)}, f32[4,448,128]{2,1,0:T(8,128)S(1)}, bf16[8,1024,1024]{2,1,0:T(8,128)(2,1)S(1)}) custom-call(s32[2,4]{1,0:T(2,128)S(4)} %get-tuple-element.24.live, bf16[2,4,1024,1024]{3,2,1,0:T(8,128)(2,1)} %ints_hbm.5, bf16[2112,128]{1,0:T(8,128)(2,1)S(1)} %collective-permute-done.3.refs_0_, ...), custom_call_target="tpu_custom_call", output_to_operand_aliasing={{2}: (6, {})} | custom-call | flops 4294967296 | bytes 8388608 | tf_op jit(solution)/shard_map/pallas_call | solution.py:256
  29.9 2.3 %collective-permute-start.8 = (f32[4,448,128]{2,1,0:T(8,128)S(1)}, f32[4,448,128]{2,1,0:T(8,128)S(1)}, u32[]{:S(2)}, u32[]{:S(2)}) collective-permute-start(f32[4,448,128]{2,1,0:T(8,128)S(1)} %get-tuple-element.30), channel_id=1, source_target_pairs={{0,1},{1,0},{2,3},{3,2},{4,5},{5,4},{6,7},{7,6},{8,9},{9,8},{10,11... | collective-permute-start | bytes 2752520 | tf_op jit(solution)/shard_map/ppermute | solution.py:105
  32.1 0.0 collective-permute-done.12.other_ref
  32.1 0.3 shard_map.60
  32.5 2.4 %collective-permute-start.13 = (s16[608,128]{1,0:T(8,128)(2,1)S(1)}, s16[608,128]{1,0:T(8,128)(2,1)S(1)}, u32[]{:S(2)}, u32[]{:S(2)}) collective-permute-start(s16[608,128]{1,0:T(8,128)(2,1)S(1)} %get-tuple-element.38), channel_id=1, source_target_pairs={{0,2},{1,3},{2,4},{3,5},{4,6},{5,7},{6,0},{7,1},{8,10},{9,11},{10,... | collective-permute-start | bytes 466952 | tf_op jit(solution)/shard_map/ppermute | solution.py:105
  34.9 3.3 %collective-permute-start.14 = (s16[608,128]{1,0:T(8,128)(2,1)S(1)}, s16[608,128]{1,0:T(8,128)(2,1)S(1)}, u32[]{:S(2)}, u32[]{:S(2)}) collective-permute-start(s16[608,128]{1,0:T(8,128)(2,1)S(1)} %get-tuple-element.39), channel_id=1, source_target_pairs={{0,4},{1,5},{2,6},{3,7},{4,0},{5,1},{6,2},{7,3},{8,12},{9,13},{10,... | collective-permute-start | bytes 466952 | tf_op jit(solution)/shard_map/ppermute | solution.py:105
  38.1 1.0 %collective-permute-start.15 = (s16[608,128]{1,0:T(8,128)(2,1)S(1)}, s16[608,128]{1,0:T(8,128)(2,1)S(1)}, u32[]{:S(2)}, u32[]{:S(2)}) collective-permute-start(s16[608,128]{1,0:T(8,128)(2,1)S(1)} %get-tuple-element.40), channel_id=1, source_target_pairs={{0,6},{1,7},{2,0},{3,1},{4,2},{5,3},{6,4},{7,5},{8,14},{9,15},{10,... | collective-permute-start | bytes 466952 | tf_op jit(solution)/shard_map/ppermute | solution.py:105
  39.2 0.0 collective-permute-done.8.other_ref
  39.2 0.3 shard_map.59
  39.5 0.3 collective-permute-start.10
  39.8 2.6 %collective-permute-start.11 = (s16[464,128]{1,0:T(8,128)(2,1)S(1)}, s16[464,128]{1,0:T(8,128)(2,1)S(1)}, u32[]{:S(2)}, u32[]{:S(2)}) collective-permute-start(s16[464,128]{1,0:T(8,128)(2,1)S(1)} %get-tuple-element.34), channel_id=1, source_target_pairs={{0,6},{1,7},{2,0},{3,1},{4,2},{5,3},{6,4},{7,5},{8,14},{9,15},{10,... | collective-permute-start | bytes 356360 | tf_op jit(solution)/shard_map/ppermute | solution.py:105
  42.3 0.0 collective-permute-done.13.a_ref
  42.4 0.0 collective-permute-start.9
  42.4 3.3 %collective-permute-done.14.b_ref = s16[608,128]{1,0:T(8,128)(2,1)S(1)} collective-permute-done((s16[608,128]{1,0:T(8,128)(2,1)S(1)}, s16[608,128]{1,0:T(8,128)(2,1)S(1)}, u32[]{:S(2)}, u32[]{:S(2)}) %collective-permute-start.14) | collective-permute-done | bytes 155680 | tf_op jit(solution)/shard_map/ppermute | solution.py:105
  45.6 0.0 collective-permute-done.15.c_ref
  45.6 0.3 shard_map.61.refs_0_
  45.9 2.3 %collective-permute-done.10.b_ref = s16[464,128]{1,0:T(8,128)(2,1)S(1)} collective-permute-done((s16[464,128]{1,0:T(8,128)(2,1)S(1)}, s16[464,128]{1,0:T(8,128)(2,1)S(1)}, u32[]{:S(2)}, u32[]{:S(2)}) %collective-permute-start.10) | collective-permute-done | bytes 118816 | tf_op jit(solution)/shard_map/ppermute | solution.py:105
  48.2 2.0 %collective-permute-done.11.c_ref = s16[464,128]{1,0:T(8,128)(2,1)S(1)} collective-permute-done((s16[464,128]{1,0:T(8,128)(2,1)S(1)}, s16[464,128]{1,0:T(8,128)(2,1)S(1)}, u32[]{:S(2)}, u32[]{:S(2)}) %collective-permute-start.11) | collective-permute-done | bytes 118816 | tf_op jit(solution)/shard_map/ppermute | solution.py:105
  50.2 0.8 %collective-permute-done.9.a_ref = s16[464,128]{1,0:T(8,128)(2,1)S(1)} collective-permute-done((s16[464,128]{1,0:T(8,128)(2,1)S(1)}, s16[464,128]{1,0:T(8,128)(2,1)S(1)}, u32[]{:S(2)}, u32[]{:S(2)}) %collective-permute-start.9) | collective-permute-done | bytes 118816 | tf_op jit(solution)/shard_map/ppermute | solution.py:105
  51.0 0.2 shard_map.62
  51.2 13.4 %all_to_all.10.in_ref = s16[16,80,128]{2,1,0:T(8,128)(2,1)S(1)} all-to-all(s16[16,80,128]{2,1,0:T(8,128)(2,1)S(1)} %shard_map.62), channel_id=1, replica_groups=mesh['occ'=16,'vir'=8] {'occ'}, dimensions={0} | all-to-all | bytes 655360 | tf_op jit(solution)/shard_map/all_to_all | solution.py:448
  64.7 0.2 shard_map.63
  64.9 13.1 %all_to_all.11.in_ref = s16[8,144,128]{2,1,0:T(8,128)(2,1)S(1)} all-to-all(s16[8,144,128]{2,1,0:T(8,128)(2,1)S(1)} %shard_map.63), channel_id=1, replica_groups=mesh['occ'=16,'vir'=8] {'vir'}, dimensions={0} | all-to-all | bytes 589824 | tf_op jit(solution)/shard_map/all_to_all | solution.py:450
  78.0 0.8 %shard_map.64 = f32[32,4096]{1,0:T(8,128)} custom-call(s16[8,144,128]{2,1,0:T(8,128)(2,1)S(1)} %all_to_all.11.in_ref), custom_call_target="tpu_custom_call" | custom-call | tf_op jit(solution)/shard_map/pallas_call | solution.py:410
  (2 shorter events, 0.1 us)
Async XLA Ops:
  1.0 5.8 %collective-permute-start = (bf16[528,128]{1,0:T(8,128)(2,1)S(1)}, bf16[528,128]{1,0:T(8,128)(2,1)S(1)}, u32[]{:S(2)}, u32[]{:S(2)}) collective-permute-start(bf16[528,128]{1,0:T(8,128)(2,1)S(1)} %shard_map.55.refs_0_), channel_id=1, source_target_pairs={{0,8},{1,33},{2,10},{3,35},{4,12},{5,37},{6,14},{7,39},{8,16},{9,4... | collective-permute-start | bytes 405512 | tf_op jit(solution)/shard_map/ppermute | solution.py:105
  3.1 3.9 %collective-permute-start.1 = (bf16[528,128]{1,0:T(8,128)(2,1)S(1)}, bf16[528,128]{1,0:T(8,128)(2,1)S(1)}, u32[]{:S(2)}, u32[]{:S(2)}) collective-permute-start(bf16[528,128]{1,0:T(8,128)(2,1)S(1)} %shard_map.55.refs_0_), channel_id=1, source_target_pairs={{0,24},{1,97},{2,26},{3,99},{4,28},{5,101},{6,30},{7,103},{8,0},{9... | collective-permute-start | bytes 405512 | tf_op jit(solution)/shard_map/ppermute | solution.py:105
  4.5 10.4 %collective-permute-start.2 = (bf16[528,128]{1,0:T(8,128)(2,1)S(1)}, bf16[528,128]{1,0:T(8,128)(2,1)S(1)}, u32[]{:S(2)}, u32[]{:S(2)}) collective-permute-start(bf16[528,128]{1,0:T(8,128)(2,1)S(1)} %shard_map.55.refs_0_), channel_id=1, source_target_pairs={{0,16},{1,65},{2,18},{3,67},{4,20},{5,69},{6,22},{7,71},{8,24},{9,... | collective-permute-start | bytes 405512 | tf_op jit(solution)/shard_map/ppermute | solution.py:105
  7.0 10.7 %collective-permute-start.6 = (bf16[1584,128]{1,0:T(8,128)(2,1)S(1)}, bf16[1584,128]{1,0:T(8,128)(2,1)S(1)}, u32[]{:S(2)}, u32[]{:S(2)}) collective-permute-start(bf16[1584,128]{1,0:T(8,128)(2,1)S(1)} %pad_maximum_fusion.1.after_ref), channel_id=1, source_target_pairs={{0,32},{1,9},{2,34},{3,11},{4,36},{5,13},{6,38},{7,15},{8,40},{9,1... | collective-permute-start | bytes 1216520 | tf_op jit(solution)/shard_map/ppermute | solution.py:105
  8.9 8.8 %collective-permute-start.7 = (bf16[1584,128]{1,0:T(8,128)(2,1)S(1)}, bf16[1584,128]{1,0:T(8,128)(2,1)S(1)}, u32[]{:S(2)}, u32[]{:S(2)}) collective-permute-start(bf16[1584,128]{1,0:T(8,128)(2,1)S(1)} %pad_maximum_fusion.1.after_ref), channel_id=1, source_target_pairs={{0,96},{1,25},{2,98},{3,27},{4,100},{5,29},{6,102},{7,31},{8,104},... | collective-permute-start | bytes 1216520 | tf_op jit(solution)/shard_map/ppermute | solution.py:105
  14.9 11.3 %collective-permute-start.3 = (bf16[2112,128]{1,0:T(8,128)(2,1)S(1)}, bf16[2112,128]{1,0:T(8,128)(2,1)S(1)}, u32[]{:S(2)}, u32[]{:S(2)}) collective-permute-start(bf16[2112,128]{1,0:T(8,128)(2,1)S(1)} %pad_maximum_fusion), channel_id=1, source_target_pairs={{0,64},{1,17},{2,66},{3,19},{4,68},{5,21},{6,70},{7,23},{8,72},{9,... | collective-permute-start | bytes 1622024 | tf_op jit(solution)/shard_map/ppermute | solution.py:105
  15.0 11.2 %collective-permute-start.4 = (bf16[528,128]{1,0:T(8,128)(2,1)S(1)}, bf16[528,128]{1,0:T(8,128)(2,1)S(1)}, u32[]{:S(2)}, u32[]{:S(2)}) collective-permute-start(bf16[528,128]{1,0:T(8,128)(2,1)S(1)} %collective-permute-done.2.refs_1_), channel_id=1, source_target_pairs={{0,32},{1,9},{2,34},{3,11},{4,36},{5,13},{6,38},{7,15},{8,40},{9,1... | collective-permute-start | bytes 405512 | tf_op jit(solution)/shard_map/ppermute | solution.py:105
  16.9 9.3 %collective-permute-start.5 = (bf16[528,128]{1,0:T(8,128)(2,1)S(1)}, bf16[528,128]{1,0:T(8,128)(2,1)S(1)}, u32[]{:S(2)}, u32[]{:S(2)}) collective-permute-start(bf16[528,128]{1,0:T(8,128)(2,1)S(1)} %collective-permute-done.2.refs_1_), channel_id=1, source_target_pairs={{0,96},{1,25},{2,98},{3,27},{4,100},{5,29},{6,102},{7,31},{8,104},... | collective-permute-start | bytes 405512 | tf_op jit(solution)/shard_map/ppermute | solution.py:105
  23.6 8.6 %collective-permute-start.12 = (f32[4,576,128]{2,1,0:T(8,128)S(1)}, f32[4,576,128]{2,1,0:T(8,128)S(1)}, u32[]{:S(2)}, u32[]{:S(2)}) collective-permute-start(f32[4,576,128]{2,1,0:T(8,128)S(1)} %get-tuple-element.36), channel_id=1, source_target_pairs={{0,1},{1,0},{2,3},{3,2},{4,5},{5,4},{6,7},{7,6},{8,9},{9,8},{10,11... | collective-permute-start | bytes 3538952 | tf_op jit(solution)/shard_map/ppermute | solution.py:105
  29.9 9.3 %collective-permute-start.8 = (f32[4,448,128]{2,1,0:T(8,128)S(1)}, f32[4,448,128]{2,1,0:T(8,128)S(1)}, u32[]{:S(2)}, u32[]{:S(2)}) collective-permute-start(f32[4,448,128]{2,1,0:T(8,128)S(1)} %get-tuple-element.30), channel_id=1, source_target_pairs={{0,1},{1,0},{2,3},{3,2},{4,5},{5,4},{6,7},{7,6},{8,9},{9,8},{10,11... | collective-permute-start | bytes 2752520 | tf_op jit(solution)/shard_map/ppermute | solution.py:105
  32.5 9.9 %collective-permute-start.13 = (s16[608,128]{1,0:T(8,128)(2,1)S(1)}, s16[608,128]{1,0:T(8,128)(2,1)S(1)}, u32[]{:S(2)}, u32[]{:S(2)}) collective-permute-start(s16[608,128]{1,0:T(8,128)(2,1)S(1)} %get-tuple-element.38), channel_id=1, source_target_pairs={{0,2},{1,3},{2,4},{3,5},{4,6},{5,7},{6,0},{7,1},{8,10},{9,11},{10,... | collective-permute-start | bytes 466952 | tf_op jit(solution)/shard_map/ppermute | solution.py:105
  34.9 10.8 %collective-permute-start.14 = (s16[608,128]{1,0:T(8,128)(2,1)S(1)}, s16[608,128]{1,0:T(8,128)(2,1)S(1)}, u32[]{:S(2)}, u32[]{:S(2)}) collective-permute-start(s16[608,128]{1,0:T(8,128)(2,1)S(1)} %get-tuple-element.39), channel_id=1, source_target_pairs={{0,4},{1,5},{2,6},{3,7},{4,0},{5,1},{6,2},{7,3},{8,12},{9,13},{10,... | collective-permute-start | bytes 466952 | tf_op jit(solution)/shard_map/ppermute | solution.py:105
  38.1 7.5 %collective-permute-start.15 = (s16[608,128]{1,0:T(8,128)(2,1)S(1)}, s16[608,128]{1,0:T(8,128)(2,1)S(1)}, u32[]{:S(2)}, u32[]{:S(2)}) collective-permute-start(s16[608,128]{1,0:T(8,128)(2,1)S(1)} %get-tuple-element.40), channel_id=1, source_target_pairs={{0,6},{1,7},{2,0},{3,1},{4,2},{5,3},{6,4},{7,5},{8,14},{9,15},{10,... | collective-permute-start | bytes 466952 | tf_op jit(solution)/shard_map/ppermute | solution.py:105
  39.5 8.7 %collective-permute-start.10 = (s16[464,128]{1,0:T(8,128)(2,1)S(1)}, s16[464,128]{1,0:T(8,128)(2,1)S(1)}, u32[]{:S(2)}, u32[]{:S(2)}) collective-permute-start(s16[464,128]{1,0:T(8,128)(2,1)S(1)} %get-tuple-element.33), channel_id=1, source_target_pairs={{0,4},{1,5},{2,6},{3,7},{4,0},{5,1},{6,2},{7,3},{8,12},{9,13},{10,... | collective-permute-start | bytes 356360 | tf_op jit(solution)/shard_map/ppermute | solution.py:105
  39.8 10.5 %collective-permute-start.11 = (s16[464,128]{1,0:T(8,128)(2,1)S(1)}, s16[464,128]{1,0:T(8,128)(2,1)S(1)}, u32[]{:S(2)}, u32[]{:S(2)}) collective-permute-start(s16[464,128]{1,0:T(8,128)(2,1)S(1)} %get-tuple-element.34), channel_id=1, source_target_pairs={{0,6},{1,7},{2,0},{3,1},{4,2},{5,3},{6,4},{7,5},{8,14},{9,15},{10,... | collective-permute-start | bytes 356360 | tf_op jit(solution)/shard_map/ppermute | solution.py:105
  42.4 8.7 %collective-permute-start.9 = (s16[464,128]{1,0:T(8,128)(2,1)S(1)}, s16[464,128]{1,0:T(8,128)(2,1)S(1)}, u32[]{:S(2)}, u32[]{:S(2)}) collective-permute-start(s16[464,128]{1,0:T(8,128)(2,1)S(1)} %get-tuple-element.32), channel_id=1, source_target_pairs={{0,2},{1,3},{2,4},{3,5},{4,6},{5,7},{6,0},{7,1},{8,10},{9,11},{10,... | collective-permute-start | bytes 356360 | tf_op jit(solution)/shard_map/ppermute | solution.py:105
